TPU v7x, 32 devices: a whole 2x2x4 slice. The times are simulated.
32 devices in a mesh: seq: 4 (over y, x), ch: 8 (over z, core).
Axes of the slice: x: 2, y: 2, z: 4, core: 2. Of those that a mesh axis runs over, the one named last changes fastest.
Arguments:
- token_ids: int32 [2048], P('seq'), may hold values from 0 to 511
- embedding: bfloat16 [512, 4096], P(None, 'ch'), may hold values from -6 to 6
- gain_first: bfloat16 [4096], P('ch'), may hold values from 0.5 to 1.5
- gain_second: bfloat16 [4096], P('ch'), may hold values from 0.5 to 1.5
- weights_first: bfloat16 [4096, 3, 4096], P(None, None, 'ch'), may hold values from -0.09375 to 0.09375
- weights_second: bfloat16 [4096, 3, 4096], P(None, None, 'ch'), may hold values from -0.09375 to 0.09375
- short_first: float32 [7, 3, 4096], P(None, None, 'ch'), may hold values from -2.5 to 2.5
- short_second: float32 [7, 3, 4096], P(None, None, 'ch'), may hold values from -2.5 to 2.5
- medium: bfloat16 [128, 4096], P(None, 'ch'), may hold values from -0.5 to 0.5
- residues: float32 [16, 4096], P(None, 'ch'), as said below
- decay_rates: float32 [16, 4096], P(None, 'ch'), as said below
- cotangent: bfloat16 [2048, 4096], P('seq', 'ch'), may hold values from -6 to 6
Outputs:
- output: bfloat16 [2048, 4096], P('seq', 'ch')
- grad_embedding: float32 [512, 4096], P(None, 'ch')
- grad_gain_first: float32 [4096], P('ch')
- grad_gain_second: float32 [4096], P('ch')
- grad_weights_first: float32 [4096, 3, 4096], P('seq', None, 'ch')
- grad_weights_second: float32 [4096, 3, 4096], P('seq', None, 'ch')
Inputs may be any that keep to these rules, and one draw needn't show every extreme that they name: `decay_rates`: positive, at most 0.06 and at least 0.05 / 2048. `residues`: magnitude at most 4 sqrt((0.12 + 1 / 2048) / 16).
All inputs are finite; a program needn't handle non-finite values.
Results may differ from a plain program's by a relative error of at most 0.028.
Values may be sent and summed in bfloat16 or wider, within the bound.
No kernel may reach another device: no remote copies, remote signals or barrier semaphores. Data moves between devices by JAX's collectives and lax.ppermute only.
A program may use at most 192 MiB of HBM per device.

v0:
```python
import jax
import jax.numpy as jnp
from jax import lax
from jax.sharding import PartitionSpec as P

epsilon = 1e-06
highest = lax.Precision.HIGHEST


def from_behind(shard, axis, by):
    devices = lax.axis_size(axis)
    pairs = [(i, i + by) for i in range(devices) if 0 <= i + by < devices]
    return lax.ppermute(shard, axis, pairs)


def short_forward(projected, short_filter):
    tap_count = short_filter.shape[0]
    row_count = projected.shape[0]
    earlier = from_behind(projected[row_count - (tap_count - 1) :], "seq", 1)
    widened = jnp.concatenate([earlier, projected], axis=0).astype(jnp.float32)
    running = jnp.zeros(projected.shape, jnp.float32)
    for offset in range(tap_count):
        first_row = tap_count - 1 - offset
        running = running + short_filter[offset] * widened[first_row : first_row + row_count]
    return running


def short_backward(gradient, short_filter):
    tap_count = short_filter.shape[0]
    row_count = gradient.shape[0]
    following = from_behind(gradient[: tap_count - 1], "seq", -1)
    widened = jnp.concatenate([gradient, following], axis=0).astype(jnp.float32)
    running = jnp.zeros(gradient.shape, jnp.float32)
    for offset in range(tap_count):
        running = running + short_filter[offset] * widened[offset : offset + row_count]
    return running


def medium_tables(medium):
    tap_count = medium.shape[0]
    lag_grid = (
        jnp.arange(tap_count, dtype=jnp.int32)[:, None]
        - jnp.arange(tap_count, dtype=jnp.int32)[None, :]
    )
    zero_value = jnp.zeros((), jnp.bfloat16)
    near_part = jnp.where(
        (lag_grid >= 0)[:, :, None],
        jnp.take(medium, jnp.clip(lag_grid, 0, tap_count - 1), axis=0),
        zero_value,
    )
    far_part = jnp.where(
        (lag_grid < 0)[:, :, None],
        jnp.take(medium, jnp.clip(lag_grid + tap_count, 0, tap_count - 1), axis=0),
        zero_value,
    )
    return (near_part, far_part)


def medium_forward(gated, near_part, far_part):
    tap_count = near_part.shape[0]
    row_count, width_local = gated.shape
    earlier = from_behind(gated[row_count - tap_count :], "seq", 1)
    blocks = gated.reshape(row_count // tap_count, tap_count, width_local)
    previous = jnp.concatenate([earlier[None], blocks[:-1]], axis=0)
    result = jnp.einsum("abc,jbc->jac", near_part, blocks, preferred_element_type=jnp.float32)
    result = result + jnp.einsum(
        "abc,jbc->jac", far_part, previous, preferred_element_type=jnp.float32
    )
    return result.reshape(row_count, width_local)


def medium_backward(gradient, near_part, far_part):
    tap_count = near_part.shape[0]
    row_count, width_local = gradient.shape
    following = from_behind(gradient[:tap_count], "seq", -1)
    blocks = gradient.reshape(row_count // tap_count, tap_count, width_local)
    later_blocks = jnp.concatenate([blocks[1:], following[None]], axis=0)
    result = jnp.einsum("abc,jac->jbc", near_part, blocks, preferred_element_type=jnp.float32)
    result = result + jnp.einsum(
        "abc,jac->jbc", far_part, later_blocks, preferred_element_type=jnp.float32
    )
    return result.reshape(row_count, width_local)


def mode_tables(decay_rates, residues, block_rows):
    lag_index = jnp.arange(block_rows + 1, dtype=jnp.float32)
    powers = jnp.exp(-decay_rates[:, None, :] * lag_index[None, :, None])
    response = jnp.sum(residues[:, None, :] * powers[:, :block_rows, :], axis=0)
    lag_grid = (
        jnp.arange(block_rows, dtype=jnp.int32)[:, None]
        - jnp.arange(block_rows, dtype=jnp.int32)[None, :]
    )
    picked = jnp.take(response, jnp.clip(lag_grid, 0, block_rows - 1), axis=0)
    toeplitz = jnp.where((lag_grid >= 0)[:, :, None], picked, jnp.zeros((), jnp.float32))
    closing_weights = powers[:, block_rows - 1 :: -1, :]
    lift_table = residues[:, None, :] * powers[:, 1:, :]
    stride = powers[:, block_rows, :]
    return (toeplitz, closing_weights, lift_table, stride)


def mode_blocks(values, tables):
    toeplitz, closing_weights, lift_table, stride = tables
    block_rows = toeplitz.shape[0]
    row_count, width_local = values.shape
    blocks = values.reshape(row_count // block_rows, block_rows, width_local)
    in_block = jnp.einsum("abc,jbc->jac", toeplitz, blocks, precision=highest)
    closing = jnp.einsum("mbc,jbc->jmc", closing_weights, blocks, precision=highest)
    return (in_block, closing)


def mode_chain(closing, stride, start_state):

    def advance(state, close_term):
        return (stride * state + close_term, state)

    last_state, entering = lax.scan(advance, start_state, closing)
    return (entering, last_state)


def mode_finish(in_block, entering, lift_table):
    added = in_block + jnp.einsum("mac,jmc->jac", lift_table, entering, precision=highest)
    return added.reshape(-1, added.shape[2])


def long_filter(signal, decay_rates, residues, backward):
    group_count = lax.axis_size("seq")
    group_width = signal.shape[1] // group_count
    offset = lax.axis_index("seq") * group_width
    rate_part = lax.dynamic_slice_in_dim(decay_rates, offset, group_width, 1)
    residue_part = lax.dynamic_slice_in_dim(residues, offset, group_width, 1)
    gathered = lax.all_to_all(signal, "seq", split_axis=1, concat_axis=0, tiled=True).astype(
        jnp.float32
    )
    if backward:
        gathered = gathered[::-1]
    tables = mode_tables(rate_part, residue_part, min(64, gathered.shape[0]))
    in_block, closing = mode_blocks(gathered, tables)
    entering, last_state = mode_chain(closing, tables[3], jnp.zeros(rate_part.shape, jnp.float32))
    result = mode_finish(in_block, entering, tables[2])
    if backward:
        result = result[::-1]
    return lax.all_to_all(
        result.astype(jnp.bfloat16), "seq", split_axis=0, concat_axis=1, tiled=True
    ).astype(result.dtype)


def mixer_input(inputs, gain, weights, short_filter):
    whole_rows, whole_gain = (
        lax.all_gather(inputs, "ch", axis=1, tiled=True),
        lax.all_gather(gain, "ch", axis=0, tiled=True),
    )
    as_float = whole_rows.astype(jnp.float32)
    row_scale = lax.rsqrt(jnp.mean(as_float * as_float, axis=1) + epsilon)
    normed = (as_float * row_scale[:, None] * whole_gain.astype(jnp.float32)).astype(jnp.bfloat16)
    features = weights.shape[0]
    width_local = weights.shape[2]
    projected = jnp.dot(
        normed, weights.reshape(features, 3 * width_local), preferred_element_type=jnp.float32
    )
    projected = projected.astype(jnp.bfloat16).reshape(-1, 3, width_local)
    featured = short_forward(projected, short_filter)
    gated = (featured[:, 1, :] * featured[:, 2, :]).astype(jnp.bfloat16)
    return (normed, row_scale, featured, gated)


def weight_grad(normed, flat_grad):
    group_count = lax.axis_size("seq")
    rows_each = normed.shape[1] // group_count
    columns = lax.all_to_all(normed, "seq", split_axis=1, concat_axis=0, tiled=True)
    all_grads = lax.all_gather(flat_grad, "seq", axis=0, tiled=True)
    row_count = flat_grad.shape[0]
    partials = lax.dot_general(
        columns.reshape(group_count, row_count, rows_each),
        all_grads.reshape(group_count, row_count, flat_grad.shape[1]),
        (((1,), (1,)), ((0,), (0,))),
        preferred_element_type=jnp.float32,
    )
    summed = jnp.sum(
        lax.optimization_barrier(partials.astype(jnp.bfloat16)).astype(jnp.float32), axis=0
    )
    return summed


def project_back(grad_featured, inputs, gain, weights, short_filter, normed, row_scale, grad_above):
    row_count, width_local = inputs.shape
    features = weights.shape[0]
    grad_projected = short_backward(grad_featured, short_filter).astype(jnp.bfloat16)
    flat_grad = grad_projected.reshape(row_count, 3 * width_local)
    partial_sum = lax.dot_general(
        flat_grad,
        weights.reshape(features, 3 * width_local),
        (((1,), (1,)), ((), ())),
        preferred_element_type=jnp.float32,
    )
    grad_normed = lax.psum_scatter(
        partial_sum.astype(jnp.bfloat16), "ch", scatter_dimension=1, tiled=True
    ).astype(jnp.float32)
    as_float = inputs.astype(jnp.float32)
    scaled = grad_normed * gain.astype(jnp.float32)
    row_terms = lax.psum(jnp.sum(scaled * as_float, axis=1), "ch")
    grad_inputs = (
        grad_above
        + row_scale[:, None] * scaled
        - as_float * (row_scale**3)[:, None] * row_terms[:, None] / features
    )
    grad_gain = jnp.sum(grad_normed * as_float * row_scale[:, None], axis=0)
    grad_weights = weight_grad(normed, flat_grad).reshape(-1, 3, width_local)
    return (grad_inputs.astype(jnp.bfloat16), grad_gain, grad_weights)


def per_device(
    token_ids,
    embedding,
    gain_first,
    gain_second,
    weights_first,
    weights_second,
    short_first,
    short_second,
    medium,
    residues,
    decay_rates,
    cotangent,
):
    vocab_size = embedding.shape[0]
    onehot = (token_ids[:, None] == jnp.arange(vocab_size, dtype=jnp.int32)[None, :]).astype(
        jnp.bfloat16
    )
    embedded = jnp.dot(onehot, embedding, preferred_element_type=jnp.float32).astype(jnp.bfloat16)
    normed_first, scale_first, featured_first, gated_first = mixer_input(
        embedded, gain_first, weights_first, short_first
    )
    near_part, far_part = medium_tables(medium)
    filtered_first = medium_forward(gated_first, near_part, far_part)
    middle = (embedded.astype(jnp.float32) + featured_first[:, 0, :] * filtered_first).astype(
        jnp.bfloat16
    )
    normed_second, scale_second, featured_second, gated_second = mixer_input(
        middle, gain_second, weights_second, short_second
    )
    filtered_second = long_filter(gated_second, decay_rates, residues, False)
    output = (middle.astype(jnp.float32) + featured_second[:, 0, :] * filtered_second).astype(
        jnp.bfloat16
    )
    above_second = cotangent.astype(jnp.float32)
    grad_filtered = (above_second * featured_second[:, 0, :]).astype(jnp.bfloat16)
    grad_gated = long_filter(grad_filtered, decay_rates, residues, True)
    grad_featured = jnp.stack(
        [
            above_second * filtered_second,
            grad_gated * featured_second[:, 2, :],
            grad_gated * featured_second[:, 1, :],
        ],
        axis=1,
    ).astype(jnp.bfloat16)
    grad_middle, gain_grad_second, weight_grad_second = project_back(
        grad_featured,
        middle,
        gain_second,
        weights_second,
        short_second,
        normed_second,
        scale_second,
        above_second,
    )
    above_first = grad_middle.astype(jnp.float32)
    grad_filtered = (above_first * featured_first[:, 0, :]).astype(jnp.bfloat16)
    grad_gated = medium_backward(grad_filtered, near_part, far_part)
    grad_featured = jnp.stack(
        [
            above_first * filtered_first,
            grad_gated * featured_first[:, 2, :],
            grad_gated * featured_first[:, 1, :],
        ],
        axis=1,
    ).astype(jnp.bfloat16)
    grad_embedded, gain_grad_first, weight_grad_first = project_back(
        grad_featured,
        embedded,
        gain_first,
        weights_first,
        short_first,
        normed_first,
        scale_first,
        above_first,
    )
    embed_part = lax.dot_general(
        onehot, grad_embedded, (((0,), (0,)), ((), ())), preferred_element_type=jnp.float32
    )
    gain_total_first, gain_total_second, embed_total = (
        lax.psum(gain_grad_first.astype(jnp.bfloat16), "seq").astype(jnp.float32),
        lax.psum(gain_grad_second.astype(jnp.bfloat16), "seq").astype(jnp.float32),
        lax.psum(embed_part.astype(jnp.bfloat16), "seq").astype(jnp.float32),
    )
    return (
        output,
        embed_total,
        gain_total_first,
        gain_total_second,
        weight_grad_first,
        weight_grad_second,
    )


def solution(mesh):
    placed = (
        P("seq"),
        P(None, "ch"),
        P("ch"),
        P("ch"),
        P(None, None, "ch"),
        P(None, None, "ch"),
        P(None, None, "ch"),
        P(None, None, "ch"),
        P(None, "ch"),
        P(None, "ch"),
        P(None, "ch"),
        P("seq", "ch"),
    )
    return jax.shard_map(
        per_device,
        mesh=mesh,
        in_specs=placed,
        out_specs=(
            P("seq", "ch"),
            P(None, "ch"),
            P("ch"),
            P("ch"),
            P("seq", None, "ch"),
            P("seq", None, "ch"),
        ),
        check_vma=False,
    )
```

profile of v0, /device:TPU:0, one launch (start us, length us, event | category | flops | bytes accessed | tf_op | source)
XLA Modules:
  0.0 997.2 jit_solution(6666590699786612041)
XLA Ops:
  10.9 14.4 %all-gather = bf16[8,1,512]{2,1,0:T(2,128)(2,1)S(1)} all-gather(bf16[1,1,512]{2,1,0:T(2,128)(2,1)S(1)} %reshape.248), channel_id=1, replica_groups=mesh['seq'=4,'ch'=8] {'ch'}, dimensions={0}, use_global_device_ids=true | all-gather | bytes 9216 | tf_op jit(solution)/shard_map/all_gather | solution.py:150
  25.3 17.0 %copy.74 = bf16[4096,3,512]{0,2,1:T(8,128)(2,1)} copy(bf16[4096,3,512]{2,0,1:T(8,128)(2,1)} %param.24) | data formatting | bytes 25165824 | tf_op args[4]
  42.7 17.5 %all-gather.7.cloned.1.call-done = bf16[512,4096]{1,0:T(8,128)(2,1)} async-done(((bf16[512,512]{1,0:T(8,128)(2,1)}), bf16[512,4096]{1,0:T(8,128)(2,1)}) %all-gather.7.cloned.1.call-update) | async-done | bytes 4194320 | tf_op jit(solution)/shard_map/all_gather | solution.py:149
  65.7 11.3 %convolution_convert_fusion.3 = bf16[512,1536]{1,0:T(8,128)(2,1)S(1)} fusion(bf16[512,4096]{1,0:T(8,128)(2,1)S(1)} %fusion.6, bf16[4096,1536]{0,1:T(8,128)(2,1)} %bitcast.195), kind=kOutput, calls=%fused_computation.97 | convolution fusion | flops 6443237376 | bytes 18350080 | tf_op jit(solution)/shard_map/dot_general | solution.py:157
  81.6 66.5 %gather_fusion = bf16[16384,512]{1,0:T(8,128)(2,1)} fusion(bf16[128,512]{1,0:T(8,128)(2,1)S(1)} %copy-done.2, s32[16384]{0:T(1024)S(1)} %bitcast_clamp_fusion.1), kind=kCustom, calls=%fused_computation.clone | custom fusion | bytes 33619968 | tf_op jit(solution)/shard_map/jit(_take)/gather | solution.py:48
  148.1 23.6 %copy.77 = bf16[128,128,512]{1,0,2:T(8,128)(2,1)} copy(bf16[128,128,512]{2,1,0:T(8,128)(2,1)} %bitcast.184) | data formatting | bytes 33554432 | tf_op jit(solution)/shard_map/jit(_take)/gather | solution.py:48
  171.6 66.4 %gather_fusion.1 = bf16[16384,512]{1,0:T(8,128)(2,1)} fusion(bf16[128,512]{1,0:T(8,128)(2,1)S(1)} %copy-done.2, s32[16384]{0:T(1024)S(1)} %bitcast_clamp_fusion), kind=kCustom, calls=%fused_computation.2.clone | custom fusion | bytes 33619968 | tf_op jit(solution)/shard_map/jit(_take)/gather | solution.py:53
  238.0 23.7 %copy.81 = bf16[128,128,512]{1,0,2:T(8,128)(2,1)} copy(bf16[128,128,512]{2,1,0:T(8,128)(2,1)} %bitcast.185) | data formatting | bytes 33554432 | tf_op jit(solution)/shard_map/jit(_take)/gather | solution.py:53
  275.6 13.0 %fusion.1 = f32[512,4,128]{2,1,0:T(4,128)} fusion(bf16[4,128,512]{1,0,2:T(4,128)(2,1)S(1)} %copy.78, bf16[128,128,512]{1,0,2:T(8,128)(2,1)} %copy.77, pred[128,128]{1,0:T(8,128)(4,1)S(1)} %get-tuple-element.187, pred[128,128]{1,0:T(8,128)(4,1)S(1)} %get-tuple-element.186), kind=kOutput, calls=%fused_computation.14 | convolution fusion | flops 83886080 | bytes 18382848 | tf_op jit(solution)/shard_map/abc,jbc->jac/dot_general | solution.py:65
  289.2 12.4 %fusion.58 = f32[4,128,512]{1,0,2:T(4,128)S(1)} fusion(f32[512,4,128]{2,1,0:T(4,128)} %fusion.1, bf16[128,128,512]{1,0,2:T(8,128)(2,1)} %copy.81, pred[128,128]{1,0:T(8,128)(4,1)S(1)} %get-tuple-element.189, pred[128,128]{1,0:T(8,128)(4,1)S(1)} %get-tuple-element.188, bf16[3,128,512]{1,0,2:T(4,128)(2,1)S(1)} %copy.80, bf16[1,128,512]{1,0,2:T(2,128)(2,1)S(1)} %copy.79), kind=kOutput, calls=%fused_computation.132 | convolution fusion | flops 85196800 | bytes 19431424 | tf_op jit(solution)/shard_map/abc,jbc->jac/dot_general | solution.py:66
  304.6 12.8 %all-gather.1 = bf16[8,1,512]{2,1,0:T(2,128)(2,1)S(1)} all-gather(bf16[1,1,512]{2,1,0:T(2,128)(2,1)S(1)} %reshape.250), channel_id=1, replica_groups=mesh['seq'=4,'ch'=8] {'ch'}, dimensions={0}, use_global_device_ids=true | all-gather | bytes 9216 | tf_op jit(solution)/shard_map/all_gather | solution.py:150
  317.5 17.0 %copy.83 = bf16[4096,3,512]{0,2,1:T(8,128)(2,1)} copy(bf16[4096,3,512]{2,0,1:T(8,128)(2,1)} %param.25) | data formatting | bytes 25165824 | tf_op args[5]
  336.2 13.6 %all-gather.9.cloned.1.call-done = bf16[512,4096]{1,0:T(8,128)(2,1)} async-done(((bf16[512,512]{1,0:T(8,128)(2,1)}), bf16[512,4096]{1,0:T(8,128)(2,1)}) %all-gather.9.cloned.1.call-update) | async-done | bytes 4194320 | tf_op jit(solution)/shard_map/all_gather | solution.py:149
  354.9 11.2 %convolution_convert_fusion.2 = bf16[512,1536]{1,0:T(8,128)(2,1)S(1)} fusion(bf16[512,4096]{1,0:T(8,128)(2,1)S(1)} %fusion.9, bf16[4096,1536]{0,1:T(8,128)(2,1)} %bitcast.194), kind=kOutput, calls=%fused_computation.96 | convolution fusion | flops 6443237376 | bytes 18350080 | tf_op jit(solution)/shard_map/dot_general | solution.py:157
  439.5 12.3 %all_to_all.81 = bf16[4,512,128]{2,1,0:T(8,128)(2,1)S(1)} all-to-all(bf16[4,512,128]{2,1,0:T(8,128)(2,1)S(1)} %bitcast.212), channel_id=1, replica_groups=mesh['seq'=4,'ch'=8] {'seq'}, dimensions={0} | all-to-all | bytes 1048576 | tf_op jit(solution)/shard_map/all_to_all | solution.py:142
  521.8 48.3 %reduce-scatter.3.cloned.1.call-done = bf16[512,512]{1,0:T(8,128)(2,1)} async-done(((bf16[512,4096]{1,0:T(8,128)(2,1)}), bf16[512,512]{1,0:T(8,128)(2,1)}) %reduce-scatter.3.cloned.1.call-update) | async-done | bytes 524304 | tf_op jit(solution)/shard_map/reduce_scatter | solution.py:195
  571.6 13.8 %psum.35 = f32[512]{0:T(512)S(1)} all-reduce(f32[512]{0:T(512)S(1)} %get-tuple-element.123), channel_id=1, replica_groups=mesh['seq'=4,'ch'=8] {'ch'}, use_global_device_ids=true, to_apply=%region_9.12 | all-reduce | flops 512 | bytes 4096 | tf_op jit(solution)/shard_map/psum | solution.py:200
  635.0 47.0 %reduce-scatter.5.cloned.1.call-done = bf16[512,512]{1,0:T(8,128)(2,1)} async-done(((bf16[512,4096]{1,0:T(8,128)(2,1)}), bf16[512,512]{1,0:T(8,128)(2,1)}) %reduce-scatter.5.cloned.1.call-update) | async-done | bytes 524304 | tf_op jit(solution)/shard_map/reduce_scatter | solution.py:195
  683.6 13.8 %psum.36 = f32[512]{0:T(512)S(1)} all-reduce(f32[512]{0:T(512)S(1)} %get-tuple-element.125), channel_id=1, replica_groups=mesh['seq'=4,'ch'=8] {'ch'}, use_global_device_ids=true, to_apply=%region_12.15 | all-reduce | flops 512 | bytes 4096 | tf_op jit(solution)/shard_map/psum | solution.py:200
  719.8 74.7 %all-to-all-done.5 = bf16[512,4,1024]{0,2,1:T(8,128)(2,1)} async-done(((bf16[512,4,1024]{0,2,1:T(8,128)(2,1)}), bf16[512,4,1024]{0,2,1:T(8,128)(2,1)}, u32[]{:S(2)}, u32[]{:S(2)}) %all-to-all-start.5) | async-done | bytes 4194336 | tf_op jit(solution)/shard_map/all_to_all | solution.py:169
  808.4 12.7 %convolution_convert_fusion = bf16[4,1024,1536]{2,1,0:T(8,128)(2,1)} fusion(bf16[4,512,1536]{2,1,0:T(8,128)(2,1)} %bitcast.198, bf16[512,4,1024]{0,2,1:T(8,128)(2,1)} %all-to-all-done.5), kind=kOutput, calls=%fused_computation.11 | convolution fusion | flops 6448742400 | bytes 23068672 | tf_op jit(solution)/shard_map/dot_general | solution.py:172
  855.9 17.8 %all-reduce.3.cloned.1.call-done = bf16[512,512]{1,0:T(8,128)(2,1)} async-done(((bf16[512,512]{1,0:T(8,128)(2,1)}), bf16[512,512]{1,0:T(8,128)(2,1)}) %all-reduce.3.cloned.1.call-update) | async-done | bytes 524304 | tf_op jit(solution)/shard_map/psum | solution.py:293
  875.8 69.7 %all-gather.11.cloned.1.call-done = bf16[2048,1536]{0,1:T(8,128)(2,1)} async-done(((bf16[512,1536]{0,1:T(8,128)(2,1)}), bf16[2048,1536]{0,1:T(8,128)(2,1)}) %all-gather.11.cloned.1.call-update) | async-done | bytes 6291472 | tf_op jit(solution)/shard_map/all_gather | solution.py:170
  954.1 12.7 %convolution_convert_fusion.1 = bf16[4,1024,1536]{2,1,0:T(8,128)(2,1)} fusion(bf16[4,512,1536]{2,1,0:T(8,128)(2,1)} %bitcast.197, bf16[512,4,1024]{0,2,1:T(8,128)(2,1)} %all-to-all-done.4), kind=kOutput, calls=%fused_computation.12 | convolution fusion | flops 6448742400 | bytes 23068672 | tf_op jit(solution)/shard_map/dot_general | solution.py:172
  (400 shorter events, 339.4 us)
Async XLA Ops:
  7.2 53.0 %all-gather.7.cloned.1.call-start = ((), (), s32[]{:S(2)}) async-start(), calls=%async_computation.8 | async-start | bytes 4718592 | tf_op jit(solution)/shard_map/all_gather | solution.py:149
  10.2 339.6 %all-gather.9.cloned.1.call-start = ((), (), s32[]{:S(2)}) async-start(), calls=%async_computation.9 | async-start | bytes 4718592 | tf_op jit(solution)/shard_map/all_gather | solution.py:149
  42.5 224.3 %copy-start.26 = (f32[3,512]{1,0:T(4,128)}, f32[3,512]{1,0:T(4,128)S(1)}, u32[]{:S(2)}) copy-start(f32[3,512]{1,0:T(4,128)S(1)} %get-tuple-element.180) | copy-start | bytes 18436
  42.5 224.3 %copy-start.28 = (f32[3,512]{1,0:T(4,128)}, f32[3,512]{1,0:T(4,128)S(1)}, u32[]{:S(2)}) copy-start(f32[3,512]{1,0:T(4,128)S(1)} %get-tuple-element.181) | copy-start | bytes 18436
  42.5 224.3 %copy-start.30 = (f32[3,512]{1,0:T(4,128)}, f32[3,512]{1,0:T(4,128)S(1)}, u32[]{:S(2)}) copy-start(f32[3,512]{1,0:T(4,128)S(1)} %get-tuple-element.182) | copy-start | bytes 18436
  42.5 224.3 %copy-start.32 = (f32[3,512]{1,0:T(4,128)}, f32[3,512]{1,0:T(4,128)S(1)}, u32[]{:S(2)}) copy-start(f32[3,512]{1,0:T(4,128)S(1)} %get-tuple-element.183) | copy-start | bytes 18436
  42.6 224.3 %copy-start.34 = (f32[3,512]{1,0:T(4,128)}, f32[3,512]{1,0:T(4,128)S(1)}, u32[]{:S(2)}) copy-start(f32[3,512]{1,0:T(4,128)S(1)} %get-tuple-element.184) | copy-start | bytes 18436
  42.6 224.3 %copy-start.36 = (f32[3,512]{1,0:T(4,128)}, f32[3,512]{1,0:T(4,128)S(1)}, u32[]{:S(2)}) copy-start(f32[3,512]{1,0:T(4,128)S(1)} %get-tuple-element.185) | copy-start | bytes 18436
  78.1 186.8 %collective-permute-start = (bf16[6,3,512]{2,0,1:T(8,128)(2,1)S(1)}, bf16[6,3,512]{2,0,1:T(8,128)(2,1)S(1)}, u32[]{:S(2)}, u32[]{:S(2)}) collective-permute-start(bf16[6,3,512]{2,0,1:T(8,128)(2,1)S(1)} %bitcast.223), channel_id=1, source_target_pairs={{0,8},{8,16},{16,24},{1,9},{9,17},{17,25},{2,10},{10,18},{18,26},{... | collective-permute-start | bytes 55304 | tf_op jit(solution)/shard_map/ppermute | solution.py:13
  81.6 185.3 %copy-start.38 = (f32[1,3,512]{2,1,0:T(4,128)}, f32[1,3,512]{2,1,0:T(4,128)S(1)}, u32[]{:S(2)}) copy-start(f32[1,3,512]{2,1,0:T(4,128)S(1)} %copy.157) | copy-start | bytes 18436
  271.7 17.2 %collective-permute-start.1 = (bf16[128,512]{1,0:T(8,128)(2,1)S(1)}, bf16[128,512]{1,0:T(8,128)(2,1)S(1)}, u32[]{:S(2)}, u32[]{:S(2)}) collective-permute-start(bf16[128,512]{1,0:T(8,128)(2,1)S(1)} %slice_bitcast_fusion.2), channel_id=1, source_target_pairs={{0,8},{8,16},{16,24},{1,9},{9,17},{17,25},{2,10},{10,18},{18,26},{... | collective-permute-start | bytes 393224 | tf_op jit(solution)/shard_map/ppermute | solution.py:13
  367.3 6.9 collective-permute-start.2
  381.3 22.5 %all-to-all-start.2 = ((bf16[512,4,128]{2,0,1:T(8,128)(2,1)}), bf16[512,4,128]{2,0,1:T(8,128)(2,1)}, u32[]{:S(2)}, u32[]{:S(2)}) async-start(bf16[512,4,128]{2,0,1:T(8,128)(2,1)} %copy_bitcast_fusion), calls=%async_computation.2 | async-start | bytes 1048576 | tf_op jit(solution)/shard_map/all_to_all | solution.py:131
  456.7 10.5 %all-to-all-start = ((bf16[512,4,128]{2,0,1:T(8,128)(2,1)}), bf16[512,4,128]{2,0,1:T(8,128)(2,1)S(1)}, u32[]{:S(2)}, u32[]{:S(2)}) async-start(bf16[512,4,128]{2,0,1:T(8,128)(2,1)} %copy.86), calls=%async_computation | async-start | bytes 1048576 | tf_op jit(solution)/shard_map/all_to_all | solution.py:131
  460.6 109.5 %reduce-scatter.3.cloned.1.call-start = ((), (), s32[]{:S(2)}) async-start(), calls=%async_computation.10 | async-start | bytes 4718592 | tf_op jit(solution)/shard_map/reduce_scatter | solution.py:195
  503.0 5.7 collective-permute-start.3
  521.7 160.3 %reduce-scatter.5.cloned.1.call-start = ((), (), s32[]{:S(2)}) async-start(), calls=%async_computation.11 | async-start | bytes 4718592 | tf_op jit(solution)/shard_map/reduce_scatter | solution.py:195
  590.5 10.5 %collective-permute-start.4 = (bf16[128,512]{1,0:T(8,128)(2,1)S(1)}, bf16[128,512]{1,0:T(8,128)(2,1)S(1)}, u32[]{:S(2)}, u32[]{:S(2)}) collective-permute-start(bf16[128,512]{1,0:T(8,128)(2,1)S(1)} %slice.323), channel_id=1, source_target_pairs={{8,0},{16,8},{24,16},{9,1},{17,9},{25,17},{10,2},{18,10},{26,18},{... | collective-permute-start | bytes 393224 | tf_op jit(solution)/shard_map/ppermute | solution.py:13
  614.0 6.6 collective-permute-start.5
  633.2 166.4 %all-gather.13.cloned.1.call-start = ((), (), s32[]{:S(2)}) async-start(), calls=%async_computation.14 | async-start | bytes 7864320 | tf_op jit(solution)/shard_map/all_gather | solution.py:170
  635.0 238.7 %all-reduce.3.cloned.1.call-start = ((), (), s32[]{:S(2)}) async-start(), calls=%async_computation.12 | async-start | bytes 1048576 | tf_op jit(solution)/shard_map/psum | solution.py:293
  700.3 245.2 %all-gather.11.cloned.1.call-start = ((), (), s32[]{:S(2)}) async-start(), calls=%async_computation.13 | async-start | bytes 7864320 | tf_op jit(solution)/shard_map/all_gather | solution.py:170
  708.4 86.1 %all-to-all-start.5 = ((bf16[512,4,1024]{0,2,1:T(8,128)(2,1)}), bf16[512,4,1024]{0,2,1:T(8,128)(2,1)}, u32[]{:S(2)}, u32[]{:S(2)}) async-start(bf16[512,4,1024]{0,2,1:T(8,128)(2,1)} %bitcast.189), calls=%async_computation.7 | async-start | bytes 8388608 | tf_op jit(solution)/shard_map/all_to_all | solution.py:169
  794.5 159.6 %all-to-all-start.4 = ((bf16[512,4,1024]{0,2,1:T(8,128)(2,1)}), bf16[512,4,1024]{0,2,1:T(8,128)(2,1)}, u32[]{:S(2)}, u32[]{:S(2)}) async-start(bf16[512,4,1024]{0,2,1:T(8,128)(2,1)} %bitcast.188), calls=%async_computation.6 | async-start | bytes 8388608 | tf_op jit(solution)/shard_map/all_to_all | solution.py:169
  (47 other events, 646.4 us)
Sparse Core Ops, SparseCore 0:
  10.3 49.8 all-gather.6
  304.7 44.9 all-gather.8
  521.9 48.1 reduce-scatter.2
  633.3 48.6 reduce-scatter.4
  683.7 110.8 all-gather.12
  798.0 75.5 all-reduce.2
  875.5 70.0 all-gather.10
where the time goes:
time: 1010 us; the launch traced here: 997 us
  local copies, waits for them, and re-layouts  336 us (33%)
  waiting for transfers between devices  304 us (30%)
  matrix products  147 us (15%)
  blocking collectives  87.3 us (9%)
  other arithmetic  70.5 us (7%)
  starting transfers between devices  33.6 us (3%)
  between operations  15.8 us (2%)
    reduce_scatter x2, waiting for transfers between devices, project_back(): lax.psum_scatter(partial_sum.astype(jnp.bfloat16), 'ch', scatter_dimensio...  95.3 us
    gather x2, local copies, waits for them, and re-layouts, medium_tables(): jnp.take(medium, jnp.clip(lag_grid, 0, tap_count - 1), axis=0)  90 us
    gather x2, local copies, waits for them, and re-layouts, medium_tables(): jnp.take(medium, jnp.clip(lag_grid + tap_count, 0, tap_count - 1), axis=0)  90 us
    all_to_all x2, waiting for transfers between devices, weight_grad(): lax.all_to_all(normed, 'seq', split_axis=1, concat_axis=0, tiled=True)  74.7 us
    all_gather x2, waiting for transfers between devices, weight_grad(): all_grads = lax.all_gather(flat_grad, 'seq', axis=0, tiled=True)  69.7 us
    unnamed x124, local copies, waits for them, and re-layouts  62 us
    all_gather x2, waiting for transfers between devices, mixer_input(): lax.all_gather(inputs, 'ch', axis=1, tiled=True)  31.1 us
    psum x2, blocking collectives, project_back(): row_terms = lax.psum(jnp.sum(scaled * as_float, axis=1), 'ch')  27.5 us
  transfers between devices with their start and end apart: 17, of which 10 were waited for; matrix products, arithmetic and copies ran while one was open for 34% of the time, Pallas kernels for 0%

commit v1 on v0

v1 whole, which is shorter than its diff:
```python
import functools

import jax
import jax.numpy as jnp
from jax import lax
from jax.experimental import pallas as pl
from jax.experimental.pallas import tpu as pltpu
from jax.sharding import PartitionSpec as P

epsilon = 1e-06
f32 = jnp.float32
bf16 = jnp.bfloat16
LANES = 128
EDGE = 16
VMEM_BYTES = 56 * 2**20


def round_up(value, multiple):
    return -(-value // multiple) * multiple


def call(kernel, grid, in_specs, out_specs, out_shape, scratch, flops, moved, prefetch=0):
    return pl.pallas_call(
        kernel,
        grid_spec=pltpu.PrefetchScalarGridSpec(
            num_scalar_prefetch=prefetch,
            grid=grid,
            in_specs=in_specs,
            out_specs=out_specs,
            scratch_shapes=scratch,
        ),
        out_shape=out_shape,
        compiler_params=pltpu.CompilerParams(vmem_limit_bytes=VMEM_BYTES),
        cost_estimate=pl.CostEstimate(flops=flops, bytes_accessed=moved, transcendentals=0),
    )


def whole(shape):
    return pl.BlockSpec(shape, lambda i, *_: (0,) * len(shape))


def lanes(shape):
    return pl.BlockSpec(shape[:-1] + (LANES,), lambda i, *_: (0,) * (len(shape) - 1) + (i,))


def project_kernel(per_step, features, x_ref, gain_ref, w_ref, p_ref, scale_ref, total, squares):
    step = pl.program_id(0)
    width = x_ref.shape[2]

    @pl.when(step == 0)
    def _():
        total[...] = jnp.zeros_like(total)
        squares[...] = jnp.zeros_like(squares)

    for part in range(per_step):
        x = x_ref[part].astype(f32)
        square = x * x
        running = squares[...]
        for lane in range(width // LANES):
            running = running + square[:, lane * LANES : (lane + 1) * LANES]
        squares[...] = running
        scaled = (x * gain_ref[part]).astype(bf16)
        for j in range(3):
            total[j] += jnp.dot(
                scaled, w_ref[j, part * width : (part + 1) * width, :], preferred_element_type=f32
            )

    @pl.when(step == pl.num_programs(0) - 1)
    def _():
        mean = jnp.sum(squares[...], axis=1, keepdims=True) / features
        scale = lax.rsqrt(mean + epsilon)
        scale_ref[...] = scale
        for j in range(3):
            p_ref[j] = (total[j] * scale).astype(bf16)


def project(chunks, gains, weights, rows):
    count, _, width = chunks.shape
    features, columns = weights.shape[1:]
    per_step = 2 if count % 2 == 0 else 1
    return call(
        functools.partial(project_kernel, per_step, features),
        (count // per_step,),
        [
            pl.BlockSpec((per_step, rows, width), lambda i: (i, 0, 0)),
            pl.BlockSpec((per_step, 1, width), lambda i: (i, 0, 0)),
            pl.BlockSpec((3, per_step * width, columns), lambda i: (0, i, 0)),
        ],
        [whole((3, rows, columns)), whole((rows, 1))],
        [
            jax.ShapeDtypeStruct((3, rows, columns), bf16),
            jax.ShapeDtypeStruct((rows, 1), f32),
        ],
        [pltpu.VMEM((3, rows, columns), f32), pltpu.VMEM((rows, LANES), f32)],
        6 * rows * features * columns,
        6 * features * columns + 2 * rows * features,
    )(chunks, gains, weights)


def back_kernel(g_ref, w_ref, o_ref):
    total = None
    for j in range(3):
        term = lax.dot_general(
            g_ref[j], w_ref[j], (((1,), (1,)), ((), ())), preferred_element_type=f32
        )
        total = term if total is None else total + term
    o_ref[0] = total.astype(bf16)


def project_back(grads, weights, count):
    _, rows, columns = grads.shape
    features = weights.shape[1]
    width = features // count
    return call(
        back_kernel,
        (count,),
        [whole((3, rows, columns)), pl.BlockSpec((3, width, columns), lambda i: (0, i, 0))],
        pl.BlockSpec((1, rows, width), lambda i: (i, 0, 0)),
        jax.ShapeDtypeStruct((count, rows, width), bf16),
        [],
        6 * rows * features * columns,
        6 * features * columns + 2 * rows * features,
    )(grads, weights)


def weight_grad_kernel(gain_ref, x_ref, g_ref, o_ref):
    for j in range(3):
        total = None
        for shard in range(x_ref.shape[0]):
            term = lax.dot_general(
                x_ref[shard, 0], g_ref[shard, j], (((0,), (0,)), ((), ())), preferred_element_type=f32
            )
            total = term if total is None else total + term
        o_ref[j] = total * gain_ref[0]


def weight_grad(columns, grads, gains):
    shards, pieces, rows, width = columns.shape
    out = grads.shape[3]
    return call(
        weight_grad_kernel,
        (pieces,),
        [
            pl.BlockSpec((1, width, 1), lambda i: (i, 0, 0)),
            pl.BlockSpec((shards, 1, rows, width), lambda i: (0, i, 0, 0)),
            whole(grads.shape),
        ],
        pl.BlockSpec((3, width, out), lambda i: (0, i, 0)),
        jax.ShapeDtypeStruct((3, pieces * width, out), f32),
        [],
        6 * shards * pieces * rows * width * out,
        2 * columns.size + 2 * grads.size + 12 * pieces * width * out,
    )(gains, columns, grads)


def fir(source, taps, target, base, rows, forward):
    stride = rows // 8
    each = max(n for n in range(1, 25) if stride % n == 0)
    chunk = 8
    tap_count = taps.shape[0]

    def tile(i, carry):
        first = i * each

        def some_taps(c, sums):
            k0 = c * chunk
            low = base + first - k0 - (chunk - 1) if forward else base + first + k0
            loaded = [
                source[pl.ds(low + n, 8, stride=stride), :] for n in range(each + chunk - 1)
            ]
            sums = list(sums)
            for k in range(chunk):
                tap = taps[pl.ds(k0 + k, 1), :]
                for p in range(each):
                    sums[p] = sums[p] + tap * loaded[p + (chunk - 1 - k if forward else k)]
            return tuple(sums)

        sums = lax.fori_loop(
            0, tap_count // chunk, some_taps, tuple(jnp.zeros((8, LANES), f32) for _ in range(each))
        )
        for p in range(each):
            target[pl.ds(first + p, 8, stride=stride), :] = sums[p]
        return carry

    lax.fori_loop(0, stride // each, tile, 0)


def short_sum(source, short, j, first, rows, sign):
    total = None
    for i in range(short.shape[1]):
        term = short[j, i : i + 1, :] * source[first + sign * i : first + sign * i + rows, :]
        total = term if total is None else total + term
    return total


def first_forward_kernel(
    front, rows, token_ref, p_ref, e_ref, short_ref, medium_ref,
    middle_ref, feature_ref, filtered_ref, onehot, projected, gated, taps, kept,
):
    window, vocab = onehot.shape

    @pl.when(pl.program_id(0) == 0)
    def _():
        grid = lax.broadcasted_iota(jnp.int32, (window, vocab), 1)
        onehot[...] = (grid == token_ref[...]).astype(f32).astype(bf16)

    taps[...] = medium_ref[...].astype(f32)
    later = window - front
    product = None
    for j in (1, 2, 0):
        projected[...] = jnp.dot(onehot[...], p_ref[j], preferred_element_type=f32)
        if j == 0:
            feature = short_sum(projected, short_ref, j, front - EDGE, later + EDGE, -1)
            feature_ref[0] = feature[EDGE:, :]
            kept[...] = feature[: rows + EDGE, :]
        else:
            feature = short_sum(projected, short_ref, j, 8, window - 8, -1)
            feature_ref[j] = feature[front - 8 :, :]
            product = feature if product is None else product * feature
    gated[8:, :] = product.astype(bf16).astype(f32)
    fir(gated, taps, projected, front - EDGE, rows + 2 * EDGE, True)
    filtered_ref[...] = projected[EDGE : rows + 2 * EDGE, :]
    embedded = jnp.dot(
        onehot[front - EDGE : front + rows, :], e_ref[...], preferred_element_type=f32
    )
    middle_ref[...] = (embedded + kept[...] * projected[: rows + EDGE, :]).astype(bf16)


def first_forward(tokens, table, embedding, short, medium, rows, front):
    window = tokens.shape[0]
    _, vocab, columns = table.shape
    later = window - front
    shapes = [
        jax.ShapeDtypeStruct((rows + EDGE, columns), bf16),
        jax.ShapeDtypeStruct((3, later, columns), f32),
        jax.ShapeDtypeStruct((rows + EDGE, columns), f32),
    ]
    return call(
        functools.partial(first_forward_kernel, front, rows),
        (columns // LANES,),
        [whole((window, 1))] + [lanes(a.shape) for a in (table, embedding, short, medium)],
        [lanes(s.shape) for s in shapes],
        shapes,
        [
            pltpu.VMEM((window, vocab), bf16),
            pltpu.VMEM((window, LANES), f32),
            pltpu.VMEM((window, LANES), f32),
            pltpu.VMEM((medium.shape[0], LANES), f32),
            pltpu.VMEM((rows + EDGE, LANES), f32),
        ],
        8 * window * vocab * columns,
        16 * window * columns,
    )(tokens, table, embedding, short, medium)


def first_backward_kernel(
    rows, token_ref, above_ref, feature_ref, filtered_ref, short_ref, medium_ref,
    out_ref, onehot, signal, grad_gated, taps, held,
):
    vocab = onehot.shape[0]
    parts = out_ref.shape[0]

    @pl.when(pl.program_id(0) == 0)
    def _():
        grid = lax.broadcasted_iota(jnp.int32, (vocab, rows), 0)
        onehot[...] = (grid == token_ref[...]).astype(f32).astype(bf16)

    taps[...] = medium_ref[...].astype(f32)
    above = above_ref[...].astype(f32)
    signal[...] = (above * feature_ref[0]).astype(bf16).astype(f32)
    extended = rows + EDGE
    fir(signal, taps, grad_gated, 0, extended, False)

    def keep(j, value):
        held[...] = value.astype(bf16).astype(f32)
        grad = short_sum(held, short_ref, j, 0, rows, 1).astype(bf16)
        total = jnp.dot(onehot[...], grad, preferred_element_type=f32).astype(bf16)
        for part in range(parts):
            size = vocab // parts
            out_ref[part, j] = total[part * size : (part + 1) * size, :]

    keep(0, above[:extended, :] * filtered_ref[...])
    keep(1, grad_gated[...] * feature_ref[2, :extended, :])
    keep(2, grad_gated[...] * feature_ref[1, :extended, :])
    total = jnp.dot(onehot[...], above_ref[:rows, :], preferred_element_type=f32).astype(bf16)
    for part in range(parts):
        size = vocab // parts
        out_ref[part, 3] = total[part * size : (part + 1) * size, :]


def first_backward(tokens, above, features, filtered, short, medium, vocab, parts):
    rows = tokens.shape[1]
    later, columns = above.shape
    shape = jax.ShapeDtypeStruct((parts, 4, vocab // parts, columns), bf16)
    return call(
        functools.partial(first_backward_kernel, rows),
        (columns // LANES,),
        [whole((1, rows))] + [lanes(a.shape) for a in (above, features, filtered, short, medium)],
        lanes(shape.shape),
        shape,
        [
            pltpu.VMEM((vocab, rows), bf16),
            pltpu.VMEM((later, LANES), f32),
            pltpu.VMEM((rows + EDGE, LANES), f32),
            pltpu.VMEM((medium.shape[0], LANES), f32),
            pltpu.VMEM((rows + EDGE, LANES), f32),
        ],
        8 * rows * vocab * columns,
        16 * later * columns,
    )(tokens, above, features, filtered, short, medium)


SEGMENTS = 8


def scan_modes(source, decays, states, length, forward, residues=None, target=None):
    def step(i, held):
        position = i if forward else length - 1 - i
        value = source[pl.ds(position, SEGMENTS, stride=length), :]
        held = tuple(d * s + value for d, s in zip(decays, held))
        if target is not None:
            terms = [r * s for r, s in zip(residues, held)]
            while len(terms) > 1:
                terms = [a + b for a, b in zip(terms[::2], terms[1::2])] + (
                    terms[-1:] if len(terms) % 2 else []
                )
            target[pl.ds(position, SEGMENTS, stride=length), :] = terms[0]
        return held

    return lax.fori_loop(0, length, step, tuple(states), unroll=4)


def spread(ref, count):
    return [jnp.broadcast_to(ref[m : m + 1, :], (SEGMENTS, LANES)) for m in range(count)]


def second_features_kernel(
    p_ref, short_ref, above_ref, rate_ref,
    feature_ref, gated_ref, signal_ref, segment_ref, closing_ref, projected, gated, signal, decay,
):
    rows = above_ref.shape[0]
    modes = rate_ref.shape[0]
    length = rows // SEGMENTS
    product = None
    for j in range(3):
        projected[...] = p_ref[j].astype(f32)
        feature = short_sum(projected, short_ref, j, EDGE, rows, -1)
        feature_ref[j] = feature
        if j == 0:
            rounded = (above_ref[...].astype(f32) * feature).astype(bf16)
            signal_ref[...] = rounded
            signal[...] = rounded.astype(f32)
        else:
            product = feature if product is None else product * feature
    rounded = product.astype(bf16)
    gated_ref[...] = rounded
    gated[...] = rounded.astype(f32)
    rates = rate_ref[...]
    decay[...] = jnp.exp(-rates)
    zeros = [jnp.zeros((SEGMENTS, LANES), f32)] * modes
    for way, source in enumerate((gated, signal)):
        ends = scan_modes(source, spread(decay, modes), zeros, length, way == 0)
        for m in range(modes):
            segment_ref[way, pl.ds(m, SEGMENTS, stride=modes), :] = ends[m]
        stride = jnp.exp(-rates * length)
        total = jnp.zeros((modes, LANES), f32)
        for n in range(SEGMENTS):
            at = n if way == 0 else SEGMENTS - 1 - n
            total = stride * total + segment_ref[way, at * modes : (at + 1) * modes, :]
        closing_ref[way] = total


def second_features(projected, short, above, rates):
    rows, columns = above.shape
    modes = rates.shape[0]
    shapes = [
        jax.ShapeDtypeStruct((3, rows, columns), f32),
        jax.ShapeDtypeStruct((rows, columns), bf16),
        jax.ShapeDtypeStruct((rows, columns), bf16),
        jax.ShapeDtypeStruct((2, SEGMENTS * modes, columns), f32),
        jax.ShapeDtypeStruct((2, modes, columns), f32),
    ]
    return call(
        second_features_kernel,
        (columns // LANES,),
        [lanes(a.shape) for a in (projected, short, above, rates)],
        [lanes(s.shape) for s in shapes],
        shapes,
        [
            pltpu.VMEM((rows + EDGE, LANES), f32),
            pltpu.VMEM((rows, LANES), f32),
            pltpu.VMEM((rows, LANES), f32),
            pltpu.VMEM((modes, LANES), f32),
        ],
        100 * rows * columns,
        24 * rows * columns,
    )(projected, short, above, rates)


def second_filter_kernel(
    shards, seq_ref, feature_ref, gated_ref, signal_ref, segment_ref, closing_ref, rate_ref,
    residue_ref, above_ref, middle_ref,
    out_ref, grad_ref, entering, source, filtered, grad_gated, decay, residue,
):
    rows = above_ref.shape[0]
    modes = rate_ref.shape[0]
    length = rows // SEGMENTS
    me = seq_ref[0]
    rates = rate_ref[...]
    decay[...] = jnp.exp(-rates)
    residue[...] = residue_ref[...]
    stride = jnp.exp(-rates * length)
    for way, (values, target) in enumerate(((gated_ref, filtered), (signal_ref, grad_gated))):
        source[...] = values[...].astype(f32)
        state = jnp.zeros((modes, LANES), f32)
        for shard in range(shards):
            ahead = me - 1 - shard if way == 0 else shard - me - 1
            weight = jnp.exp(-rates * (rows * jnp.maximum(ahead, 0)).astype(f32))
            state = state + jnp.where(ahead >= 0, weight * closing_ref[shard, way], 0.0)
        for n in range(SEGMENTS):
            at = n if way == 0 else SEGMENTS - 1 - n
            entering[at * modes : (at + 1) * modes, :] = state
            state = stride * state + segment_ref[way, at * modes : (at + 1) * modes, :]
        starts = [entering[pl.ds(m, SEGMENTS, stride=modes), :] for m in range(modes)]
        scan_modes(
            source, spread(decay, modes), starts, length, way == 0, spread(residue, modes), target
        )
    above = above_ref[...].astype(f32)
    out_ref[...] = (middle_ref[EDGE:, :].astype(f32) + feature_ref[0] * filtered[...]).astype(bf16)
    grad_ref[0] = (above * filtered[...]).astype(bf16)
    grad_ref[1] = (grad_gated[...] * feature_ref[2]).astype(bf16)
    grad_ref[2] = (grad_gated[...] * feature_ref[1]).astype(bf16)


def second_filter(seq, features, gated, signal, segments, closings, rates, residues, above, middle):
    rows, columns = above.shape
    modes = rates.shape[0]
    shapes = [
        jax.ShapeDtypeStruct((rows, columns), bf16),
        jax.ShapeDtypeStruct((3, rows, columns), bf16),
    ]
    operands = (features, gated, signal, segments, closings, rates, residues, above, middle)
    return call(
        functools.partial(second_filter_kernel, closings.shape[0]),
        (columns // LANES,),
        [lanes(a.shape) for a in operands],
        [lanes(s.shape) for s in shapes],
        shapes,
        [pltpu.VMEM((SEGMENTS * modes, LANES), f32)]
        + [pltpu.VMEM((rows, LANES), f32)] * 3
        + [pltpu.VMEM((modes, LANES), f32)] * 2,
        140 * rows * columns,
        28 * rows * columns,
        prefetch=1,
    )(seq, *operands)


def second_grads_kernel(grad_ref, halo_ref, p_ref, short_ref, scale_ref, out_ref, term_ref, held):
    rows = grad_ref.shape[1]
    scale = scale_ref[...]
    terms = None
    for j in range(3):
        held[:rows, :] = grad_ref[j].astype(f32)
        held[rows:, :] = halo_ref[j].astype(f32)
        grad = short_sum(held, short_ref, j, 0, rows, 1)
        term = grad * p_ref[j, EDGE:, :].astype(f32)
        terms = term if terms is None else terms + term
        out_ref[j] = (grad * scale).astype(bf16)
    total = jnp.sum(terms, axis=1, keepdims=True)

    @pl.when(pl.program_id(0) == 0)
    def _():
        term_ref[...] = total

    @pl.when(pl.program_id(0) > 0)
    def _():
        term_ref[...] += total


def second_grads(grads, halo, projected, short, scale):
    _, rows, columns = grads.shape
    shapes = [
        jax.ShapeDtypeStruct((3, rows, columns), bf16),
        jax.ShapeDtypeStruct((rows, 1), f32),
    ]
    return call(
        second_grads_kernel,
        (columns // LANES,),
        [lanes(a.shape) for a in (grads, halo, projected, short)] + [whole((rows, 1))],
        [lanes(shapes[0].shape), whole((rows, 1))],
        shapes,
        [pltpu.VMEM((rows + EDGE, LANES), f32)],
        60 * rows * columns,
        24 * rows * columns,
    )(grads, halo, projected, short, scale)


def shift(value, axis, by):
    devices = lax.axis_size(axis)
    pairs = [(i, i + by) for i in range(devices) if 0 <= i + by < devices]
    return lax.ppermute(value, axis, pairs)


def gather_ch(value):
    return lax.all_gather(value, "ch", axis=0, tiled=False)


def scatter_ch(value):
    return lax.psum_scatter(value, "ch", scatter_dimension=0, tiled=False)


def gather_seq(value):
    return lax.all_gather(value, "seq", axis=0, tiled=False)


def exchange_seq(value):
    return lax.all_to_all(value, "seq", split_axis=0, concat_axis=0, tiled=True)


def per_device(
    token_ids,
    embedding,
    gain_first,
    gain_second,
    weights_first,
    weights_second,
    short_first,
    short_second,
    medium,
    residues,
    decay_rates,
    cotangent,
):
    shards = lax.axis_size("seq")
    pieces = lax.axis_size("ch")
    seq = lax.axis_index("seq")
    vocab, width = embedding.shape
    rows = token_ids.shape[0]
    features = width * pieces
    taps, tap_count = medium.shape[0], short_first.shape[0]
    front = round_up(EDGE + taps - 1 + tap_count - 1, 16)
    back = round_up(EDGE + taps - 1, 16)
    w_first, w_second = (jnp.transpose(w, (1, 0, 2)) for w in (weights_first, weights_second))
    s_first, s_second = (jnp.transpose(s, (1, 0, 2)) for s in (short_first, short_second))

    gains = jnp.concatenate(
        [gain_first[None], gain_second[None], jnp.zeros((EDGE - 2, width), bf16)], axis=0
    )
    gathered = gather_ch(jnp.concatenate([embedding, gains], axis=0))
    gains_first = gathered[:, vocab : vocab + 1, :].astype(f32)
    gains_second = gathered[:, vocab + 1 : vocab + 2, :].astype(f32)
    table, scale_table = project(gathered, gains_first, w_first, vocab)

    tokens = lax.all_gather(token_ids, "seq", axis=0, tiled=True)
    tokens = jnp.pad(tokens, (front, back), constant_values=-1)
    tokens = lax.dynamic_slice_in_dim(tokens, seq * rows, front + rows + back, 0)
    middle, features_first, filtered_first = first_forward(
        tokens[:, None], table, embedding, s_first, medium, rows, front
    )

    middles = gather_ch(middle)
    projected, scale = project(middles, gains_second, w_second, rows + EDGE)
    features_second, gated, signal, segments, closing = second_features(
        projected, s_second, cotangent, decay_rates
    )
    closings = gather_seq(closing)
    output, grad_featured = second_filter(
        seq[None], features_second, gated, signal, segments, closings,
        decay_rates, residues, cotangent, middle,
    )
    halo = shift(grad_featured[:, :EDGE, :], "seq", -1)
    scale = scale[EDGE:]
    grads, terms = second_grads(grad_featured, halo, projected, s_second, scale)
    terms = lax.psum(terms[:, 0], "ch")
    grad_normed = scatter_ch(project_back(grads, w_second, pieces)).astype(f32)
    as_float = middle[EDGE:].astype(f32)
    grad_middle = (
        cotangent.astype(f32)
        + gain_second.astype(f32) * grad_normed
        - as_float * (scale * scale) * terms[:, None] / features
    ).astype(bf16)
    grad_gain_second = jnp.sum(grad_normed * as_float, axis=0)

    each = pieces // shards
    own = middles[:, EDGE:, :].reshape(shards, each, rows, width)
    columns = exchange_seq(own)
    block_gains = lax.dynamic_slice_in_dim(gains_second, seq * each, each, 0)
    grad_weights_second = weight_grad(
        columns, gather_seq(grads), jnp.swapaxes(block_gains, 1, 2)
    )

    above = jnp.concatenate([grad_middle, shift(grad_middle[:back], "seq", -1)], axis=0)
    sums = first_backward(
        token_ids[None], above, features_first, filtered_first, s_first, medium, vocab, shards
    )
    own_sums = jnp.sum(exchange_seq(sums).astype(f32), axis=0)
    share = vocab // shards
    at = seq * share
    own_scale = lax.dynamic_slice_in_dim(scale_table, at, share, 0)
    own_table = lax.dynamic_slice_in_dim(table, at, share, 1).astype(f32)
    own_embedding = lax.dynamic_slice_in_dim(embedding, at, share, 0).astype(f32)
    own_grads = own_sums[:3]
    terms = lax.psum(jnp.sum(own_grads * own_table, axis=(0, 2)), "ch")
    own_grads = (own_grads * own_scale[None]).astype(bf16)
    grad_normed = scatter_ch(project_back(own_grads, w_first, pieces)).astype(f32)
    grad_embedding = (
        own_sums[3]
        + gain_first.astype(f32) * grad_normed
        - own_embedding * (own_scale * own_scale) * terms[:, None] / features
    )
    grad_gain_first = jnp.sum(grad_normed * own_embedding, axis=0)
    last = jnp.concatenate(
        [
            grad_embedding,
            grad_gain_first[None],
            grad_gain_second[None],
            jnp.zeros((6, width), f32),
        ],
        axis=0,
    )
    last = gather_seq(last)
    block = lax.dynamic_slice_in_dim(gathered, seq * each, each, 0)[:, :vocab, :]
    block_gains = lax.dynamic_slice_in_dim(gains_first, seq * each, each, 0)
    all_grads = jnp.swapaxes(gather_seq(own_grads), 0, 1).reshape(1, 3, vocab, width)
    grad_weights_first = weight_grad(block[None], all_grads, jnp.swapaxes(block_gains, 1, 2))
    return (
        output,
        last[:, :share].reshape(vocab, width),
        jnp.sum(last[:, share], axis=0),
        jnp.sum(last[:, share + 1], axis=0),
        jnp.transpose(grad_weights_first, (1, 0, 2)),
        jnp.transpose(grad_weights_second, (1, 0, 2)),
    )


def solution(mesh):
    placed = (
        P("seq"),
        P(None, "ch"),
        P("ch"),
        P("ch"),
        P(None, None, "ch"),
        P(None, None, "ch"),
        P(None, None, "ch"),
        P(None, None, "ch"),
        P(None, "ch"),
        P(None, "ch"),
        P(None, "ch"),
        P("seq", "ch"),
    )
    return jax.shard_map(
        per_device,
        mesh=mesh,
        in_specs=placed,
        out_specs=(
            P("seq", "ch"),
            P(None, "ch"),
            P("ch"),
            P("ch"),
            P("seq", None, "ch"),
            P("seq", None, "ch"),
        ),
        check_vma=False,
    )
```

time: 1010 us -> 514 us (0.51); the launches traced: 997 us -> 512 us
  local copies, waits for them, and re-layouts: 336 us -> 20.1 us
  matrix products: 147 us -> 0 us
  Pallas kernels: 0 us -> 125 us
  other arithmetic: 70.5 us -> 13.4 us
  blocking collectives: 87.3 us -> 50.8 us
  waiting for transfers between devices: 304 us -> 277 us
  starting transfers between devices: 33.6 us -> 11.6 us
    gather x6 -> x0, local copies, waits for them, and re-layouts: 195 us -> none  [the longest x2 90 us: medium_tables(): jnp.take(medium, jnp.clip(lag_grid, 0, tap_count - 1), axis=0)]
    dot_general x18 -> x0, matrix products: 147 us -> none  [the longest x2 25.4 us: weight_grad(): lax.dot_general(columns.reshape(group_count, row_count, rows_each), all_g...]
    pallas_call x0 -> x11, Pallas kernels: none -> 125 us  [the longest x2 23.7 us: project(): call(functools.partial(project_kernel, per_step, features), (count // per...]
    all_gather x4 -> x5, waiting for transfers between devices: 101 us -> 175 us  [the longest x2 88 us: gather_ch(): return lax.all_gather(value, 'ch', axis=0, tiled=False)]
    unnamed x124 -> x16, local copies, waits for them, and re-layouts: 62 us -> 1.56 us
    reduce_scatter x2, waiting for transfers between devices: 95.3 us -> 39 us  [scatter_ch(): return lax.psum_scatter(value, 'ch', scatter_dimension=0, tiled=False)]
    all_to_all x4 -> x2, waiting for transfers between devices: 81.2 us -> 51.8 us  [exchange_seq(): return lax.all_to_all(value, 'seq', split_axis=0, concat_axis=0, tiled=True)]
    reduce_sum x6 -> x3, other arithmetic: 29.2 us -> 3.74 us  [the longest x1 1.9 us: per_device(): terms = lax.psum(jnp.sum(own_grads * own_table, axis=(0, 2)), 'ch')]
  transfers between devices with their start and end apart: 17 -> 11, of which waited for: 10 -> 11; matrix products, arithmetic and copies ran while one was open for 34% -> 3% of each run, Pallas kernels for 0% -> 3%
where the time goes in v1:
time: 514 us; the launch traced here: 512 us
  waiting for transfers between devices  277 us (54%)
  Pallas kernels  125 us (24%)
  blocking collectives  50.8 us (10%)
  local copies, waits for them, and re-layouts  20.1 us (4%)
  between operations  14.3 us (3%)
  other arithmetic  13.4 us (3%)
  starting transfers between devices  11.6 us (2%)
    all_gather x2, waiting for transfers between devices, gather_ch(): return lax.all_gather(value, 'ch', axis=0, tiled=False)  88 us
    all_gather x3, waiting for transfers between devices, gather_seq(): return lax.all_gather(value, 'seq', axis=0, tiled=False)  87.4 us
    all_to_all x2, waiting for transfers between devices, exchange_seq(): return lax.all_to_all(value, 'seq', split_axis=0, concat_axis=0, tiled=True)  51.8 us
    reduce_scatter x2, waiting for transfers between devices, scatter_ch(): return lax.psum_scatter(value, 'ch', scatter_dimension=0, tiled=False)  39 us
    pallas_call x2, Pallas kernels, project(): call(functools.partial(project_kernel, per_step, features), (count // per...  23.7 us
    pallas_call x2, Pallas kernels, project_back(): call(back_kernel, (count,), [whole((3, rows, columns)), pl.BlockSpec((3,...  23.1 us
    pallas_call x1, Pallas kernels, first_forward(): call(functools.partial(first_forward_kernel, front, rows), (columns // LA...  19.3 us
    pallas_call x2, Pallas kernels, weight_grad(): call(weight_grad_kernel, (pieces,), [pl.BlockSpec((1, width, 1), lambda i...  17.5 us
  transfers between devices with their start and end apart: 11, of which 11 were waited for; matrix products, arithmetic and copies ran while one was open for 3% of the time, Pallas kernels for 3%

profile of v1, /device:TPU:0, one launch (start us, length us, event | category | flops | bytes accessed | tf_op | source)
XLA Modules:
  0.0 512.2 jit_solution(16105100769562013656)
XLA Ops:
  10.8 9.5 %all-gather.6 = s32[4,1,512]{2,1,0:T(1,128)S(1)} all-gather(s32[1,1,512]{2,1,0:T(1,128)S(1)} %bitcast.59), channel_id=1, replica_groups=mesh['seq'=4,'ch'=8] {'seq'}, dimensions={0}, use_global_device_ids=true | all-gather | bytes 10240 | tf_op jit(solution)/shard_map/all_gather | solution.py:554
  21.3 40.7 %all-gather.13.cloned.1.call-done = bf16[4224,512]{1,0:T(8,128)(2,1)} async-done(((bf16[528,512]{1,0:T(8,128)(2,1)}), bf16[4224,512]{1,0:T(8,128)(2,1)}) %all-gather.13.cloned.1.call-update) | async-done | bytes 4325392 | tf_op jit(solution)/shard_map/all_gather | solution.py:505
  63.6 11.7 %shard_map.163 = (bf16[3,512,512]{2,1,0:T(8,128)(2,1)}, f32[512,1]{1,0:T(8,128)}) custom-call(bf16[8,528,512]{2,1,0:T(8,128)(2,1)} %bitcast.50, f32[8,1,512]{2,1,0:T(1,128)} %get-tuple-element.43.gain_ref, bf16[3,4096,512]{2,1,0:T(8,128)(2,1)} %bitcast.38), custom_call_target="tpu_custom_call" | custom-call | flops 6442450944 | bytes 16777216 | tf_op jit(solution)/shard_map/pallas_call | solution.py:81
  75.3 19.3 %shard_map.164 = (bf16[528,512]{1,0:T(8,128)(2,1)}, f32[3,656,512]{2,1,0:T(8,128)}, f32[528,512]{1,0:T(8,128)}) custom-call(s32[816,1]{1,0:T(8,128)} %broadcast_in_dim.45.token_ref, bf16[3,512,512]{2,1,0:T(8,128)(2,1)} %get-tuple-element.22.p_ref, bf16[512,512]{1,0:T(8,128)(2,1)} %e_ref.1, f32[3,7,512]{2,1,0:T(8,128)} %bitcast.54, bf16[128,512]{1,0:T(8,128)(2,1)} %medium_ref.3), custom_call_target="tpu_custom_call" | custom-call | flops 1711276032 | bytes 6684672 | tf_op jit(solution)/shard_map/pallas_call | solution.py:238
  94.7 47.3 %all-gather.15.cloned.1.call-done = bf16[4224,512]{1,0:T(8,128)(2,1)} async-done(((bf16[528,512]{1,0:T(8,128)(2,1)}), bf16[4224,512]{1,0:T(8,128)(2,1)}) %all-gather.15.cloned.1.call-update) | async-done | bytes 4325392 | tf_op jit(solution)/shard_map/all_gather | solution.py:505
  141.9 11.9 %shard_map.165 = (bf16[3,528,512]{2,1,0:T(8,128)(2,1)}, f32[528,1]{1,0:T(8,128)}) custom-call(bf16[8,528,512]{2,1,0:T(8,128)(2,1)} %bitcast.42, f32[8,1,512]{2,1,0:T(1,128)} %get-tuple-element.42.gain_ref, bf16[3,4096,512]{2,1,0:T(8,128)(2,1)} %bitcast.61), custom_call_target="tpu_custom_call" | custom-call | flops 6643777536 | bytes 16908288 | tf_op jit(solution)/shard_map/pallas_call | solution.py:81
  153.9 9.1 %shard_map.166 = (f32[3,512,512]{2,1,0:T(8,128)}, bf16[512,512]{1,0:T(8,128)(2,1)}, bf16[512,512]{1,0:T(8,128)(2,1)}, f32[2,128,512]{2,1,0:T(8,128)}, f32[2,16,512]{2,1,0:T(8,128)}) custom-call(bf16[3,528,512]{2,1,0:T(8,128)(2,1)} %get-tuple-element.24.p_ref, f32[3,7,512]{2,1,0:T(8,128)} %bitcast.52, bf16[512,512]{1,0:T(8,128)(2,1)} %above_ref.3, ...), custom_call_target="tpu_custom_call" | custom-call | flops 26214400 | bytes 6291456 | tf_op jit(solution)/shard_map/pallas_call | solution.py:383
  163.0 10.5 %all-gather.2 = f32[8,16,512]{2,1,0:T(8,128)} all-gather(f32[2,16,512]{2,1,0:T(8,128)} %get-tuple-element.29), channel_id=4, replica_groups=mesh['seq'=4,'ch'=8] {'seq'}, dimensions={0}, use_global_device_ids=true | all-gather | bytes 327680 | tf_op jit(solution)/shard_map/all_gather | solution.py:513
  173.4 9.7 %shard_map.167 = (bf16[512,512]{1,0:T(8,128)(2,1)}, bf16[3,512,512]{2,1,0:T(8,128)(2,1)}) custom-call(s32[1]{0:T(128)} %bitcast.seq_ref, f32[3,512,512]{2,1,0:T(8,128)} %get-tuple-element.25.feature_ref, bf16[512,512]{1,0:T(8,128)(2,1)} %get-tuple-element.26.gated_ref, bf16[512,512]{1,0:T(8,128)(2,1)} %get-tuple-element.27.signal_ref, ...), custom_call_target="tpu_custom_call" | custom-call | flops 36700160 | bytes 7340032 | tf_op jit(solution)/shard_map/pallas_call | solution.py:443
  190.5 6.0 %shard_map.168 = (bf16[3,512,512]{2,1,0:T(8,128)(2,1)}, f32[512,1]{1,0:T(8,128)}) custom-call(bf16[3,512,512]{2,1,0:T(8,128)(2,1)} %get-tuple-element.31.grad_ref, bf16[3,16,512]{2,1,0:T(8,128)(2,1)} %copy-done.4, bf16[3,528,512]{2,1,0:T(8,128)(2,1)} %get-tuple-element.24.p_ref, f32[3,7,512]{2,1,0:T(8,128)} %bitcast.53, f32[512,1]{1,0:T(8,128)} %get-tuple-element.51.scale_ref), custom_call_target="tpu_custom_call" | custom-call | flops 15728640 | bytes 6291456 | tf_op jit(solution)/shard_map/pallas_call | solution.py:486
  196.6 12.9 %shard_map.169 = bf16[8,512,512]{2,1,0:T(8,128)(2,1)} custom-call(bf16[3,512,512]{2,1,0:T(8,128)(2,1)} %get-tuple-element.33.g_ref, bf16[3,4096,512]{2,1,0:T(8,128)(2,1)} %bitcast.62), custom_call_target="tpu_custom_call" | custom-call | flops 6442450944 | bytes 16777216 | tf_op jit(solution)/shard_map/pallas_call | solution.py:114
  210.6 14.0 %psum.14 = f32[512]{0:T(512)S(1)} all-reduce(f32[512]{0:T(512)S(1)} %reduce.3), channel_id=1, replica_groups=mesh['seq'=4,'ch'=8] {'ch'}, use_global_device_ids=true, to_apply=%region_1.2 | all-reduce | flops 512 | bytes 4096 | tf_op jit(solution)/shard_map/psum | solution.py:574
  224.6 33.1 %reduce-scatter.3.cloned.1.call-done = bf16[1,512,512]{2,1,0:T(8,128)(2,1)} async-done(((bf16[8,512,512]{2,1,0:T(8,128)(2,1)}), bf16[1,512,512]{2,1,0:T(8,128)(2,1)}) %reduce-scatter.3.cloned.1.call-update) | async-done | bytes 524304 | tf_op jit(solution)/shard_map/reduce_scatter | solution.py:509
  260.6 5.7 %collective-permute-done.1 = bf16[144,512]{1,0:T(8,128)(2,1)S(1)} collective-permute-done((bf16[144,512]{1,0:T(8,128)(2,1)S(1)}, bf16[144,512]{1,0:T(8,128)(2,1)S(1)}, u32[]{:S(2)}, u32[]{:S(2)}) %collective-permute-start.1) | collective-permute-done | bytes 147488 | tf_op jit(solution)/shard_map/ppermute | solution.py:501
  267.2 16.7 %shard_map.170 = bf16[4,4,128,512]{3,2,1,0:T(8,128)(2,1)} custom-call(s32[1,512]{1,0:T(1,128)} %bitcast.58, bf16[656,512]{1,0:T(8,128)(2,1)} %pad_maximum_fusion.above_ref, f32[3,656,512]{2,1,0:T(8,128)} %get-tuple-element.35.feature_ref, f32[528,512]{1,0:T(8,128)} %get-tuple-element.36.filtered_ref, f32[3,7,512]{2,1,0:T(8,128)} %bitcast.55, ...), custom_call_target="tpu_custom_call" | custom-call | flops 1073741824 | bytes 5373952 | tf_op jit(solution)/shard_map/pallas_call | solution.py:295
  288.5 21.5 %all-to-all-done = bf16[4,4,128,512]{3,2,1,0:T(8,128)(2,1)S(1)} async-done(((bf16[4,4,128,512]{3,2,1,0:T(8,128)(2,1)}), bf16[4,4,128,512]{3,2,1,0:T(8,128)(2,1)S(1)}, u32[]{:S(2)}, u32[]{:S(2)}) %all-to-all-start) | async-done | bytes 2097184 | tf_op jit(solution)/shard_map/all_to_all | solution.py:517
  312.3 10.1 %shard_map.171 = bf16[8,128,512]{2,1,0:T(8,128)(2,1)} custom-call(bf16[3,128,512]{2,1,0:T(8,128)(2,1)} %get-tuple-element.47.g_ref, bf16[3,4096,512]{2,1,0:T(8,128)(2,1)} %bitcast.39), custom_call_target="tpu_custom_call" | custom-call | flops 1610612736 | bytes 13631488 | tf_op jit(solution)/shard_map/pallas_call | solution.py:114
  333.2 16.9 %psum.15 = f32[128]{0:T(128)S(1)} all-reduce(f32[128]{0:T(128)S(1)} %get-tuple-element.46), channel_id=1, replica_groups=mesh['seq'=4,'ch'=8] {'ch'}, use_global_device_ids=true, to_apply=%region_5.6 | all-reduce | flops 128 | bytes 1024 | tf_op jit(solution)/shard_map/psum | solution.py:603
  350.1 5.8 %reduce-scatter.5.cloned.1.call-done = bf16[1,128,512]{2,1,0:T(8,128)(2,1)} async-done(((bf16[8,128,512]{2,1,0:T(8,128)(2,1)}), bf16[1,128,512]{2,1,0:T(8,128)(2,1)}) %reduce-scatter.5.cloned.1.call-update) | async-done | bytes 131088 | tf_op jit(solution)/shard_map/reduce_scatter | solution.py:509
  363.6 30.3 %all-to-all-done.1.x_ref = bf16[4,2,512,512]{3,2,1,0:T(8,128)(2,1)} async-done(((bf16[4,2,512,512]{3,2,1,0:T(8,128)(2,1)}), bf16[4,2,512,512]{3,2,1,0:T(8,128)(2,1)}, u32[]{:S(2)}, u32[]{:S(2)}) %all-to-all-start.1) | async-done | bytes 4194336 | tf_op jit(solution)/shard_map/all_to_all | solution.py:517
  393.9 45.9 %all-gather.21.cloned.1.call-done = bf16[12,512,512]{2,1,0:T(8,128)(2,1)} async-done(((bf16[3,512,512]{2,1,0:T(8,128)(2,1)}), bf16[12,512,512]{2,1,0:T(8,128)(2,1)}) %all-gather.21.cloned.1.call-update) | async-done | bytes 6291472 | tf_op jit(solution)/shard_map/all_gather | solution.py:513
  439.8 12.1 %shard_map.173 = f32[3,1024,512]{2,1,0:T(8,128)} custom-call(f32[2,512,1]{2,1,0:T(8,128)} %transpose.44.gain_ref, bf16[4,2,512,512]{3,2,1,0:T(8,128)(2,1)} %all-to-all-done.1.x_ref, bf16[4,3,512,512]{3,2,1,0:T(8,128)(2,1)} %bitcast.63), custom_call_target="tpu_custom_call" | custom-call | flops 6442450944 | bytes 16777216 | tf_op jit(solution)/shard_map/pallas_call | solution.py:140
  451.9 20.6 %all-gather.19.cloned.1.call-done = bf16[12,128,512]{2,1,0:T(8,128)(2,1)} async-done(((bf16[3,128,512]{2,1,0:T(8,128)(2,1)}), bf16[12,128,512]{2,1,0:T(8,128)(2,1)}) %all-gather.19.cloned.1.call-update) | async-done | bytes 1572880 | tf_op jit(solution)/shard_map/all_gather | solution.py:513
  480.5 21.0 %all-gather.17.cloned.1.call-done = f32[544,512]{1,0:T(8,128)} async-done(((f32[136,512]{1,0:T(8,128)}), f32[544,512]{1,0:T(8,128)}) %all-gather.17.cloned.1.call-update) | async-done | bytes 1114128 | tf_op jit(solution)/shard_map/all_gather | solution.py:513
  (68 shorter events, 55.4 us)
Async XLA Ops:
  7.2 3.6 copy-start.5
  7.2 54.8 %all-gather.13.cloned.1.call-start = ((), (), s32[]{:S(2)}) async-start(), calls=%async_computation.6 | async-start | bytes 4866048 | tf_op jit(solution)/shard_map/all_gather | solution.py:505
  10.7 131.2 %all-gather.15.cloned.1.call-start = ((), (), s32[]{:S(2)}) async-start(), calls=%async_computation.7 | async-start | bytes 4866048 | tf_op jit(solution)/shard_map/all_gather | solution.py:505
  94.6 163.1 %reduce-scatter.3.cloned.1.call-start = ((), (), s32[]{:S(2)}) async-start(), calls=%async_computation.4 | async-start | bytes 4718592 | tf_op jit(solution)/shard_map/reduce_scatter | solution.py:509
  173.4 11.8 %copy-start.3 = (f32[528,1]{1,0:T(8,128)S(1)}, f32[528,1]{1,0:T(8,128)}, u32[]{:S(2)}) copy-start(f32[528,1]{1,0:T(8,128)} %get-tuple-element.32) | copy-start | bytes 6340
  183.9 6.0 %collective-permute-start = (bf16[3,16,512]{2,1,0:T(8,128)(2,1)S(1)}, bf16[3,16,512]{2,1,0:T(8,128)(2,1)S(1)}, u32[]{:S(2)}, u32[]{:S(2)}) collective-permute-start(bf16[3,16,512]{2,1,0:T(8,128)(2,1)S(1)} %slice.41), channel_id=1, source_target_pairs={{8,0},{16,8},{24,16},{9,1},{17,9},{25,17},{10,2},{18,10},{26,18},{... | collective-permute-start | bytes 147464 | tf_op jit(solution)/shard_map/ppermute | solution.py:501
  189.9 0.6 copy-start.4
  209.5 0.7 copy-start.6
  209.5 1.0 copy-start.2
  209.5 48.3 %copy-start = (bf16[528,512]{1,0:T(8,128)(2,1)S(1)}, bf16[528,512]{1,0:T(8,128)(2,1)}, u32[]{:S(2)}) copy-start(bf16[528,512]{1,0:T(8,128)(2,1)} %get-tuple-element.23.middle_ref) | copy-start | bytes 1622020
  209.5 48.3 %copy-start.1 = (bf16[512,512]{1,0:T(8,128)(2,1)S(1)}, bf16[512,512]{1,0:T(8,128)(2,1)}, u32[]{:S(2)}) copy-start(bf16[512,512]{1,0:T(8,128)(2,1)} %above_ref.3) | copy-start | bytes 1572868
  259.3 7.0 %collective-permute-start.1 = (bf16[144,512]{1,0:T(8,128)(2,1)S(1)}, bf16[144,512]{1,0:T(8,128)(2,1)S(1)}, u32[]{:S(2)}, u32[]{:S(2)}) collective-permute-start(bf16[144,512]{1,0:T(8,128)(2,1)S(1)} %slice.54), channel_id=1, source_target_pairs={{8,0},{16,8},{24,16},{9,1},{17,9},{25,17},{10,2},{18,10},{26,18},{... | collective-permute-start | bytes 442376 | tf_op jit(solution)/shard_map/ppermute | solution.py:501
  283.9 26.1 %all-to-all-start = ((bf16[4,4,128,512]{3,2,1,0:T(8,128)(2,1)}), bf16[4,4,128,512]{3,2,1,0:T(8,128)(2,1)S(1)}, u32[]{:S(2)}, u32[]{:S(2)}) async-start(bf16[4,4,128,512]{3,2,1,0:T(8,128)(2,1)} %shard_map.170), calls=%async_computation.1 | async-start | bytes 4194304 | tf_op jit(solution)/shard_map/all_to_all | solution.py:517
  287.6 68.4 %reduce-scatter.5.cloned.1.call-start = ((), (), s32[]{:S(2)}) async-start(), calls=%async_computation.5 | async-start | bytes 1179648 | tf_op jit(solution)/shard_map/reduce_scatter | solution.py:509
  322.5 117.3 %all-gather.21.cloned.1.call-start = ((), (), s32[]{:S(2)}) async-start(), calls=%async_computation.10 | async-start | bytes 7864320 | tf_op jit(solution)/shard_map/all_gather | solution.py:513
  323.0 149.4 %all-gather.19.cloned.1.call-start = ((), (), s32[]{:S(2)}) async-start(), calls=%async_computation.9 | async-start | bytes 1966080 | tf_op jit(solution)/shard_map/all_gather | solution.py:513
  328.1 5.0 copy-start.7
  328.1 65.8 %all-to-all-start.1 = ((bf16[4,2,512,512]{3,2,1,0:T(8,128)(2,1)}), bf16[4,2,512,512]{3,2,1,0:T(8,128)(2,1)}, u32[]{:S(2)}, u32[]{:S(2)}) async-start(bf16[4,2,512,512]{3,2,1,0:T(8,128)(2,1)} %bitcast.37), calls=%async_computation.3 | async-start | bytes 8388608 | tf_op jit(solution)/shard_map/all_to_all | solution.py:517
  333.1 168.4 %all-gather.17.cloned.1.call-start = ((), (), s32[]{:S(2)}) async-start(), calls=%async_computation.8 | async-start | bytes 1392640 | tf_op jit(solution)/shard_map/all_gather | solution.py:513
Sparse Core Ops, SparseCore 0:
  10.8 51.1 all-gather.12
  94.7 47.1 all-gather.14
  209.7 48.0 reduce-scatter.2
  322.6 33.3 reduce-scatter.4
  357.7 82.0 all-gather.20
  441.5 30.9 all-gather.18
  474.3 27.1 all-gather.16

commit v2 on v1

--- a/solution.py
+++ b/solution.py
@@ -97,60 +97,76 @@
     )(chunks, gains, weights)
 
 
-def back_kernel(g_ref, w_ref, o_ref):
+def back_kernel(order_ref, g_ref, w_ref, extra_ref, o_ref):
     total = None
     for j in range(3):
         term = lax.dot_general(
             g_ref[j], w_ref[j], (((1,), (1,)), ((), ())), preferred_element_type=f32
         )
         total = term if total is None else total + term
-    o_ref[0] = total.astype(bf16)
-
-
-def project_back(grads, weights, count):
+    rows = g_ref.shape[1]
+    o_ref[0, :rows, :] = total.astype(bf16)
+    if o_ref.shape[1] > rows:
+        o_ref[0, rows:, :] = extra_ref[...]
+
+
+def project_back(grads, weights, order, extra=None):
     _, rows, columns = grads.shape
     features = weights.shape[1]
+    count = order.shape[0]
     width = features // count
+    more = 0 if extra is None else extra.shape[0]
+    if extra is None:
+        extra = jnp.zeros((EDGE, width), bf16)
     return call(
         back_kernel,
         (count,),
-        [whole((3, rows, columns)), pl.BlockSpec((3, width, columns), lambda i: (0, i, 0))],
-        pl.BlockSpec((1, rows, width), lambda i: (i, 0, 0)),
-        jax.ShapeDtypeStruct((count, rows, width), bf16),
+        [
+            whole((3, rows, columns)),
+            pl.BlockSpec((3, width, columns), lambda i, order: (0, order[i], 0)),
+            whole(extra.shape),
+        ],
+        pl.BlockSpec((1, rows + more, width), lambda i, *_: (i, 0, 0)),
+        jax.ShapeDtypeStruct((count, rows + more, width), bf16),
         [],
         6 * rows * features * columns,
         6 * features * columns + 2 * rows * features,
-    )(grads, weights)
-
-
-def weight_grad_kernel(gain_ref, x_ref, g_ref, o_ref):
+        prefetch=1,
+    )(order, grads, weights, extra)
+
+
+def weight_grad_kernel(spans, order_ref, gain_ref, x_ref, *refs):
+    out_ref = refs[-1]
     for j in range(3):
         total = None
-        for shard in range(x_ref.shape[0]):
+        for (slot, first), g_ref in zip(spans, refs[:-1]):
+            some = x_ref[order_ref[slot], 0, first : first + g_ref.shape[1], :]
             term = lax.dot_general(
-                x_ref[shard, 0], g_ref[shard, j], (((0,), (0,)), ((), ())), preferred_element_type=f32
+                some, g_ref[j], (((0,), (0,)), ((), ())), preferred_element_type=f32
             )
             total = term if total is None else total + term
-        o_ref[j] = total * gain_ref[0]
-
-
-def weight_grad(columns, grads, gains):
+        out_ref[j] = total * gain_ref[0]
+
+
+def weight_grad(columns, grads, order, gains):
     shards, pieces, rows, width = columns.shape
-    out = grads.shape[3]
+    out = grads[0][2].shape[2]
+    arrays = [array for _, _, array in grads]
     return call(
-        weight_grad_kernel,
+        functools.partial(weight_grad_kernel, [(slot, first) for slot, first, _ in grads]),
         (pieces,),
         [
-            pl.BlockSpec((1, width, 1), lambda i: (i, 0, 0)),
-            pl.BlockSpec((shards, 1, rows, width), lambda i: (0, i, 0, 0)),
-            whole(grads.shape),
-        ],
-        pl.BlockSpec((3, width, out), lambda i: (0, i, 0)),
+            pl.BlockSpec((1, width, 1), lambda i, *_: (i, 0, 0)),
+            pl.BlockSpec((shards, 1, rows, width), lambda i, *_: (0, i, 0, 0)),
+        ]
+        + [whole(array.shape) for array in arrays],
+        pl.BlockSpec((3, width, out), lambda i, *_: (0, i, 0)),
         jax.ShapeDtypeStruct((3, pieces * width, out), f32),
         [],
         6 * shards * pieces * rows * width * out,
-        2 * columns.size + 2 * grads.size + 12 * pieces * width * out,
-    )(gains, columns, grads)
+        2 * columns.size + 6 * shards * rows * out + 12 * pieces * width * out,
+        prefetch=1,
+    )(order, gains, columns, *arrays)
 
 
 def fir(source, taps, target, base, rows, forward):
@@ -208,7 +224,8 @@
     later = window - front
     product = None
     for j in (1, 2, 0):
-        projected[...] = jnp.dot(onehot[...], p_ref[j], preferred_element_type=f32)
+        rows_j = p_ref[:, j].reshape(vocab, LANES)
+        projected[...] = jnp.dot(onehot[...], rows_j, preferred_element_type=f32)
         if j == 0:
             feature = short_sum(projected, short_ref, j, front - EDGE, later + EDGE, -1)
             feature_ref[0] = feature[EDGE:, :]
@@ -228,7 +245,7 @@
 
 def first_forward(tokens, table, embedding, short, medium, rows, front):
     window = tokens.shape[0]
-    _, vocab, columns = table.shape
+    vocab, columns = embedding.shape
     later = window - front
     shapes = [
         jax.ShapeDtypeStruct((rows + EDGE, columns), bf16),
@@ -255,7 +272,7 @@
 
 def first_backward_kernel(
     rows, token_ref, above_ref, feature_ref, filtered_ref, short_ref, medium_ref,
-    out_ref, onehot, signal, grad_gated, taps, held,
+    out_ref, other_ref, onehot, signal, grad_gated, taps, held,
 ):
     vocab = onehot.shape[0]
     parts = out_ref.shape[0]
@@ -285,19 +302,22 @@
     total = jnp.dot(onehot[...], above_ref[:rows, :], preferred_element_type=f32).astype(bf16)
     for part in range(parts):
         size = vocab // parts
-        out_ref[part, 3] = total[part * size : (part + 1) * size, :]
+        other_ref[part] = total[part * size : (part + 1) * size, :]
 
 
 def first_backward(tokens, above, features, filtered, short, medium, vocab, parts):
     rows = tokens.shape[1]
     later, columns = above.shape
-    shape = jax.ShapeDtypeStruct((parts, 4, vocab // parts, columns), bf16)
+    shapes = [
+        jax.ShapeDtypeStruct((parts, 3, vocab // parts, columns), bf16),
+        jax.ShapeDtypeStruct((parts, vocab // parts, columns), bf16),
+    ]
     return call(
         functools.partial(first_backward_kernel, rows),
         (columns // LANES,),
         [whole((1, rows))] + [lanes(a.shape) for a in (above, features, filtered, short, medium)],
-        lanes(shape.shape),
-        shape,
+        [lanes(s.shape) for s in shapes],
+        shapes,
         [
             pltpu.VMEM((vocab, rows), bf16),
             pltpu.VMEM((later, LANES), f32),
@@ -509,12 +529,86 @@
     return lax.psum_scatter(value, "ch", scatter_dimension=0, tiled=False)
 
 
-def gather_seq(value):
-    return lax.all_gather(value, "seq", axis=0, tiled=False)
-
-
 def exchange_seq(value):
     return lax.all_to_all(value, "seq", split_axis=0, concat_axis=0, tiled=True)
+
+
+def gather_seq(value):
+    return exchange_seq(jnp.broadcast_to(value[None], (lax.axis_size("seq"),) + value.shape))
+
+
+def seq_ring():
+    devices = lax.axis_size("seq")
+    if devices % 2:
+        return list(range(devices))
+    return list(range(0, devices, 2)) + list(range(devices - 1, 0, -2))
+
+
+def seq_hop(value, by):
+    ring = seq_ring()
+    pairs = [(ring[i], ring[(i + by) % len(ring)]) for i in range(len(ring))]
+    return lax.ppermute(value, "seq", pairs)
+
+
+def ring_order():
+    ring = seq_ring()
+    twice = jnp.array(ring + ring, jnp.int32)
+    place = jnp.argmax(twice[: len(ring)] == lax.axis_index("seq")).astype(jnp.int32)
+    return lax.dynamic_slice_in_dim(twice, place, len(ring), 0)
+
+
+def ch_hop(value, by):
+    devices = lax.axis_size("ch")
+    pairs = [(i, (i + 2 * by) % devices) for i in range(devices)]
+    return lax.ppermute(value, "ch", pairs)
+
+
+def sibling(value):
+    return lax.ppermute(value, "ch", [(i, i ^ 1) for i in range(lax.axis_size("ch"))])
+
+
+def scatter_order():
+    devices = lax.axis_size("ch")
+    me = lax.axis_index("ch")
+    places = jnp.arange(devices // 2, dtype=jnp.int32)
+    return jnp.concatenate([(2 * places + other) % devices for other in (me, me ^ 1)])
+
+
+def added(*terms):
+    return functools.reduce(lambda a, b: a + b, [t.astype(f32) for t in terms])
+
+
+def ring_scatter(pieces):
+    half = pieces.shape[0] // 2
+    mine = added(pieces[:half], sibling(pieces[half:])).astype(bf16)
+    if half == 1:
+        return mine[0].astype(f32)
+    steps = (half - 1) // 2
+    rows = mine.shape[1]
+    middle = rows // 32 * 16
+    up = down = None
+    if half % 2 == 0:
+        far = mine[half // 2]
+        up, down = ch_hop(far[:middle], 1), ch_hop(far[middle:], -1)
+        if half == 2:
+            return added(mine[0], jnp.concatenate([up, down], axis=0))
+    for step in range(steps, 0, -1):
+        first, second = mine[step], mine[half - step]
+        if up is not None and step == steps and half % 2 == 0:
+            first = jnp.concatenate(
+                [added(first[:middle], up).astype(bf16), first[middle:]], axis=0
+            )
+            second = jnp.concatenate(
+                [second[:middle], added(second[middle:], down).astype(bf16)], axis=0
+            )
+        elif up is not None:
+            first, second = added(first, up).astype(bf16), added(second, down).astype(bf16)
+        up, down = ch_hop(first, 1), ch_hop(second, -1)
+    return added(mine[0], up, down)
+
+
+def tie(*values):
+    return lax.optimization_barrier(values)
 
 
 def per_device(
@@ -543,15 +637,23 @@
     w_first, w_second = (jnp.transpose(w, (1, 0, 2)) for w in (weights_first, weights_second))
     s_first, s_second = (jnp.transpose(s, (1, 0, 2)) for s in (short_first, short_second))
 
+    order = ring_order()
+    each = pieces // shards
+    share = vocab // shards
+    at = seq * share
+
     gains = jnp.concatenate(
         [gain_first[None], gain_second[None], jnp.zeros((EDGE - 2, width), bf16)], axis=0
     )
-    gathered = gather_ch(jnp.concatenate([embedding, gains], axis=0))
-    gains_first = gathered[:, vocab : vocab + 1, :].astype(f32)
-    gains_second = gathered[:, vocab + 1 : vocab + 2, :].astype(f32)
-    table, scale_table = project(gathered, gains_first, w_first, vocab)
-
+    own_embedding = lax.dynamic_slice_in_dim(embedding, at, share, 0)
+    gathered = gather_ch(jnp.concatenate([own_embedding, gains], axis=0))
     tokens = lax.all_gather(token_ids, "seq", axis=0, tiled=True)
+    tokens, gathered = tie(tokens, gathered)
+    gains_first = gathered[:, share : share + 1, :].astype(f32)
+    gains_second = gathered[:, share + 1 : share + 2, :].astype(f32)
+    own_table, own_scale = project(gathered, gains_first, w_first, share)
+    table = gather_seq(own_table)
+
     tokens = jnp.pad(tokens, (front, back), constant_values=-1)
     tokens = lax.dynamic_slice_in_dim(tokens, seq * rows, front + rows + back, 0)
     middle, features_first, filtered_first = first_forward(
@@ -559,11 +661,22 @@
     )
 
     middles = gather_ch(middle)
+    block = exchange_seq(gathered[:, :share, :].reshape(shards, each, share, width))
+    block, middles = tie(block, middles)
+    core = lax.axis_index("ch") % each
+    own = middles[:, EDGE:, :].reshape(shards, each, rows, width)
+    own = lax.dynamic_index_in_dim(own, core, 1, keepdims=False)
+    columns = exchange_seq(own)
     projected, scale = project(middles, gains_second, w_second, rows + EDGE)
     features_second, gated, signal, segments, closing = second_features(
         projected, s_second, cotangent, decay_rates
     )
+    columns, closing = tie(columns, closing)
     closings = gather_seq(closing)
+    other = sibling(columns)
+    columns = jnp.where(
+        core == 0, jnp.stack([columns, other], axis=1), jnp.stack([other, columns], axis=1)
+    )
     output, grad_featured = second_filter(
         seq[None], features_second, gated, signal, segments, closings,
         decay_rates, residues, cotangent, middle,
@@ -571,8 +684,17 @@
     halo = shift(grad_featured[:, :EDGE, :], "seq", -1)
     scale = scale[EDGE:]
     grads, terms = second_grads(grad_featured, halo, projected, s_second, scale)
+    pieces_of = [(0, 0, grads)]
+    up = down = grads
+    for step in range(1, (shards + 1) // 2):
+        up, down = seq_hop(up, 1), seq_hop(down, -1)
+        pieces_of += [(shards - step, 0, up), (step, 0, down)]
+    partial = project_back(grads, w_second, jnp.arange(pieces, dtype=jnp.int32))
+    partial_sum = scatter_ch(partial)
     terms = lax.psum(terms[:, 0], "ch")
-    grad_normed = scatter_ch(project_back(grads, w_second, pieces)).astype(f32)
+    partial_sum, *arrays = tie(partial_sum, *[array for _, _, array in pieces_of[1:]])
+    pieces_of[1:] = [old[:2] + (new,) for old, new in zip(pieces_of[1:], arrays)]
+    grad_normed = partial_sum.astype(f32)
     as_float = middle[EDGE:].astype(f32)
     grad_middle = (
         cotangent.astype(f32)
@@ -581,48 +703,57 @@
     ).astype(bf16)
     grad_gain_second = jnp.sum(grad_normed * as_float, axis=0)
 
-    each = pieces // shards
-    own = middles[:, EDGE:, :].reshape(shards, each, rows, width)
-    columns = exchange_seq(own)
+    above = jnp.concatenate([grad_middle, shift(grad_middle[:back], "seq", -1)], axis=0)
+    if shards % 2 == 0:
+        half = rows // 2
+        if shards > 2:
+            up, down = pieces_of[-2][2], pieces_of[-1][2]
+        above, up, down = tie(above, up, down)
+        up, down = seq_hop(up[:, :half], 1), seq_hop(down[:, half:], -1)
+        pieces_of += [(shards // 2, 0, up), (shards // 2, half, down)]
+    sums, others = first_backward(
+        token_ids[None], above, features_first, filtered_first, s_first, medium, vocab, shards
+    )
+    sums = exchange_seq(sums)
     block_gains = lax.dynamic_slice_in_dim(gains_second, seq * each, each, 0)
-    grad_weights_second = weight_grad(
-        columns, gather_seq(grads), jnp.swapaxes(block_gains, 1, 2)
-    )
-
-    above = jnp.concatenate([grad_middle, shift(grad_middle[:back], "seq", -1)], axis=0)
-    sums = first_backward(
-        token_ids[None], above, features_first, filtered_first, s_first, medium, vocab, shards
-    )
-    own_sums = jnp.sum(exchange_seq(sums).astype(f32), axis=0)
-    share = vocab // shards
-    at = seq * share
-    own_scale = lax.dynamic_slice_in_dim(scale_table, at, share, 0)
-    own_table = lax.dynamic_slice_in_dim(table, at, share, 1).astype(f32)
-    own_embedding = lax.dynamic_slice_in_dim(embedding, at, share, 0).astype(f32)
-    own_grads = own_sums[:3]
-    terms = lax.psum(jnp.sum(own_grads * own_table, axis=(0, 2)), "ch")
-    own_grads = (own_grads * own_scale[None]).astype(bf16)
-    grad_normed = scatter_ch(project_back(own_grads, w_first, pieces)).astype(f32)
+    grad_weights_second = weight_grad(columns, pieces_of, order, jnp.swapaxes(block_gains, 1, 2))
+    sums, grad_weights_second = tie(sums, grad_weights_second)
+    own_sums = jnp.sum(sums.astype(f32), axis=0)
+    terms = jnp.sum(own_sums * own_table.astype(f32), axis=(0, 2))
+    own_grads = (own_sums * own_scale[None]).astype(bf16)
+    extra_rows = -(-share // width)
+    extra = jnp.pad(terms, (0, EDGE * width - share)).reshape(EDGE, width).astype(bf16)
+    partial = project_back(own_grads, w_first, scatter_order(), extra)
+    grad_normed = ring_scatter(partial)
+    terms = grad_normed[share : share + extra_rows].reshape(-1)[:share]
+    grad_normed = grad_normed[:share]
+    own_others = jnp.sum(exchange_seq(others).astype(f32), axis=0)
+    all_grads = gather_seq(own_grads)
+    block_gains = lax.dynamic_slice_in_dim(gains_first, seq * each, each, 0)
+    grad_weights_first = weight_grad(
+        block,
+        [(shard, 0, all_grads[shard]) for shard in range(shards)],
+        jnp.arange(shards, dtype=jnp.int32),
+        jnp.swapaxes(block_gains, 1, 2),
+    )
+
+    as_float = own_embedding.astype(f32)
     grad_embedding = (
-        own_sums[3]
+        own_others
         + gain_first.astype(f32) * grad_normed
-        - own_embedding * (own_scale * own_scale) * terms[:, None] / features
-    )
-    grad_gain_first = jnp.sum(grad_normed * own_embedding, axis=0)
+        - as_float * (own_scale * own_scale) * terms[:, None] / features
+    )
+    grad_gain_first = jnp.sum(grad_normed * as_float, axis=0)
     last = jnp.concatenate(
         [
             grad_embedding,
             grad_gain_first[None],
             grad_gain_second[None],
-            jnp.zeros((6, width), f32),
+            jnp.zeros((EDGE - 2, width), f32),
         ],
         axis=0,
-    )
-    last = gather_seq(last)
-    block = lax.dynamic_slice_in_dim(gathered, seq * each, each, 0)[:, :vocab, :]
-    block_gains = lax.dynamic_slice_in_dim(gains_first, seq * each, each, 0)
-    all_grads = jnp.swapaxes(gather_seq(own_grads), 0, 1).reshape(1, 3, vocab, width)
-    grad_weights_first = weight_grad(block[None], all_grads, jnp.swapaxes(block_gains, 1, 2))
+    ).astype(bf16)
+    last = gather_seq(last).astype(f32)
     return (
         output,
         last[:, :share].reshape(vocab, width),

time: 514 us -> 404 us (0.79)
  waiting for transfers between devices: 277 us -> 141 us
  starting transfers between devices: 11.6 us -> 40.9 us
  blocking collectives: 50.8 us -> 33.6 us
  local copies, waits for them, and re-layouts: 20.1 us -> 29.5 us
    all_gather x3 -> x0, waiting for transfers between devices: 87.4 us -> none  [gather_seq(): return lax.all_gather(value, 'seq', axis=0, tiled=False)]
    all_gather x2, waiting for transfers between devices: 88 us -> 45.4 us  [gather_ch(): return lax.all_gather(value, 'ch', axis=0, tiled=False)]
    reduce_scatter x2 -> x1, waiting for transfers between devices: 39 us -> 13.1 us  [scatter_ch(): return lax.psum_scatter(value, 'ch', scatter_dimension=0, tiled=False)]
    ppermute x0 -> x10, waiting for transfers between devices: none -> 23.2 us  [the longest x4 17.8 us: seq_hop(): return lax.ppermute(value, 'seq', pairs)]
    all_to_all x2 -> x7, starting transfers between devices: 8.61 us -> 26.8 us  [exchange_seq(): return lax.all_to_all(value, 'seq', split_axis=0, concat_axis=0, tiled=True)]
    psum x1 -> x0, blocking collectives: 16.9 us -> none  [per_device(): terms = lax.psum(jnp.sum(own_grads * own_table, axis=(0, 2)), 'ch')]
    ppermute x0 -> x10, starting transfers between devices: none -> 11.5 us  [the longest x4 7.01 us: ch_hop(): return lax.ppermute(value, 'ch', pairs)]
    all_gather x1 -> x0, blocking collectives: 10.5 us -> none  [gather_seq(): return lax.all_gather(value, 'seq', axis=0, tiled=False)]
  transfers between devices with their start and end apart: 11 -> 22, of which waited for: 11 -> 14; matrix products, arithmetic and copies ran while one was open for 3% -> 6% of each run, Pallas kernels for 3% -> 14%
where the time goes in v2:
time: 404 us; the launch traced here: 403 us
  waiting for transfers between devices  141 us (35%)
  Pallas kernels  125 us (31%)
  starting transfers between devices  40.9 us (10%)
  blocking collectives  33.6 us (8%)
  local copies, waits for them, and re-layouts  29.5 us (7%)
  other arithmetic  16.4 us (4%)
  between operations  16.2 us (4%)
    all_to_all x7, waiting for transfers between devices, exchange_seq(): return lax.all_to_all(value, 'seq', split_axis=0, concat_axis=0, tiled=True)  50 us
    all_gather x2, waiting for transfers between devices, gather_ch(): return lax.all_gather(value, 'ch', axis=0, tiled=False)  45.4 us
    all_to_all x7, starting transfers between devices, exchange_seq(): return lax.all_to_all(value, 'seq', split_axis=0, concat_axis=0, tiled=True)  26.8 us
    pallas_call x2, Pallas kernels, project_back(): call(back_kernel, (count,), [whole((3, rows, columns)), pl.BlockSpec((3,...  24.5 us
    pallas_call x2, Pallas kernels, weight_grad(): call(functools.partial(weight_grad_kernel, [(slot, first) for slot, first...  20.4 us
    pallas_call x1, Pallas kernels, first_forward(): call(functools.partial(first_forward_kernel, front, rows), (columns // LA...  19.4 us
    pallas_call x2, Pallas kernels, project(): call(functools.partial(project_kernel, per_step, features), (count // per...  19.3 us
    ppermute x4, waiting for transfers between devices, seq_hop(): return lax.ppermute(value, 'seq', pairs)  17.8 us
  transfers between devices with their start and end apart: 22, of which 14 were waited for; matrix products, arithmetic and copies ran while one was open for 6% of the time, Pallas kernels for 14%

profile of v2, /device:TPU:0, one launch (start us, length us, event | category | flops | bytes accessed | tf_op | source)
XLA Modules:
  0.0 402.5 jit_solution(2172705404286841875)
XLA Ops:
  10.4 9.6 %all-gather.2 = s32[4,1,512]{2,1,0:T(1,128)S(1)} all-gather(s32[1,1,512]{2,1,0:T(1,128)} %bitcast.72), channel_id=1, replica_groups=mesh['seq'=4,'ch'=8] {'seq'}, dimensions={0}, use_global_device_ids=true | all-gather | bytes 10240 | tf_op jit(solution)/shard_map/all_gather | solution.py:650
  20.0 15.9 %all-gather.6.cloned.1.call-done = bf16[1152,512]{1,0:T(8,128)(2,1)} async-done(((bf16[144,512]{1,0:T(8,128)(2,1)}), bf16[1152,512]{1,0:T(8,128)(2,1)}) %all-gather.6.cloned.1.call-update) | async-done | bytes 1179664 | tf_op jit(solution)/shard_map/all_gather | solution.py:525
  37.4 7.3 %shard_map.172 = (bf16[3,128,512]{2,1,0:T(8,128)(2,1)}, f32[128,1]{1,0:T(8,128)}) custom-call(bf16[8,144,512]{2,1,0:T(8,128)(2,1)} %bitcast.61, f32[8,1,512]{2,1,0:T(1,128)} %get-tuple-element.81.gain_ref, bf16[3,4096,512]{2,1,0:T(8,128)(2,1)} %bitcast.55), custom_call_target="tpu_custom_call" | custom-call | flops 1610612736 | bytes 13631488 | tf_op jit(solution)/shard_map/pallas_call | solution.py:81
  51.7 18.8 %all-to-all-done.1.p_ref = bf16[4,3,128,512]{3,2,1,0:T(8,128)(2,1)S(1)} async-done(((bf16[4,3,128,512]{3,2,1,0:T(8,128)(2,1)}), bf16[4,3,128,512]{3,2,1,0:T(8,128)(2,1)S(1)}, u32[]{:S(2)}, u32[]{:S(2)}) %all-to-all-start.1) | async-done | bytes 1572896 | tf_op jit(solution)/shard_map/all_to_all | solution.py:533
  71.6 19.4 %shard_map.173 = (bf16[528,512]{1,0:T(8,128)(2,1)}, f32[3,656,512]{2,1,0:T(8,128)}, f32[528,512]{1,0:T(8,128)}) custom-call(s32[816,1]{1,0:T(8,128)} %broadcast_in_dim.64.token_ref, bf16[4,3,128,512]{3,2,1,0:T(8,128)(2,1)} %copy-done.6, bf16[512,512]{1,0:T(8,128)(2,1)} %e_ref.1, f32[3,7,512]{2,1,0:T(8,128)} %bitcast.69, bf16[128,512]{1,0:T(8,128)(2,1)} %medium_ref.3), custom_call_target="tpu_custom_call" | custom-call | flops 1711276032 | bytes 6684672 | tf_op jit(solution)/shard_map/pallas_call | solution.py:255
  95.6 13.3 %all-to-all-done.x_ref = bf16[4,2,128,512]{3,2,1,0:T(8,128)(2,1)S(1)} async-done(((bf16[4,2,128,512]{3,2,1,0:T(8,128)(2,1)}), bf16[4,2,128,512]{3,2,1,0:T(8,128)(2,1)S(1)}, u32[]{:S(2)}, u32[]{:S(2)}) %all-to-all-start) | async-done | bytes 1048608 | tf_op jit(solution)/shard_map/all_to_all | solution.py:533
  109.0 29.6 %all-gather.8.cloned.1.call-done = bf16[4224,512]{1,0:T(8,128)(2,1)} async-done(((bf16[528,512]{1,0:T(8,128)(2,1)}), bf16[4224,512]{1,0:T(8,128)(2,1)}) %all-gather.8.cloned.1.call-update) | async-done | bytes 4325392 | tf_op jit(solution)/shard_map/all_gather | solution.py:525
  146.3 12.0 %shard_map.174 = (bf16[3,528,512]{2,1,0:T(8,128)(2,1)}, f32[528,1]{1,0:T(8,128)}) custom-call(bf16[8,528,512]{2,1,0:T(8,128)(2,1)} %bitcast.64, f32[8,1,512]{2,1,0:T(1,128)} %get-tuple-element.80.gain_ref, bf16[3,4096,512]{2,1,0:T(8,128)(2,1)} %bitcast.74), custom_call_target="tpu_custom_call" | custom-call | flops 6643777536 | bytes 16908288 | tf_op jit(solution)/shard_map/pallas_call | solution.py:81
  158.3 9.1 %shard_map.175 = (f32[3,512,512]{2,1,0:T(8,128)}, bf16[512,512]{1,0:T(8,128)(2,1)}, bf16[512,512]{1,0:T(8,128)(2,1)}, f32[2,128,512]{2,1,0:T(8,128)}, f32[2,16,512]{2,1,0:T(8,128)}) custom-call(bf16[3,528,512]{2,1,0:T(8,128)(2,1)} %get-tuple-element.44.p_ref, f32[3,7,512]{2,1,0:T(8,128)} %bitcast.67, bf16[512,512]{1,0:T(8,128)(2,1)} %above_ref.3, ...), custom_call_target="tpu_custom_call" | custom-call | flops 26214400 | bytes 6291456 | tf_op jit(solution)/shard_map/pallas_call | solution.py:403
  172.7 8.8 %all_to_all.40.closing_ref = f32[4,2,16,512]{3,2,1,0:T(8,128)} all-to-all(f32[4,2,16,512]{3,2,1,0:T(8,128)S(1)} %broadcast_in_dim.28), channel_id=1, replica_groups=mesh['seq'=4,'ch'=8] {'seq'}, dimensions={0} | all-to-all | bytes 524288 | tf_op jit(solution)/shard_map/all_to_all | solution.py:533
  181.4 9.7 %shard_map.176 = (bf16[512,512]{1,0:T(8,128)(2,1)}, bf16[3,512,512]{2,1,0:T(8,128)(2,1)}) custom-call(s32[1]{0:T(128)} %bitcast.seq_ref, f32[3,512,512]{2,1,0:T(8,128)} %get-tuple-element.45.feature_ref, bf16[512,512]{1,0:T(8,128)(2,1)} %get-tuple-element.46.gated_ref, bf16[512,512]{1,0:T(8,128)(2,1)} %get-tuple-element.47.signal_ref, ...), custom_call_target="tpu_custom_call" | custom-call | flops 36700160 | bytes 7340032 | tf_op jit(solution)/shard_map/pallas_call | solution.py:463
  198.5 6.0 %shard_map.177 = (bf16[3,512,512]{2,1,0:T(8,128)(2,1)}, f32[512,1]{1,0:T(8,128)}) custom-call(bf16[3,512,512]{2,1,0:T(8,128)(2,1)} %get-tuple-element.52.grad_ref, bf16[3,16,512]{2,1,0:T(8,128)(2,1)} %copy-done.11, bf16[3,528,512]{2,1,0:T(8,128)(2,1)} %get-tuple-element.44.p_ref, f32[3,7,512]{2,1,0:T(8,128)} %bitcast.68, f32[512,1]{1,0:T(8,128)} %get-tuple-element.93.scale_ref), custom_call_target="tpu_custom_call" | custom-call | flops 15728640 | bytes 6291456 | tf_op jit(solution)/shard_map/pallas_call | solution.py:506
  205.6 13.6 %shard_map.178 = bf16[8,512,512]{2,1,0:T(8,128)(2,1)} custom-call(s32[8]{0:T(128)} %iota.15.order_ref, bf16[3,512,512]{2,1,0:T(8,128)(2,1)} %get-tuple-element.54.g_ref.refs_0_, bf16[3,4096,512]{2,1,0:T(8,128)(2,1)} %bitcast.75, bf16[16,512]{1,0:T(8,128)(2,1)} %broadcast_in_dim.30.extra_ref), custom_call_target="tpu_custom_call" | custom-call | flops 6442450944 | bytes 16777216 | tf_op jit(solution)/shard_map/pallas_call | solution.py:121
  221.6 15.2 %psum.7 = f32[512]{0:T(512)S(1)} all-reduce(f32[512]{0:T(512)S(1)} %reduce.21), channel_id=1, replica_groups=mesh['seq'=4,'ch'=8] {'ch'}, use_global_device_ids=true, to_apply=%region_1.2 | all-reduce | flops 512 | bytes 4096 | tf_op jit(solution)/shard_map/psum | solution.py:694
  236.8 16.3 %collective-permute-done.2.refs_2_ = bf16[3,512,512]{2,1,0:T(8,128)(2,1)} collective-permute-done((bf16[3,512,512]{2,1,0:T(8,128)(2,1)}, bf16[3,512,512]{2,1,0:T(8,128)(2,1)}, u32[]{:S(2)}, u32[]{:S(2)}) %collective-permute-start.2) | collective-permute-done | bytes 1572896 | tf_op jit(solution)/shard_map/ppermute | solution.py:550
  254.6 13.1 %reduce-scatter.2.cloned.1.call-done = bf16[1,512,512]{2,1,0:T(8,128)(2,1)} async-done(((bf16[8,512,512]{2,1,0:T(8,128)(2,1)}), bf16[1,512,512]{2,1,0:T(8,128)(2,1)}) %reduce-scatter.2.cloned.1.call-update) | async-done | bytes 524304 | tf_op jit(solution)/shard_map/reduce_scatter | solution.py:529
  271.2 5.0 %collective-permute-done.3 = bf16[144,512]{1,0:T(8,128)(2,1)S(1)} collective-permute-done((bf16[144,512]{1,0:T(8,128)(2,1)S(1)}, bf16[144,512]{1,0:T(8,128)(2,1)S(1)}, u32[]{:S(2)}, u32[]{:S(2)}) %collective-permute-start.3) | collective-permute-done | bytes 147488 | tf_op jit(solution)/shard_map/ppermute | solution.py:521
  282.8 16.9 %shard_map.179 = (bf16[4,3,128,512]{3,2,1,0:T(8,128)(2,1)}, bf16[4,128,512]{2,1,0:T(8,128)(2,1)}) custom-call(s32[1,512]{1,0:T(1,128)} %bitcast.73, bf16[656,512]{1,0:T(8,128)(2,1)} %pad_maximum_fusion.above_ref, f32[3,656,512]{2,1,0:T(8,128)} %get-tuple-element.60.feature_ref, f32[528,512]{1,0:T(8,128)} %get-tuple-element.61.filtered_ref, ...), custom_call_target="tpu_custom_call" | custom-call | flops 1073741824 | bytes 5373952 | tf_op jit(solution)/shard_map/pallas_call | solution.py:315
  299.6 4.7 %all-to-all-start.5 = ((bf16[4,3,128,512]{3,2,1,0:T(8,128)(2,1)}), bf16[4,3,128,512]{3,2,1,0:T(8,128)(2,1)}, u32[]{:S(2)}, u32[]{:S(2)}) async-start(bf16[4,3,128,512]{3,2,1,0:T(8,128)(2,1)} %get-tuple-element.63), calls=%async_computation.6 | async-start | bytes 3145728 | tf_op jit(solution)/shard_map/all_to_all | solution.py:533
  309.4 4.5 %maximum_select_fusion.x_ref = bf16[4,2,512,512]{3,2,1,0:T(8,128)(2,1)} fusion(bf16[4,1,512,512]{3,2,1,0:T(8,128)(2,1)} %bitcast.15, bf16[4,1,512,512]{3,2,1,0:T(8,128)(2,1)S(1)} %bitcast.58, pred[]{:T(512)S(6)} %eq.18), kind=kLoop, calls=%fused_computation | loop fusion | flops 6291456 | bytes 8388609 | tf_op jit(solution)/shard_map/jit(_where)/select_n | solution.py:677
  313.9 12.8 %shard_map.180 = f32[3,1024,512]{2,1,0:T(8,128)} custom-call(s32[4]{0:T(128)} %dynamic_slice.22.order_ref, f32[2,512,1]{2,1,0:T(8,128)} %transpose.45.gain_ref, bf16[4,2,512,512]{3,2,1,0:T(8,128)(2,1)} %maximum_select_fusion.x_ref, bf16[3,512,512]{2,1,0:T(8,128)(2,1)} %get-tuple-element.54.g_ref.refs_0_, ...), custom_call_target="tpu_custom_call" | custom-call | flops 6442450944 | bytes 16777216 | tf_op jit(solution)/shard_map/pallas_call | solution.py:155
  330.0 10.9 %shard_map.181 = bf16[8,144,512]{2,1,0:T(8,128)(2,1)} custom-call(s32[8]{0:T(128)} %pad_add_fusion.order_ref, bf16[3,128,512]{2,1,0:T(8,128)(2,1)} %get-tuple-element.85.g_ref, bf16[3,4096,512]{2,1,0:T(8,128)(2,1)} %bitcast.56, bf16[16,512]{1,0:T(8,128)(2,1)} %convert_element_type.109.extra_ref), custom_call_target="tpu_custom_call" | custom-call | flops 1610612736 | bytes 13631488 | tf_op jit(solution)/shard_map/pallas_call | solution.py:121
  366.8 12.0 %all-to-all-done.7 = bf16[4,3,128,512]{3,2,1,0:T(8,128)(2,1)S(1)} async-done(((bf16[4,3,128,512]{3,2,1,0:T(8,128)(2,1)}), bf16[4,3,128,512]{3,2,1,0:T(8,128)(2,1)S(1)}, u32[]{:S(2)}, u32[]{:S(2)}) %all-to-all-start.7) | async-done | bytes 1572896 | tf_op jit(solution)/shard_map/all_to_all | solution.py:533
  386.5 7.6 %shard_map.182 = f32[3,1024,512]{2,1,0:T(8,128)} custom-call(s32[4]{0:T(128)} %iota.18.order_ref, f32[2,512,1]{2,1,0:T(8,128)} %transpose.46.gain_ref, bf16[4,2,128,512]{3,2,1,0:T(8,128)(2,1)} %copy-done.4, bf16[3,128,512]{2,1,0:T(8,128)(2,1)} %get-tuple-element.79.refs_0_, bf16[3,128,512]{2,1,0:T(8,128)(2,1)} %get-tuple-element.78.refs_1_, ...), custom_call_target="tpu_custom_call" | custom-call | flops 1610612736 | bytes 8912896 | tf_op jit(solution)/shard_map/pallas_call | solution.py:155
  (131 shorter events, 94.4 us)
Async XLA Ops:
  7.2 28.7 %all-gather.6.cloned.1.call-start = ((), (), s32[]{:S(2)}) async-start(), calls=%async_computation.10 | async-start | bytes 1327104 | tf_op jit(solution)/shard_map/all_gather | solution.py:525
  47.0 23.5 %all-to-all-start.1 = ((bf16[4,3,128,512]{3,2,1,0:T(8,128)(2,1)}), bf16[4,3,128,512]{3,2,1,0:T(8,128)(2,1)S(1)}, u32[]{:S(2)}, u32[]{:S(2)}) async-start(bf16[4,3,128,512]{3,2,1,0:T(8,128)(2,1)} %broadcast_in_dim.27), calls=%async_computation.1 | async-start | bytes 3145728 | tf_op jit(solution)/shard_map/all_to_all | solution.py:533
  50.7 87.8 %all-gather.8.cloned.1.call-start = ((), (), s32[]{:S(2)}) async-start(), calls=%async_computation.11 | async-start | bytes 4866048 | tf_op jit(solution)/shard_map/all_gather | solution.py:525
  92.1 16.9 %all-to-all-start = ((bf16[4,2,128,512]{3,2,1,0:T(8,128)(2,1)}), bf16[4,2,128,512]{3,2,1,0:T(8,128)(2,1)S(1)}, u32[]{:S(2)}, u32[]{:S(2)}) async-start(bf16[4,2,128,512]{3,2,1,0:T(8,128)(2,1)} %bitcast.4), calls=%async_computation | async-start | bytes 2097152 | tf_op jit(solution)/shard_map/all_to_all | solution.py:533
  142.7 29.1 %all-to-all-start.2 = ((bf16[4,512,512]{2,1,0:T(8,128)(2,1)}), bf16[4,512,512]{2,1,0:T(8,128)(2,1)S(1)}, u32[]{:S(2)}, u32[]{:S(2)}) async-start(bf16[4,512,512]{2,1,0:T(8,128)(2,1)} %dynamic-slice_bitcast_fusion), calls=%async_computation.2 | async-start | bytes 4194304 | tf_op jit(solution)/shard_map/all_to_all | solution.py:533
  146.3 121.4 %reduce-scatter.2.cloned.1.call-start = ((), (), s32[]{:S(2)}) async-start(), calls=%async_computation.9 | async-start | bytes 4718592 | tf_op jit(solution)/shard_map/reduce_scatter | solution.py:529
  191.9 6.0 %collective-permute-start = (bf16[3,16,512]{2,1,0:T(8,128)(2,1)S(1)}, bf16[3,16,512]{2,1,0:T(8,128)(2,1)S(1)}, u32[]{:S(2)}, u32[]{:S(2)}) collective-permute-start(bf16[3,16,512]{2,1,0:T(8,128)(2,1)S(1)} %slice.117), channel_id=1, source_target_pairs={{8,0},{16,8},{24,16},{9,1},{17,9},{25,17},{10,2},{18,10},{26,18},{... | collective-permute-start | bytes 147464 | tf_op jit(solution)/shard_map/ppermute | solution.py:521
  219.3 48.4 %copy-start = (bf16[528,512]{1,0:T(8,128)(2,1)S(1)}, bf16[528,512]{1,0:T(8,128)(2,1)}, u32[]{:S(2)}) copy-start(bf16[528,512]{1,0:T(8,128)(2,1)} %get-tuple-element.42.middle_ref) | copy-start | bytes 1622020
  219.3 51.2 %copy-start.14 = (s32[4]{0:T(128)S(1)}, s32[4]{0:T(128)}, u32[]{:S(2)}) copy-start(s32[4]{0:T(128)} %constant.80) | copy-start | bytes 52
  219.3 33.7 %collective-permute-start.2 = (bf16[3,512,512]{2,1,0:T(8,128)(2,1)}, bf16[3,512,512]{2,1,0:T(8,128)(2,1)}, u32[]{:S(2)}, u32[]{:S(2)}) collective-permute-start(bf16[3,512,512]{2,1,0:T(8,128)(2,1)} %get-tuple-element.54.g_ref.refs_0_), channel_id=1, source_target_pairs={{0,8},{16,0},{24,16},{8,24},{1,9},{17,1},{25,17},{9,25},{2,10},{18... | collective-permute-start | bytes 4718600 | tf_op jit(solution)/shard_map/ppermute | solution.py:550
  221.2 33.4 %collective-permute-start.1 = (bf16[3,512,512]{2,1,0:T(8,128)(2,1)}, bf16[3,512,512]{2,1,0:T(8,128)(2,1)}, u32[]{:S(2)}, u32[]{:S(2)}) collective-permute-start(bf16[3,512,512]{2,1,0:T(8,128)(2,1)} %get-tuple-element.54.g_ref.refs_0_), channel_id=1, source_target_pairs={{0,16},{16,24},{24,8},{8,0},{1,17},{17,25},{25,9},{9,1},{2,18},{18... | collective-permute-start | bytes 4718600 | tf_op jit(solution)/shard_map/ppermute | solution.py:550
  221.4 88.0 %collective-permute-start.4 = (bf16[4,512,512]{2,1,0:T(8,128)(2,1)S(1)}, bf16[4,512,512]{2,1,0:T(8,128)(2,1)}, u32[]{:S(2)}, u32[]{:S(2)}) collective-permute-start(bf16[4,512,512]{2,1,0:T(8,128)(2,1)S(1)} %all-to-all-done.2), channel_id=1, source_target_pairs={{0,1},{1,0},{2,3},{3,2},{4,5},{5,4},{6,7},{7,6},{8,9},{9,8},{10,11... | collective-permute-start | bytes 6291464 | tf_op jit(solution)/shard_map/ppermute | solution.py:567
  269.2 7.0 %collective-permute-start.3 = (bf16[144,512]{1,0:T(8,128)(2,1)S(1)}, bf16[144,512]{1,0:T(8,128)(2,1)S(1)}, u32[]{:S(2)}, u32[]{:S(2)}) collective-permute-start(bf16[144,512]{1,0:T(8,128)(2,1)S(1)} %slice.146), channel_id=1, source_target_pairs={{8,0},{16,8},{24,16},{9,1},{17,9},{25,17},{10,2},{18,10},{26,18},{... | collective-permute-start | bytes 442376 | tf_op jit(solution)/shard_map/ppermute | solution.py:521
  280.4 33.5 %collective-permute-start.6 = (bf16[3,256,512]{2,1,0:T(8,128)(2,1)}, bf16[3,256,512]{2,1,0:T(8,128)(2,1)}, u32[]{:S(2)}, u32[]{:S(2)}) collective-permute-start(bf16[3,256,512]{2,1,0:T(8,128)(2,1)} %slice.123), channel_id=1, source_target_pairs={{0,8},{16,0},{24,16},{8,24},{1,9},{17,1},{25,17},{9,25},{2,10},{18... | collective-permute-start | bytes 2359304 | tf_op jit(solution)/shard_map/ppermute | solution.py:550
  282.8 31.1 %collective-permute-start.5 = (bf16[3,256,512]{2,1,0:T(8,128)(2,1)S(1)}, bf16[3,256,512]{2,1,0:T(8,128)(2,1)}, u32[]{:S(2)}, u32[]{:S(2)}) collective-permute-start(bf16[3,256,512]{2,1,0:T(8,128)(2,1)S(1)} %slice.122), channel_id=1, source_target_pairs={{0,16},{16,24},{24,8},{8,0},{1,17},{17,25},{25,9},{9,1},{2,18},{18... | collective-permute-start | bytes 2359304 | tf_op jit(solution)/shard_map/ppermute | solution.py:550
  299.6 27.0 %all-to-all-start.5 = ((bf16[4,3,128,512]{3,2,1,0:T(8,128)(2,1)}), bf16[4,3,128,512]{3,2,1,0:T(8,128)(2,1)}, u32[]{:S(2)}, u32[]{:S(2)}) async-start(bf16[4,3,128,512]{3,2,1,0:T(8,128)(2,1)} %get-tuple-element.63), calls=%async_computation.6 | async-start | bytes 3145728 | tf_op jit(solution)/shard_map/all_to_all | solution.py:533
  342.1 4.2 %collective-permute-start.7 = (bf16[4,144,512]{2,1,0:T(8,128)(2,1)S(1)}, bf16[4,144,512]{2,1,0:T(8,128)(2,1)S(1)}, u32[]{:S(2)}, u32[]{:S(2)}) collective-permute-start(bf16[4,144,512]{2,1,0:T(8,128)(2,1)S(1)} %slice.148), channel_id=1, source_target_pairs={{0,1},{1,0},{2,3},{3,2},{4,5},{5,4},{6,7},{7,6},{8,9},{9,8},{10,11... | collective-permute-start | bytes 1769480 | tf_op jit(solution)/shard_map/ppermute | solution.py:567
  342.1 12.7 %all-to-all-start.4 = ((bf16[4,128,512]{2,1,0:T(8,128)(2,1)}), bf16[4,128,512]{2,1,0:T(8,128)(2,1)S(1)}, u32[]{:S(2)}, u32[]{:S(2)}) async-start(bf16[4,128,512]{2,1,0:T(8,128)(2,1)} %get-tuple-element.62), calls=%async_computation.5 | async-start | bytes 1048576 | tf_op jit(solution)/shard_map/all_to_all | solution.py:533
  346.4 6.8 %collective-permute-start.8 = (bf16[64,512]{1,0:T(8,128)(2,1)S(1)}, bf16[64,512]{1,0:T(8,128)(2,1)S(1)}, u32[]{:S(2)}, u32[]{:S(2)}) collective-permute-start(bf16[64,512]{1,0:T(8,128)(2,1)S(1)} %get-tuple-element.86), channel_id=1, source_target_pairs={{0,2},{1,3},{2,4},{3,5},{4,6},{5,7},{6,0},{7,1},{8,10},{9,11},{10,... | collective-permute-start | bytes 196616 | tf_op jit(solution)/shard_map/ppermute | solution.py:563
  346.5 6.8 %collective-permute-start.10 = (bf16[80,512]{1,0:T(8,128)(2,1)S(1)}, bf16[80,512]{1,0:T(8,128)(2,1)S(1)}, u32[]{:S(2)}, u32[]{:S(2)}) collective-permute-start(bf16[80,512]{1,0:T(8,128)(2,1)S(1)} %get-tuple-element.89), channel_id=1, source_target_pairs={{0,6},{1,7},{2,0},{3,1},{4,2},{5,3},{6,4},{7,5},{8,14},{9,15},{10,... | collective-permute-start | bytes 245768 | tf_op jit(solution)/shard_map/ppermute | solution.py:563
  353.3 9.7 %collective-permute-start.9 = (bf16[144,512]{1,0:T(8,128)(2,1)S(1)}, bf16[144,512]{1,0:T(8,128)(2,1)S(1)}, u32[]{:S(2)}, u32[]{:S(2)}) collective-permute-start(bf16[144,512]{1,0:T(8,128)(2,1)S(1)} %pad_maximum_fusion.1), channel_id=1, source_target_pairs={{0,2},{1,3},{2,4},{3,5},{4,6},{5,7},{6,0},{7,1},{8,10},{9,11},{10,... | collective-permute-start | bytes 442376 | tf_op jit(solution)/shard_map/ppermute | solution.py:563
  356.1 22.6 %all-to-all-start.7 = ((bf16[4,3,128,512]{3,2,1,0:T(8,128)(2,1)}), bf16[4,3,128,512]{3,2,1,0:T(8,128)(2,1)S(1)}, u32[]{:S(2)}, u32[]{:S(2)}) async-start(bf16[4,3,128,512]{3,2,1,0:T(8,128)(2,1)} %broadcast_in_dim.63), calls=%async_computation.8 | async-start | bytes 3145728 | tf_op jit(solution)/shard_map/all_to_all | solution.py:533
  359.8 5.7 %collective-permute-start.11 = (bf16[144,512]{1,0:T(8,128)(2,1)S(1)}, bf16[144,512]{1,0:T(8,128)(2,1)S(1)}, u32[]{:S(2)}, u32[]{:S(2)}) collective-permute-start(bf16[144,512]{1,0:T(8,128)(2,1)S(1)} %pad_maximum_fusion.2), channel_id=1, source_target_pairs={{0,6},{1,7},{2,0},{3,1},{4,2},{5,3},{6,4},{7,5},{8,14},{9,15},{10,... | collective-permute-start | bytes 442376 | tf_op jit(solution)/shard_map/ppermute | solution.py:563
  379.6 14.5 %all-to-all-start.6 = ((bf16[4,144,512]{2,1,0:T(8,128)(2,1)}), bf16[4,144,512]{2,1,0:T(8,128)(2,1)S(1)}, u32[]{:S(2)}, u32[]{:S(2)}) async-start(bf16[4,144,512]{2,1,0:T(8,128)(2,1)} %broadcast_in_dim.62), calls=%async_computation.7 | async-start | bytes 1179648 | tf_op jit(solution)/shard_map/all_to_all | solution.py:533
  (14 other events, 161.5 us)
Sparse Core Ops, SparseCore 0:
  10.5 25.3 all-gather.5
  91.2 47.3 all-gather.7
  219.4 48.2 reduce-scatter.1

commit v3 on v2

v3 whole, which is shorter than its diff:
```python
import functools

import jax
import jax.numpy as jnp
from jax import lax
from jax.experimental import pallas as pl
from jax.experimental.pallas import tpu as pltpu
from jax.sharding import PartitionSpec as P

epsilon = 1e-06
f32 = jnp.float32
bf16 = jnp.bfloat16
LANES = 128
EDGE = 16
VECTOR = 160


def round_up(value, multiple):
    return -(-value // multiple) * multiple


def call(kernel, grid, in_specs, out_specs, out_shape, scratch, flops, moved, prefetch=0, mib=54):
    return pl.pallas_call(
        kernel,
        grid_spec=pltpu.PrefetchScalarGridSpec(
            num_scalar_prefetch=prefetch,
            grid=grid,
            in_specs=in_specs,
            out_specs=out_specs,
            scratch_shapes=scratch,
        ),
        out_shape=out_shape,
        compiler_params=pltpu.CompilerParams(vmem_limit_bytes=mib * 2**20),
        cost_estimate=pl.CostEstimate(flops=flops, bytes_accessed=moved, transcendentals=0),
    )


def whole(shape):
    return pl.BlockSpec(shape, lambda i, *_: (0,) * len(shape))


def lanes(shape):
    return pl.BlockSpec(shape[:-1] + (LANES,), lambda i, *_: (0,) * (len(shape) - 1) + (i,))


def project_kernel(
    per_step, features, rows, gain_row, x_ref, gain_ref, w_ref, p_ref, scale_ref, total, squares
):
    step = pl.program_id(0)
    width = x_ref.shape[2]

    @pl.when(step == 0)
    def _():
        total[...] = jnp.zeros_like(total)
        squares[...] = jnp.zeros_like(squares)

    for part in range(per_step):
        x = x_ref[part, :rows, :].astype(f32)
        square = x * x
        running = squares[...]
        for lane in range(width // LANES):
            running = running + square[:, lane * LANES : (lane + 1) * LANES]
        squares[...] = running
        gain = gain_ref[part, gain_row : gain_row + 1, :].astype(f32)
        scaled = (x * gain).astype(bf16)
        for j in range(3):
            total[j] += jnp.dot(
                scaled, w_ref[j, part * width : (part + 1) * width, :], preferred_element_type=f32
            )

    @pl.when(step == pl.num_programs(0) - 1)
    def _():
        mean = jnp.sum(squares[...], axis=1, keepdims=True) / features
        scale = lax.rsqrt(mean + epsilon)
        scale_ref[...] = scale
        for j in range(3):
            p_ref[j] = (total[j] * scale).astype(bf16)


def project(chunks, gains, gain_block, gain_row, weights, rows):
    count, _, width = chunks.shape
    features, columns = weights.shape[1:]
    per_step = 2 if count % 2 == 0 else 1
    return call(
        functools.partial(project_kernel, per_step, features, rows, gain_row),
        (count // per_step,),
        [
            pl.BlockSpec((per_step, chunks.shape[1], width), lambda i: (i, 0, 0)),
            pl.BlockSpec((per_step, EDGE, width), lambda i: (i, gain_block // EDGE, 0)),
            pl.BlockSpec((3, per_step * width, columns), lambda i: (0, i, 0)),
        ],
        [whole((3, rows, columns)), whole((rows, 1))],
        [
            jax.ShapeDtypeStruct((3, rows, columns), bf16),
            jax.ShapeDtypeStruct((rows, 1), f32),
        ],
        [pltpu.VMEM((3, rows, columns), f32), pltpu.VMEM((rows, LANES), f32)],
        6 * rows * features * columns,
        6 * features * columns + 2 * rows * features,
    )(chunks, gains, weights)


def back_kernel(parts, order_ref, *refs):
    g_refs, w_refs = refs[:parts], refs[parts : parts + 2]
    extra_ref, o_ref, grads = refs[parts + 2 :]
    rows, columns = grads.shape[0], grads.shape[1] // 3

    @pl.when(pl.program_id(0) == 0)
    def _():
        first = 0
        for g_ref in g_refs:
            more = g_ref.shape[1]
            for j in range(3):
                grads[first : first + more, j * columns : (j + 1) * columns] = g_ref[j]
            first += more

    for piece, w_ref in enumerate(w_refs):
        weights = jnp.concatenate([w_ref[j] for j in range(3)], axis=1)
        o_ref[piece, :rows, :] = lax.dot_general(
            grads[...], weights, (((1,), (1,)), ((), ())), preferred_element_type=f32
        ).astype(bf16)
        if o_ref.shape[1] > rows:
            o_ref[piece, rows:, :] = extra_ref[...]


def project_back(parts, weights, order, extra=None):
    columns = parts[0].shape[2]
    rows = sum(part.shape[1] for part in parts)
    features = weights.shape[1]
    count = order.shape[0]
    width = features // count
    more = 0 if extra is None else extra.shape[0]
    if extra is None:
        extra = jnp.zeros((EDGE, width), bf16)
    return call(
        functools.partial(back_kernel, len(parts)),
        (count // 2,),
        [whole(part.shape) for part in parts]
        + [
            pl.BlockSpec((3, width, columns), lambda i, order: (0, order[2 * i], 0)),
            pl.BlockSpec((3, width, columns), lambda i, order: (0, order[2 * i + 1], 0)),
            whole(extra.shape),
        ],
        pl.BlockSpec((2, rows + more, width), lambda i, *_: (i, 0, 0)),
        jax.ShapeDtypeStruct((count, rows + more, width), bf16),
        [pltpu.VMEM((rows, 3 * columns), bf16)],
        6 * rows * features * columns,
        6 * features * columns + 2 * rows * features,
        prefetch=1,
    )(order, *parts, weights, weights, extra)


def weight_grad_kernel(spans, pieces, order_ref, piece_ref, gain_ref, *refs):
    x_refs, g_refs, out_ref = refs[:pieces], refs[pieces:-1], refs[-1]

    for piece, x_ref in enumerate(x_refs):

        @pl.when(pl.program_id(0) == piece)
        def _(x_ref=x_ref):
            for j in range(3):
                total = None
                for (slot, first), g_ref in zip(spans, g_refs):
                    some = x_ref[order_ref[slot], first : first + g_ref.shape[1], :]
                    term = lax.dot_general(
                        some, g_ref[j], (((0,), (0,)), ((), ())), preferred_element_type=f32
                    )
                    total = term if total is None else total + term
                out_ref[j] = total * gain_ref[0]


def weight_grad(columns, places, grads, order, gains):
    shards, rows, width = columns[0].shape
    pieces = len(columns)
    out = grads[0][2].shape[2]
    arrays = [array for _, _, array in grads]
    return call(
        functools.partial(weight_grad_kernel, [(slot, first) for slot, first, _ in grads], pieces),
        (pieces,),
        [pl.BlockSpec((1, width, 1), lambda i, order, places: (places[i], 0, 0))]
        + [whole(array.shape) for array in list(columns) + arrays],
        pl.BlockSpec((3, width, out), lambda i, order, places: (0, places[i], 0)),
        jax.ShapeDtypeStruct((3, pieces * width, out), f32),
        [],
        6 * shards * pieces * rows * width * out,
        2 * shards * pieces * rows * width + 6 * shards * rows * out + 12 * pieces * width * out,
        prefetch=2,
    )(order, places, gains, *columns, *arrays)


def fir(source, taps, target, mixed, mixed_taps, base, rows, forward):
    stride = rows // 8
    steps = stride // 4
    tap_count = taps.shape[0]
    quarter = tap_count // 4
    span = steps + quarter

    def row(position):
        return base + (position if forward else stride - 1 - position)

    def combine(x):
        even, odd, low, high = x[0] + x[2], x[1] + x[3], x[0] + x[1], x[2] + x[3]
        return [x[0], x[2], even, x[1], x[3], odd, low, high, even + odd]

    def mix(n, carry):
        first = 4 * (n - quarter)
        values = [source[pl.ds(row(first + p), 8, stride=stride), :] for p in range(4)]
        for c, value in enumerate(combine(values)):
            mixed[c, n] = value
        return carry

    lax.fori_loop(0, span, mix, 0, unroll=7 if span % 7 == 0 else 1)
    for c, value in enumerate(combine([taps[pl.ds(p, quarter, stride=4), :] for p in range(4)])):
        mixed_taps[c * quarter : (c + 1) * quarter, :] = value

    chunk = 8
    outs = steps + 1

    def product(c, carry):
        sums = [jnp.zeros((8, LANES), f32)] * outs
        for k0 in range(0, quarter, chunk):
            loaded = [mixed[c, quarter - 1 - k0 - (chunk - 1) + n] for n in range(outs + chunk - 1)]
            for k in range(chunk):
                tap = mixed_taps[pl.ds(c * quarter + k0 + k, 1), :]
                for p in range(outs):
                    sums[p] = sums[p] + tap * loaded[p + chunk - 1 - k]
        for p in range(outs):
            mixed[c, p] = sums[p]
        return carry

    lax.fori_loop(0, 9, product, 0, unroll=3)

    def finish(p, carry):
        now = [mixed[c, p + 1] for c in range(9)]
        old = [mixed[c, p] for c in range(6)]
        even_0, even_1 = now[0] + old[1], now[2] - now[0] - now[1]
        odd_0, odd_1 = now[3] + old[4], now[5] - now[3] - now[4]
        odd_old = old[5] - old[3] - old[4]
        both_0, both_1 = now[6] + mixed[7, p], now[8] - now[6] - now[7]
        values = [even_0 + odd_old, both_0 - even_0 - odd_0, even_1 + odd_0, both_1 - even_1 - odd_1]
        for n, value in enumerate(values):
            target[pl.ds(row(4 * p + n) - base, 8, stride=stride), :] = value
        return carry

    lax.fori_loop(0, steps, finish, 0, unroll=True)


def fir_scratch(rows, tap_count):
    return [
        pltpu.VMEM((9, rows // 32 + tap_count // 4, 8, LANES), f32),
        pltpu.VMEM((9 * tap_count // 4, LANES), f32),
    ]


def short_sum(source, short, j, first, rows, sign):
    total = None
    for i in range(short.shape[1]):
        term = short[j, i : i + 1, :] * source[first + sign * i : first + sign * i + rows, :]
        total = term if total is None else total + term
    return total


def look_up(token_ref, onehot):
    grid = lax.broadcasted_iota(jnp.int32, onehot.shape, 1)
    onehot[...] = (grid == token_ref[...]).astype(f32).astype(bf16)


def first_forward_kernel(
    front, rows, places, token_ref, e_ref, short_ref, medium_ref, *refs,
):
    p_refs = refs[: len(places)]
    middle_ref, filtered_ref = refs[len(places) : len(places) + 2]
    onehot, table, projected, gated, taps, kept, *mixed = refs[len(places) + 2 :]
    window, vocab = onehot.shape

    @pl.when(pl.program_id(0) == 0)
    def _():
        look_up(token_ref, onehot)

    taps[...] = medium_ref[...].astype(f32)
    extended = rows + 2 * EDGE
    for j in range(3):
        for place, p_ref in zip(places, p_refs):
            table[place : place + p_ref.shape[1], j * LANES : (j + 1) * LANES] = p_ref[j]
    looked = jnp.dot(onehot[...], table[...], preferred_element_type=f32)
    product = None
    for j in (1, 2, 0):
        projected[...] = looked[:, j * LANES : (j + 1) * LANES]
        if j == 0:
            kept[...] = short_sum(projected, short_ref, j, front - EDGE, extended, -1)
        else:
            feature = short_sum(projected, short_ref, j, 8, window - 8, -1)
            product = feature if product is None else product * feature
    gated[8:, :] = product.astype(bf16).astype(f32)
    fir(gated, taps, projected, *mixed, front - EDGE, extended, True)
    filtered = projected[:extended, :]
    filtered_ref[...] = filtered[EDGE:, :]
    embedded = jnp.dot(onehot[front - EDGE :, :], e_ref[...], preferred_element_type=f32)
    middle_ref[...] = (embedded + kept[...] * filtered).astype(bf16)


def first_forward(tokens, tables, embedding, short, medium, rows, front):
    share = tables[0][2].shape[1]
    places = [slot * share + first for slot, first, _ in tables]
    tables = [table for _, _, table in tables]
    extended = rows + 2 * EDGE
    window = front + rows + EDGE
    vocab, columns = embedding.shape
    shapes = [
        jax.ShapeDtypeStruct((extended, columns), bf16),
        jax.ShapeDtypeStruct((rows + EDGE, columns), f32),
    ]
    return call(
        functools.partial(first_forward_kernel, front, rows, places),
        (columns // LANES,),
        [pl.BlockSpec((window, 1), lambda i, *_: (0, 0))]
        + [lanes(a.shape) for a in (embedding, short, medium, *tables)],
        [lanes(s.shape) for s in shapes],
        shapes,
        [
            pltpu.VMEM((window, vocab), bf16),
            pltpu.VMEM((vocab, 3 * LANES), bf16),
            pltpu.VMEM((window, LANES), f32),
            pltpu.VMEM((window, LANES), f32),
            pltpu.VMEM((medium.shape[0], LANES), f32),
            pltpu.VMEM((extended, LANES), f32),
        ]
        + fir_scratch(extended, medium.shape[0]),
        8 * window * vocab * columns + 250 * VECTOR * rows * columns,
        8 * window * columns,
    )(tokens[:window], embedding, short, medium, *tables)


def first_features_kernel(places, token_ref, short_ref, *refs):
    p_refs = refs[: len(places)]
    feature_ref, onehot, table, projected = refs[len(places) :]

    @pl.when(pl.program_id(0) == 0)
    def _():
        look_up(token_ref, onehot)

    for j in range(3):
        for place, p_ref in zip(places, p_refs):
            table[place : place + p_ref.shape[1], :] = p_ref[j]
        projected[...] = jnp.dot(onehot[...], table[...], preferred_element_type=f32)
        feature_ref[j] = short_sum(projected, short_ref, j, EDGE, feature_ref.shape[1], -1)


def first_features(tokens, tables, short):
    share = tables[0][2].shape[1]
    places = [slot * share + first for slot, first, _ in tables]
    vocab = share * (1 + max(slot for slot, _, _ in tables))
    tables = [table for _, _, table in tables]
    window = tokens.shape[0]
    columns = tables[0].shape[2]
    shape = jax.ShapeDtypeStruct((3, window - EDGE, columns), f32)
    return call(
        functools.partial(first_features_kernel, places),
        (columns // LANES,),
        [whole((window, 1))] + [lanes(a.shape) for a in (short, *tables)],
        lanes(shape.shape),
        shape,
        [
            pltpu.VMEM((window, vocab), bf16),
            pltpu.VMEM((vocab, LANES), bf16),
            pltpu.VMEM((window, LANES), f32),
        ],
        6 * window * vocab * columns + 50 * VECTOR * window * columns,
        16 * window * columns,
    )(tokens, short, *tables)


def first_backward_kernel(
    rows, token_ref, above_ref, halo_ref, feature_ref, filtered_ref, short_ref, medium_ref,
    out_ref, onehot, signal, grad_gated, taps, held, *mixed,
):
    vocab = onehot.shape[0]
    parts = out_ref.shape[0]

    @pl.when(pl.program_id(0) == 0)
    def _():
        grid = lax.broadcasted_iota(jnp.int32, (vocab, rows), 0)
        onehot[...] = (grid == token_ref[...]).astype(f32).astype(bf16)

    taps[...] = medium_ref[...].astype(f32)
    extended = rows + EDGE
    above = jnp.concatenate([above_ref[...], halo_ref[...]], axis=0).astype(f32)
    signal[...] = (above * feature_ref[0]).astype(bf16).astype(f32)
    fir(signal, taps, grad_gated, *mixed, 0, extended + EDGE, False)

    def keep(j, value):
        held[...] = value.astype(bf16).astype(f32)
        grad = short_sum(held, short_ref, j, 0, rows, 1).astype(bf16)
        total = jnp.dot(onehot[...], grad, preferred_element_type=f32).astype(bf16)
        for part in range(parts):
            size = vocab // parts
            out_ref[part, j] = total[part * size : (part + 1) * size, :]

    keep(0, above[:extended, :] * filtered_ref[...])
    keep(1, grad_gated[:extended, :] * feature_ref[2, :extended, :])
    keep(2, grad_gated[:extended, :] * feature_ref[1, :extended, :])
    total = jnp.dot(onehot[...], above_ref[...], preferred_element_type=f32).astype(bf16)
    for part in range(parts):
        size = vocab // parts
        out_ref[part, 3] = total[part * size : (part + 1) * size, :]


def first_backward(tokens, above, halo, features, filtered, short, medium, vocab, parts):
    rows, columns = above.shape
    later = rows + halo.shape[0]
    operands = (above, halo, features, filtered, short, medium)
    shape = jax.ShapeDtypeStruct((parts, 4, vocab // parts, columns), bf16)
    return call(
        functools.partial(first_backward_kernel, rows),
        (columns // LANES,),
        [whole((1, rows))] + [lanes(a.shape) for a in operands],
        lanes(shape.shape),
        shape,
        [
            pltpu.VMEM((vocab, rows), bf16),
            pltpu.VMEM((later, LANES), f32),
            pltpu.VMEM((rows + 2 * EDGE, LANES), f32),
            pltpu.VMEM((medium.shape[0], LANES), f32),
            pltpu.VMEM((rows + EDGE, LANES), f32),
        ]
        + fir_scratch(rows + 2 * EDGE, medium.shape[0]),
        8 * rows * vocab * columns + 250 * VECTOR * rows * columns,
        16 * later * columns,
    )(tokens, *operands)


SEGMENTS = 8
SHIFT = 8


def summed(terms):
    while len(terms) > 1:
        terms = [a + b for a, b in zip(terms[::2], terms[1::2])] + terms[len(terms) // 2 * 2 :]
    return terms[0]


def scan_modes(source, decays, states, length, forward, residues=None, target=None):
    first = 0 if forward else SHIFT

    def step(i, held):
        position = first + (i if forward else length - 1 - i)
        value = source[pl.ds(position, SEGMENTS, stride=length), :]
        held = tuple(d * s + value for d, s in zip(decays, held))
        if target is not None:
            target[pl.ds(position, SEGMENTS, stride=length), :] = summed(
                [r * s for r, s in zip(residues, held)]
            )
        return held

    return lax.fori_loop(0, length, step, tuple(states), unroll=4)


def spread(ref, count):
    return [jnp.broadcast_to(ref[m : m + 1, :], (SEGMENTS, LANES)) for m in range(count)]


def second_features_kernel(
    p_ref, short_ref, above_ref, rate_ref,
    feature_ref, gated_ref, signal_ref, segment_ref, closing_ref, projected, gated, signal, decay,
):
    extended = above_ref.shape[0]
    modes = rate_ref.shape[0]
    length = (extended - EDGE) // SEGMENTS
    product = None
    for j in range(3):
        projected[...] = p_ref[j].astype(f32)
        feature = short_sum(projected, short_ref, j, EDGE, extended, -1)
        feature_ref[j] = feature
        if j == 0:
            rounded = (above_ref[...].astype(f32) * feature).astype(bf16)
            signal_ref[...] = rounded
            signal[...] = rounded.astype(f32)
        else:
            product = feature if product is None else product * feature
    rounded = product.astype(bf16)
    gated_ref[...] = rounded
    gated[...] = rounded.astype(f32)
    rates = rate_ref[...]
    decay[...] = jnp.exp(-rates)
    zeros = [jnp.zeros((SEGMENTS, LANES), f32)] * modes
    for way, source in enumerate((gated, signal)):
        ends = scan_modes(source, spread(decay, modes), zeros, length, way == 0)
        for m in range(modes):
            segment_ref[way, pl.ds(m, SEGMENTS, stride=modes), :] = ends[m]
        stride = jnp.exp(-rates * length)
        total = jnp.zeros((modes, LANES), f32)
        for n in range(SEGMENTS):
            at = n if way == 0 else SEGMENTS - 1 - n
            total = stride * total + segment_ref[way, at * modes : (at + 1) * modes, :]
        closing_ref[way] = total


def second_features(projected, short, above, rates):
    extended, columns = above.shape
    modes = rates.shape[0]
    shapes = [
        jax.ShapeDtypeStruct((3, extended, columns), f32),
        jax.ShapeDtypeStruct((extended, columns), bf16),
        jax.ShapeDtypeStruct((extended, columns), bf16),
        jax.ShapeDtypeStruct((2, SEGMENTS * modes, columns), f32),
        jax.ShapeDtypeStruct((2, modes, columns), f32),
    ]
    return call(
        second_features_kernel,
        (columns // LANES,),
        [lanes(a.shape) for a in (projected, short, above, rates)],
        [lanes(s.shape) for s in shapes],
        shapes,
        [
            pltpu.VMEM((extended + EDGE, LANES), f32),
            pltpu.VMEM((extended, LANES), f32),
            pltpu.VMEM((extended, LANES), f32),
            pltpu.VMEM((modes, LANES), f32),
        ],
        120 * VECTOR * extended * columns,
        24 * extended * columns,
    )(projected, short, above, rates)


def second_filter_kernel(
    shards, seq_ref, feature_ref, gated_ref, signal_ref, segment_ref, closing_ref, rate_ref,
    residue_ref, above_ref, middle_ref, p_ref, short_ref, scale_ref,
    out_ref, top_ref, bottom_ref, term_ref,
    entering, source, filtered, grad_gated, decay, residue, ends, held,
):
    rows = out_ref.shape[0]
    modes = rate_ref.shape[0]
    length = rows // SEGMENTS
    reach = rows + SHIFT
    me = seq_ref[0]
    rates = rate_ref[...]
    decay[...] = jnp.exp(-rates)
    residue[...] = residue_ref[...]
    stride = jnp.exp(-rates * length)
    for way, (values, target) in enumerate(((gated_ref, filtered), (signal_ref, grad_gated))):
        source[way] = values[...].astype(f32)
        state = jnp.zeros((modes, LANES), f32)
        for shard in range(shards):
            ahead = me - 1 - shard if way == 0 else shard - me - 1
            weight = jnp.exp(-rates * (rows * jnp.maximum(ahead, 0)).astype(f32))
            state = state + jnp.where(ahead >= 0, weight * closing_ref[shard, way], 0.0)
        for n in range(SEGMENTS):
            at = n if way == 0 else SEGMENTS - 1 - n
            entering[at * modes : (at + 1) * modes, :] = state
            state = stride * state + segment_ref[way, at * modes : (at + 1) * modes, :]
        ends[way] = state
        starts = [entering[pl.ds(m, SEGMENTS, stride=modes), :] for m in range(modes)]
        scan_modes(
            source.at[way], spread(decay, modes), starts, length, way == 0,
            spread(residue, modes), target,
        )

    upper = lax.broadcasted_iota(jnp.int32, (SEGMENTS, LANES), 0) < SEGMENTS // 2
    decays, residues = spread(decay, modes), spread(residue, modes)
    states = [
        jnp.where(upper, a, b)
        for a, b in zip(spread(ends.at[0], modes), spread(ends.at[1], modes))
    ]
    for i in range(SHIFT):
        after, before = rows + i, SHIFT - 1 - i
        value = jnp.where(upper, source[0, after : after + 1, :], source[1, before : before + 1, :])
        states = [d * s + value for d, s in zip(decays, states)]
        result = summed([r * s for r, s in zip(residues, states)])
        filtered[after : after + 1, :] = result[:1, :]
        grad_gated[before : before + 1, :] = result[SEGMENTS // 2 : SEGMENTS // 2 + 1, :]

    out_ref[...] = (
        middle_ref[EDGE : EDGE + rows, :].astype(f32) + feature_ref[0, :rows, :] * filtered[:rows, :]
    ).astype(bf16)
    above = above_ref[...].astype(f32)[:reach, :]
    scale = scale_ref[EDGE : EDGE + rows, :]
    terms = None
    for j in range(3):
        if j == 0:
            grad = above * filtered[...]
        else:
            grad = grad_gated[...] * feature_ref[3 - j, :reach, :]
        held[...] = grad.astype(bf16).astype(f32)
        grad = short_sum(held, short_ref, j, 0, rows, 1)
        term = grad * p_ref[j, EDGE : EDGE + rows, :].astype(f32)
        terms = term if terms is None else terms + term
        scaled = (grad * scale).astype(bf16)
        top_ref[j] = scaled[: rows // 2, :]
        bottom_ref[j] = scaled[rows // 2 :, :]
    total = jnp.sum(terms, axis=1, keepdims=True)

    @pl.when(pl.program_id(0) == 0)
    def _():
        term_ref[...] = total

    @pl.when(pl.program_id(0) > 0)
    def _():
        term_ref[...] += total


def second_filter(
    seq, features, gated, signal, segments, closings, rates, residues, above, middle, projected,
    short, scale,
):
    extended, columns = above.shape
    rows = extended - EDGE
    modes = rates.shape[0]
    shapes = [
        jax.ShapeDtypeStruct((rows, columns), bf16),
        jax.ShapeDtypeStruct((3, rows // 2, columns), bf16),
        jax.ShapeDtypeStruct((3, rows // 2, columns), bf16),
        jax.ShapeDtypeStruct((rows, 1), f32),
    ]
    operands = (
        features, gated, signal, segments, closings, rates, residues, above, middle, projected, short,
    )
    return call(
        functools.partial(second_filter_kernel, closings.shape[0]),
        (columns // LANES,),
        [lanes(a.shape) for a in operands] + [whole(scale.shape)],
        [lanes(s.shape) for s in shapes[:3]] + [whole((rows, 1))],
        shapes,
        [pltpu.VMEM((SEGMENTS * modes, LANES), f32), pltpu.VMEM((2, extended, LANES), f32)]
        + [pltpu.VMEM((rows + SHIFT, LANES), f32)] * 2
        + [pltpu.VMEM((modes, LANES), f32)] * 2
        + [pltpu.VMEM((2, modes, LANES), f32), pltpu.VMEM((rows + SHIFT, LANES), f32)],
        250 * VECTOR * rows * columns,
        40 * rows * columns,
        prefetch=1,
    )(seq, *operands, scale)


def shift(value, axis, by):
    devices = lax.axis_size(axis)
    pairs = [(i, i + by) for i in range(devices) if 0 <= i + by < devices]
    return lax.ppermute(value, axis, pairs)


def gather_ch(value):
    return lax.all_gather(value, "ch", axis=0, tiled=False)


def scatter_ch(value):
    return lax.psum_scatter(value, "ch", scatter_dimension=0, tiled=False)


def exchange_seq(value):
    return lax.all_to_all(value, "seq", split_axis=0, concat_axis=0, tiled=True)


def gather_seq(value):
    return exchange_seq(jnp.broadcast_to(value[None], (lax.axis_size("seq"),) + value.shape))


def seq_ring():
    devices = lax.axis_size("seq")
    if devices % 2:
        return list(range(devices))
    return list(range(0, devices, 2)) + list(range(devices - 1, 0, -2))


def seq_hop(value, by):
    ring = seq_ring()
    pairs = [(ring[i], ring[(i + by) % len(ring)]) for i in range(len(ring))]
    return lax.ppermute(value, "seq", pairs)


def ring_gather(parts):
    shards = lax.axis_size("seq")
    firsts = [0, parts[0].shape[1]][: len(parts)]
    out = [(0, first, part) for first, part in zip(firsts, parts)]
    up = down = parts
    for step in range(1, (shards + 1) // 2):
        up, down = [seq_hop(a, 1) for a in up], [seq_hop(a, -1) for a in down]
        out += [(shards - step, first, part) for first, part in zip(firsts, up)]
        out += [(step, first, part) for first, part in zip(firsts, down)]
    if shards % 2 == 0:
        if len(parts) == 1:
            half = parts[0].shape[1] // 2
            up, down = [up[0][:, :half]], [down[0][:, half:]]
        else:
            half = firsts[1]
        out += [(shards // 2, 0, seq_hop(up[0], 1)), (shards // 2, half, seq_hop(down[-1], -1))]
    return out


def ring_order():
    ring = seq_ring()
    twice = jnp.array(ring + ring, jnp.int32)
    place = jnp.argmax(twice[: len(ring)] == lax.axis_index("seq")).astype(jnp.int32)
    return lax.dynamic_slice_in_dim(twice, place, len(ring), 0)


def ch_hop(value, by):
    devices = lax.axis_size("ch")
    pairs = [(i, (i + 2 * by) % devices) for i in range(devices)]
    return lax.ppermute(value, "ch", pairs)


def sibling(value):
    return lax.ppermute(value, "ch", [(i, i ^ 1) for i in range(lax.axis_size("ch"))])


def scatter_order():
    devices = lax.axis_size("ch")
    me = lax.axis_index("ch")
    places = jnp.arange(devices // 2, dtype=jnp.int32)
    return jnp.concatenate([(2 * places + other) % devices for other in (me, me ^ 1)])


def added(*terms):
    return functools.reduce(lambda a, b: a + b, [t.astype(f32) for t in terms])


def ring_scatter(pieces, near, far):
    half = pieces.shape[0] // 2
    pieces, *near = tie(pieces, *near)
    mine = added(pieces[:half], sibling(pieces[half:])).astype(bf16)
    if half == 1:
        return mine[0].astype(f32), near, far
    steps = (half - 1) // 2
    rows = mine.shape[1]
    middle = rows // 32 * 16
    up = down = None
    if half % 2 == 0:
        opposite = mine[half // 2]
        up, down = ch_hop(opposite[:middle], 1), ch_hop(opposite[middle:], -1)
        if half == 2:
            return added(mine[0], jnp.concatenate([up, down], axis=0)), near, far
    for step in range(steps, 0, -1):
        first, second = mine[step], mine[half - step]
        if up is not None and step == steps and half % 2 == 0:
            first = jnp.concatenate(
                [added(first[:middle], up).astype(bf16), first[middle:]], axis=0
            )
            second = jnp.concatenate(
                [second[:middle], added(second[middle:], down).astype(bf16)], axis=0
            )
        elif up is not None:
            first, second = added(first, up).astype(bf16), added(second, down).astype(bf16)
        up, down = ch_hop(first, 1), ch_hop(second, -1)
    up, down, *far = tie(up, down, *far)
    return added(mine[0], up, down), near, far


def tie(*values):
    return lax.optimization_barrier(values)


def per_device(
    token_ids,
    embedding,
    gain_first,
    gain_second,
    weights_first,
    weights_second,
    short_first,
    short_second,
    medium,
    residues,
    decay_rates,
    cotangent,
):
    shards = lax.axis_size("seq")
    pieces = lax.axis_size("ch")
    seq = lax.axis_index("seq")
    vocab, width = embedding.shape
    rows = token_ids.shape[0]
    features = width * pieces
    taps, tap_count = medium.shape[0], short_first.shape[0]
    front = round_up(EDGE + taps - 1 + tap_count - 1, 16)
    back = round_up(2 * EDGE + taps - 1, 16)
    w_first, w_second = (jnp.transpose(w, (1, 0, 2)) for w in (weights_first, weights_second))
    s_first, s_second = (jnp.transpose(s, (1, 0, 2)) for s in (short_first, short_second))

    order = ring_order()
    each = pieces // shards
    share = vocab // shards
    at = seq * share

    gains = jnp.concatenate(
        [gain_first[None], gain_second[None], jnp.zeros((EDGE - 2, width), bf16)], axis=0
    )
    own_embedding = lax.dynamic_slice_in_dim(embedding, at, share, 0)
    gathered = gather_ch(jnp.concatenate([own_embedding, gains], axis=0))
    tokens = lax.all_gather(token_ids, "seq", axis=0, tiled=True)
    slots = jnp.zeros(shards, jnp.int32).at[order].set(jnp.arange(shards, dtype=jnp.int32))
    turned = jnp.take(embedding.reshape(shards, share, width), order, axis=0)
    turned = turned.reshape(vocab, width)
    tokens = jnp.take(slots, tokens // share) * share + tokens % share
    tokens = jnp.pad(tokens, (front, back), constant_values=-1)
    tokens = lax.dynamic_slice_in_dim(tokens, seq * rows, front + rows + back, 0)
    behind = shift(cotangent[:EDGE], "seq", -1)
    cotangents = jnp.concatenate([cotangent, behind], axis=0)
    tokens, turned, cotangents, gathered = tie(tokens[:, None], turned, cotangents, gathered)
    gains_first = gathered[:, share : share + 1, :].astype(f32)
    gains_second = gathered[:, share + 1 : share + 2, :].astype(f32)
    own_table, own_scale = project(gathered, gathered, share, 0, w_first, share)
    tables = ring_gather([own_table])

    middle, filtered_first = first_forward(tokens, tables, turned, s_first, medium, rows, front)
    later, held = tie(tokens[front - EDGE :], middle)
    features_first = first_features(later, tables, s_first)

    middles = gather_ch(middle)
    block = exchange_seq(gathered[:, :share, :].reshape(shards, each, share, width))
    block, features_first, middles = tie(block, features_first, middles)
    core = lax.axis_index("ch") % each
    own = middles.reshape(shards, each, rows + 2 * EDGE, width)
    own = lax.dynamic_slice(own, (0, core, EDGE, 0), (shards, 1, rows, width))
    projected, scale = project(middles, gathered, share, 1, w_second, rows + 2 * EDGE)
    features_second, gated, signal, segments, closing = second_features(
        projected, s_second, cotangents, decay_rates
    )
    own, closings = tie(own[:, 0], gather_seq(closing))
    columns = exchange_seq(own)
    output, *grads, terms = second_filter(
        seq[None], features_second, gated, signal, segments, closings,
        decay_rates, residues, cotangents, middle, projected, s_second, scale,
    )
    scale = scale[EDGE : EDGE + rows]
    pieces_of = ring_gather(grads)
    partial = project_back(grads, w_second, jnp.arange(pieces, dtype=jnp.int32))
    partial, columns = tie(partial, columns)
    other = sibling(columns)
    partial_sum = scatter_ch(partial)
    terms = lax.psum(terms[:, 0], "ch")
    partial_sum, other, *arrays = tie(partial_sum, other, *[a for _, _, a in pieces_of[2:-2]])
    pieces_of[2:-2] = [old[:2] + (new,) for old, new in zip(pieces_of[2:-2], arrays)]
    grad_normed = partial_sum.astype(f32)
    as_float = middle[EDGE : EDGE + rows].astype(f32)
    grad_middle = (
        cotangent.astype(f32)
        + gain_second.astype(f32) * grad_normed
        - as_float * (scale * scale) * terms[:, None] / features
    ).astype(bf16)
    grad_gain_second = jnp.sum(grad_normed * as_float, axis=0)

    halo = shift(grad_middle[:back], "seq", -1)
    halo, far_up, far_down = tie(halo, pieces_of[-2][2], pieces_of[-1][2])
    pieces_of[-2:] = [pieces_of[-2][:2] + (far_up,), pieces_of[-1][:2] + (far_down,)]
    sums = first_backward(
        token_ids[None], grad_middle, halo, features_first, filtered_first, s_first, medium, vocab, shards
    )
    sums = exchange_seq(sums)
    block_gains = lax.dynamic_slice_in_dim(gains_second, seq * each, each, 0)
    places = jnp.stack([core, 1 - core]).astype(jnp.int32)
    grad_weights_second = weight_grad(
        [columns, other], places, pieces_of, order, jnp.swapaxes(block_gains, 1, 2)
    )
    sums, grad_weights_second = tie(sums, grad_weights_second)
    own_sums = jnp.sum(sums.astype(f32), axis=0)
    terms = jnp.sum(own_sums[:3] * own_table.astype(f32), axis=(0, 2))
    own_grads = (own_sums[:3] * own_scale[None]).astype(bf16)
    all_grads = ring_gather([own_grads])
    extra_rows = -(-share // width)
    extra = jnp.pad(terms, (0, EDGE * width - share)).reshape(EDGE, width).astype(bf16)
    partial = project_back([own_grads], w_first, scatter_order(), extra)
    grad_normed, near, far = ring_scatter(
        partial, [a for _, _, a in all_grads[1:-2]], [a for _, _, a in all_grads[-2:]]
    )
    all_grads[1:] = [old[:2] + (new,) for old, new in zip(all_grads[1:], near + far)]
    terms = grad_normed[share : share + extra_rows].reshape(-1)[:share]
    grad_normed = grad_normed[:share]
    block_gains = lax.dynamic_slice_in_dim(gains_first, seq * each, each, 0)
    grad_weights_first = weight_grad(
        [block[:, i] for i in range(each)],
        jnp.arange(each, dtype=jnp.int32),
        all_grads,
        order,
        jnp.swapaxes(block_gains, 1, 2),
    )

    as_float = own_embedding.astype(f32)
    grad_embedding = (
        own_sums[3]
        + gain_first.astype(f32) * grad_normed
        - as_float * (own_scale * own_scale) * terms[:, None] / features
    )
    grad_gain_first = jnp.sum(grad_normed * as_float, axis=0)
    last = jnp.concatenate(
        [
            grad_embedding,
            grad_gain_first[None],
            grad_gain_second[None],
            jnp.zeros((EDGE - 2, width), f32),
        ],
        axis=0,
    ).astype(bf16)
    last = gather_seq(last).astype(f32)
    return (
        output,
        last[:, :share].reshape(vocab, width),
        jnp.sum(last[:, share], axis=0),
        jnp.sum(last[:, share + 1], axis=0),
        jnp.transpose(grad_weights_first, (1, 0, 2)),
        jnp.transpose(grad_weights_second, (1, 0, 2)),
    )


def solution(mesh):
    placed = (
        P("seq"),
        P(None, "ch"),
        P("ch"),
        P("ch"),
        P(None, None, "ch"),
        P(None, None, "ch"),
        P(None, None, "ch"),
        P(None, None, "ch"),
        P(None, "ch"),
        P(None, "ch"),
        P(None, "ch"),
        P("seq", "ch"),
    )
    return jax.shard_map(
        per_device,
        mesh=mesh,
        in_specs=placed,
        out_specs=(
            P("seq", "ch"),
            P(None, "ch"),
            P("ch"),
            P("ch"),
            P("seq", None, "ch"),
            P("seq", None, "ch"),
        ),
        check_vma=False,
    )
```

time: 404 us -> 352 us (0.87)
  waiting for transfers between devices: 141 us -> 101 us
  blocking collectives: 33.6 us -> 26 us
    all_to_all x7 -> x5, waiting for transfers between devices: 50 us -> 13.7 us  [exchange_seq(): return lax.all_to_all(value, 'seq', split_axis=0, concat_axis=0, tiled=True)]
    ppermute x4 -> x14, waiting for transfers between devices: 17.8 us -> 35 us  [seq_hop(): return lax.ppermute(value, 'seq', pairs)]
    all_gather x2, waiting for transfers between devices: 45.4 us -> 32.1 us  [gather_ch(): return lax.all_gather(value, 'ch', axis=0, tiled=False)]
    ppermute x4 -> x14, starting transfers between devices: 4.46 us -> 14.5 us  [seq_hop(): return lax.ppermute(value, 'seq', pairs)]
    all_to_all x1 -> x0, blocking collectives: 8.79 us -> none  [exchange_seq(): return lax.all_to_all(value, 'seq', split_axis=0, concat_axis=0, tiled=True)]
    all_to_all x7 -> x5, starting transfers between devices: 26.8 us -> 19.1 us  [exchange_seq(): return lax.all_to_all(value, 'seq', split_axis=0, concat_axis=0, tiled=True)]
    pallas_call x6, Pallas kernels: 69.2 us -> 62.7 us  [the longest x2 21 us: project_back(): call(functools.partial(back_kernel, len(parts)), (count // 2,), [whole(pa...]
    ppermute x2, waiting for transfers between devices: 8.96 us -> 3.32 us  [shift(): return lax.ppermute(value, axis, pairs)]
  transfers between devices with their start and end apart: 22 -> 30, of which waited for: 14 -> 18; matrix products, arithmetic and copies ran while one was open for 6% -> 8% of each run, Pallas kernels for 14% -> 18%
where the time goes in v3:
time: 352 us; the launch traced here: 351 us
  Pallas kernels  122 us (35%)
  waiting for transfers between devices  101 us (29%)
  starting transfers between devices  44.3 us (13%)
  local copies, waits for them, and re-layouts  26.6 us (8%)
  blocking collectives  26 us (7%)
  between operations  16.2 us (5%)
  other arithmetic  14.2 us (4%)
    ppermute x14, waiting for transfers between devices, seq_hop(): return lax.ppermute(value, 'seq', pairs)  35 us
    all_gather x2, waiting for transfers between devices, gather_ch(): return lax.all_gather(value, 'ch', axis=0, tiled=False)  32.1 us
    pallas_call x2, Pallas kernels, weight_grad(): call(functools.partial(weight_grad_kernel, [(slot, first) for slot, first...  22.2 us
    pallas_call x2, Pallas kernels, project_back(): call(functools.partial(back_kernel, len(parts)), (count // 2,), [whole(pa...  21 us
    pallas_call x2, Pallas kernels, project(): call(functools.partial(project_kernel, per_step, features, rows, gain_row...  19.5 us
    all_to_all x5, starting transfers between devices, exchange_seq(): return lax.all_to_all(value, 'seq', split_axis=0, concat_axis=0, tiled=True)  19.1 us
    pallas_call x1, Pallas kernels, first_forward(): call(functools.partial(first_forward_kernel, front, rows, places), (colum...  15 us
    ppermute x14, starting transfers between devices, seq_hop(): return lax.ppermute(value, 'seq', pairs)  14.5 us
  transfers between devices with their start and end apart: 30, of which 18 were waited for; matrix products, arithmetic and copies ran while one was open for 8% of the time, Pallas kernels for 18%

profile of v3, /device:TPU:0, one launch (start us, length us, event | category | flops | bytes accessed | tf_op | source)
XLA Modules:
  0.0 350.6 jit_solution(11113670517393046207)
XLA Ops:
  18.7 11.6 %all-gather.2 = s32[4,1,512]{2,1,0:T(1,128)S(1)} all-gather(s32[1,1,512]{2,1,0:T(1,128)} %bitcast.84), channel_id=1, replica_groups=mesh['seq'=4,'ch'=8] {'seq'}, dimensions={0}, use_global_device_ids=true | all-gather | bytes 10240 | tf_op jit(solution)/shard_map/all_gather | solution.py:785
  36.0 7.4 %shard_map.172 = (bf16[3,128,512]{2,1,0:T(8,128)(2,1)}, f32[128,1]{1,0:T(8,128)}) custom-call(bf16[8,144,512]{2,1,0:T(8,128)(2,1)} %bitcast.72, bf16[8,144,512]{2,1,0:T(8,128)(2,1)} %bitcast.73, bf16[3,4096,512]{2,1,0:T(8,128)(2,1)} %bitcast.66), custom_call_target="tpu_custom_call" | custom-call | flops 1610612736 | bytes 13631488 | tf_op jit(solution)/shard_map/pallas_call | solution.py:84
  45.6 9.2 %collective-permute-done.1.refs_1_ = bf16[3,128,512]{2,1,0:T(8,128)(2,1)S(1)} collective-permute-done((bf16[3,128,512]{2,1,0:T(8,128)(2,1)}, bf16[3,128,512]{2,1,0:T(8,128)(2,1)S(1)}, u32[]{:S(2)}, u32[]{:S(2)}) %collective-permute-start.1) | collective-permute-done | bytes 393248 | tf_op jit(solution)/shard_map/ppermute | solution.py:664
  63.0 15.0 %shard_map.173 = (bf16[544,512]{1,0:T(8,128)(2,1)}, f32[528,512]{1,0:T(8,128)}) custom-call(s32[688,1]{1,0:T(8,128)} %get-tuple-element.118.token_ref, bf16[512,512]{1,0:T(8,128)(2,1)} %bitcast_select_fusion.e_ref, f32[3,7,512]{2,1,0:T(8,128)} %bitcast.88, bf16[128,512]{1,0:T(8,128)(2,1)} %medium_ref.3, bf16[3,128,512]{2,1,0:T(8,128)(2,1)} %get-tuple-element.56.refs_0_, ...), custom_call_target="tpu_custom_call" | custom-call | flops 11928600576 | bytes 2818048 | tf_op jit(solution)/shard_map/pallas_call | solution.py:312
  82.6 7.2 %shard_map.174.feature_ref = f32[3,672,512]{2,1,0:T(8,128)} custom-call(s32[688,1]{1,0:T(8,128)} %get-tuple-element.58.token_ref, f32[3,7,512]{2,1,0:T(8,128)} %bitcast.89, bf16[3,128,512]{2,1,0:T(8,128)(2,1)} %get-tuple-element.56.refs_0_, bf16[3,128,512]{2,1,0:T(8,128)(2,1)} %copy-done.17, bf16[3,128,512]{2,1,0:T(8,128)(2,1)} %copy-done.18, ...), custom_call_target="tpu_custom_call" | custom-call | flops 3900178432 | bytes 5636096 | tf_op jit(solution)/shard_map/pallas_call | solution.py:356
  89.8 5.1 %all-to-all-done = bf16[4,2,128,512]{3,2,1,0:T(8,128)(2,1)S(1)} async-done(((bf16[4,2,128,512]{3,2,1,0:T(8,128)(2,1)}), bf16[4,2,128,512]{3,2,1,0:T(8,128)(2,1)S(1)}, u32[]{:S(2)}, u32[]{:S(2)}) %all-to-all-start) | async-done | bytes 1048608 | tf_op jit(solution)/shard_map/all_to_all | solution.py:647
  94.8 31.6 %all-gather.8.cloned.1.call-done = bf16[4352,512]{1,0:T(8,128)(2,1)} async-done(((bf16[544,512]{1,0:T(8,128)(2,1)}), bf16[4352,512]{1,0:T(8,128)(2,1)}) %all-gather.8.cloned.1.call-update) | async-done | bytes 4456464 | tf_op jit(solution)/shard_map/all_gather | solution.py:639
  126.5 12.2 %shard_map.175 = (bf16[3,544,512]{2,1,0:T(8,128)(2,1)}, f32[544,1]{1,0:T(8,128)}) custom-call(bf16[8,544,512]{2,1,0:T(8,128)(2,1)} %bitcast.80, bf16[8,144,512]{2,1,0:T(8,128)(2,1)} %bitcast.74, bf16[3,4096,512]{2,1,0:T(8,128)(2,1)} %bitcast.69), custom_call_target="tpu_custom_call" | custom-call | flops 6845104128 | bytes 17039360 | tf_op jit(solution)/shard_map/pallas_call | solution.py:84
  138.6 9.2 %shard_map.176 = (f32[3,528,512]{2,1,0:T(8,128)}, bf16[528,512]{1,0:T(8,128)(2,1)}, bf16[528,512]{1,0:T(8,128)(2,1)}, f32[2,128,512]{2,1,0:T(8,128)}, f32[2,16,512]{2,1,0:T(8,128)}) custom-call(bf16[3,544,512]{2,1,0:T(8,128)(2,1)} %get-tuple-element.60.p_ref, f32[3,7,512]{2,1,0:T(8,128)} %bitcast.86, bf16[528,512]{1,0:T(8,128)(2,1)} %pad_maximum_fusion.above_ref, ...), custom_call_target="tpu_custom_call" | custom-call | flops 5190451200 | bytes 6488064 | tf_op jit(solution)/shard_map/pallas_call | solution.py:507
  149.4 3.6 %all-to-all-start.1 = ((f32[4,2,16,512]{3,2,1,0:T(8,128)}), f32[4,2,16,512]{3,2,1,0:T(8,128)S(1)}, u32[]{:S(2)}, u32[]{:S(2)}) async-start(f32[4,2,16,512]{3,2,1,0:T(8,128)} %broadcast_in_dim.78), calls=%async_computation.1 | async-start | bytes 524288 | tf_op jit(solution)/shard_map/all_to_all | solution.py:647
  159.5 4.4 %all-to-all-start.2 = ((bf16[4,512,512]{2,1,0:T(8,128)(2,1)}), bf16[4,512,512]{2,1,0:T(8,128)(2,1)}, u32[]{:S(2)}, u32[]{:S(2)}) async-start(bf16[4,512,512]{2,1,0:T(8,128)(2,1)} %dynamic-slice_bitcast_fusion), calls=%async_computation.2 | async-start | bytes 4194304 | tf_op jit(solution)/shard_map/all_to_all | solution.py:647
  164.0 14.2 %shard_map.177 = (bf16[512,512]{1,0:T(8,128)(2,1)}, bf16[3,256,512]{2,1,0:T(8,128)(2,1)}, bf16[3,256,512]{2,1,0:T(8,128)(2,1)}, f32[512,1]{1,0:T(8,128)}) custom-call(s32[1]{0:T(128)} %bitcast.seq_ref, f32[3,528,512]{2,1,0:T(8,128)} %get-tuple-element.62.feature_ref, bf16[528,512]{1,0:T(8,128)(2,1)} %get-tuple-element.63.gated_ref, ...), custom_call_target="tpu_custom_call" | custom-call | flops 10485760000 | bytes 10485760 | tf_op jit(solution)/shard_map/pallas_call | solution.py:616
  179.4 12.0 %shard_map.178 = bf16[8,512,512]{2,1,0:T(8,128)(2,1)} custom-call(s32[8]{0:T(128)} %iota.20.order_ref, bf16[3,256,512]{2,1,0:T(8,128)(2,1)} %get-tuple-element.70.refs_0_.refs_2_, bf16[3,256,512]{2,1,0:T(8,128)(2,1)} %get-tuple-element.71.refs_1_.refs_3_, bf16[3,4096,512]{2,1,0:T(8,128)(2,1)} %bitcast.70, bf16[3,4096,512]{2,1,0:T(8,128)(2,1)} %bitcast.71, ...), custom_call_target="tpu_custom_call" | custom-call | flops 6442450944 | bytes 16777216 | tf_op jit(solution)/shard_map/pallas_call | solution.py:135
  196.6 16.5 %collective-permute-done.6.refs_4_ = bf16[3,256,512]{2,1,0:T(8,128)(2,1)} collective-permute-done((bf16[3,256,512]{2,1,0:T(8,128)(2,1)S(1)}, bf16[3,256,512]{2,1,0:T(8,128)(2,1)}, u32[]{:S(2)}, u32[]{:S(2)}) %collective-permute-start.6) | collective-permute-done | bytes 786464 | tf_op jit(solution)/shard_map/ppermute | solution.py:664
  215.6 14.5 %psum.7 = f32[512]{0:T(512)S(1)} all-reduce(f32[512]{0:T(512)S(1)} %reduce.21), channel_id=1, replica_groups=mesh['seq'=4,'ch'=8] {'ch'}, use_global_device_ids=true, to_apply=%region_3.4 | all-reduce | flops 512 | bytes 4096 | tf_op jit(solution)/shard_map/psum | solution.py:826
  232.1 9.1 %reduce-scatter.2.cloned.1.call-done = bf16[1,512,512]{2,1,0:T(8,128)(2,1)} async-done(((bf16[8,512,512]{2,1,0:T(8,128)(2,1)}), bf16[1,512,512]{2,1,0:T(8,128)(2,1)}) %reduce-scatter.2.cloned.1.call-update) | async-done | bytes 524304 | tf_op jit(solution)/shard_map/reduce_scatter | solution.py:643
  251.1 13.9 %shard_map.179 = bf16[4,4,128,512]{3,2,1,0:T(8,128)(2,1)} custom-call(s32[1,512]{1,0:T(1,128)} %bitcast.85, bf16[512,512]{1,0:T(8,128)(2,1)} %copy-done.7, bf16[160,512]{1,0:T(8,128)(2,1)} %copy-done.30, f32[3,672,512]{2,1,0:T(8,128)} %shard_map.174.feature_ref, f32[528,512]{1,0:T(8,128)} %get-tuple-element.79.filtered_ref, f32[3,7,512]{2,1,0:T(8,128)} %bitcast.90, ...), custom_call_target="tpu_custom_call" | custom-call | flops 11559501824 | bytes 5505024 | tf_op jit(solution)/shard_map/pallas_call | solution.py:412
  265.0 3.8 %all-to-all-start.3 = ((bf16[4,4,128,512]{3,2,1,0:T(8,128)(2,1)}), bf16[4,4,128,512]{3,2,1,0:T(8,128)(2,1)S(1)}, u32[]{:S(2)}, u32[]{:S(2)}) async-start(bf16[4,4,128,512]{3,2,1,0:T(8,128)(2,1)} %shard_map.179), calls=%async_computation.4 | async-start | bytes 4194304 | tf_op jit(solution)/shard_map/all_to_all | solution.py:647
  272.7 13.4 %shard_map.180 = f32[3,1024,512]{2,1,0:T(8,128)} custom-call(s32[4]{0:T(128)} %dynamic_slice.18.order_ref, s32[2]{0:T(128)} %pad_add_fusion.piece_ref, f32[2,512,1]{2,1,0:T(8,128)} %transpose.59.gain_ref, bf16[4,512,512]{2,1,0:T(8,128)(2,1)} %all-to-all-done.2.refs_0_, bf16[4,512,512]{2,1,0:T(8,128)(2,1)} %collective-permute-done.5.refs_1_, ...), custom_call_target="tpu_custom_call" | custom-call | flops 6442450944 | bytes 16777216 | tf_op jit(solution)/shard_map/pallas_call | solution.py:176
  286.1 6.0 %all-to-all-done.3 = bf16[4,4,128,512]{3,2,1,0:T(8,128)(2,1)S(1)} async-done(((bf16[4,4,128,512]{3,2,1,0:T(8,128)(2,1)}), bf16[4,4,128,512]{3,2,1,0:T(8,128)(2,1)S(1)}, u32[]{:S(2)}, u32[]{:S(2)}) %all-to-all-start.3) | async-done | bytes 2097184 | tf_op jit(solution)/shard_map/all_to_all | solution.py:647
  296.2 9.0 %shard_map.181 = bf16[8,144,512]{2,1,0:T(8,128)(2,1)} custom-call(s32[8]{0:T(128)} %pad_add_fusion.1.order_ref, bf16[3,128,512]{2,1,0:T(8,128)(2,1)} %copy-done.4, bf16[3,4096,512]{2,1,0:T(8,128)(2,1)} %bitcast.67, bf16[3,4096,512]{2,1,0:T(8,128)(2,1)} %bitcast.68, bf16[16,512]{1,0:T(8,128)(2,1)} %convert_element_type.104.refs_3_), custom_call_target="tpu_custom_call" | custom-call | flops 1610612736 | bytes 13631488 | tf_op jit(solution)/shard_map/pallas_call | solution.py:135
  319.8 3.7 %collective-permute-done.17 = bf16[144,512]{1,0:T(8,128)(2,1)S(1)} collective-permute-done((bf16[144,512]{1,0:T(8,128)(2,1)S(1)}, bf16[144,512]{1,0:T(8,128)(2,1)S(1)}, u32[]{:S(2)}, u32[]{:S(2)}) %collective-permute-start.17) | collective-permute-done | bytes 147488 | tf_op jit(solution)/shard_map/ppermute | solution.py:696
  327.0 3.7 %all-to-all-start.4 = ((bf16[4,144,512]{2,1,0:T(8,128)(2,1)}), bf16[4,144,512]{2,1,0:T(8,128)(2,1)S(1)}, u32[]{:S(2)}, u32[]{:S(2)}) async-start(bf16[4,144,512]{2,1,0:T(8,128)(2,1)} %broadcast_in_dim.81), calls=%async_computation.5 | async-start | bytes 1179648 | tf_op jit(solution)/shard_map/all_to_all | solution.py:647
  333.4 8.8 %shard_map.182 = f32[3,1024,512]{2,1,0:T(8,128)} custom-call(s32[4]{0:T(128)} %dynamic_slice.18.order_ref, s32[2]{0:T(128)} %iota.22.piece_ref, f32[2,512,1]{2,1,0:T(8,128)} %transpose.60.gain_ref, bf16[4,128,512]{2,1,0:T(8,128)(2,1)} %get-tuple-element.109.refs_0_, bf16[4,128,512]{2,1,0:T(8,128)(2,1)} %get-tuple-element.108.refs_1_, ...), custom_call_target="tpu_custom_call" | custom-call | flops 1610612736 | bytes 8912896 | tf_op jit(solution)/shard_map/pallas_call | solution.py:176
  (185 shorter events, 89.3 us)
Async XLA Ops:
  7.2 28.8 %all-gather.6.cloned.1.call-start = ((), (), s32[]{:S(2)}) async-start(), calls=%async_computation.7 | async-start | bytes 1327104 | tf_op jit(solution)/shard_map/all_gather | solution.py:639
  10.4 116.0 %all-gather.8.cloned.1.call-start = ((), (), s32[]{:S(2)}) async-start(), calls=%async_computation.8 | async-start | bytes 5013504 | tf_op jit(solution)/shard_map/all_gather | solution.py:639
  11.2 23.4 %collective-permute-start = (bf16[16,512]{1,0:T(8,128)(2,1)S(1)}, bf16[16,512]{1,0:T(8,128)(2,1)S(1)}, u32[]{:S(2)}, u32[]{:S(2)}) collective-permute-start(bf16[16,512]{1,0:T(8,128)(2,1)S(1)} %slice.124), channel_id=1, source_target_pairs={{8,0},{16,8},{24,16},{9,1},{17,9},{25,17},{10,2},{18,10},{26,18},{... | collective-permute-start | bytes 49160 | tf_op jit(solution)/shard_map/ppermute | solution.py:635
  43.3 11.5 %collective-permute-start.1 = (bf16[3,128,512]{2,1,0:T(8,128)(2,1)}, bf16[3,128,512]{2,1,0:T(8,128)(2,1)S(1)}, u32[]{:S(2)}, u32[]{:S(2)}) collective-permute-start(bf16[3,128,512]{2,1,0:T(8,128)(2,1)} %get-tuple-element.56.refs_0_), channel_id=1, source_target_pairs={{0,16},{16,24},{24,8},{8,0},{1,17},{17,25},{25,9},{9,1},{2,18},{18... | collective-permute-start | bytes 1179656 | tf_op jit(solution)/shard_map/ppermute | solution.py:664
  44.8 11.5 %collective-permute-start.2 = (bf16[3,128,512]{2,1,0:T(8,128)(2,1)}, bf16[3,128,512]{2,1,0:T(8,128)(2,1)S(1)}, u32[]{:S(2)}, u32[]{:S(2)}) collective-permute-start(bf16[3,128,512]{2,1,0:T(8,128)(2,1)} %get-tuple-element.56.refs_0_), channel_id=1, source_target_pairs={{0,8},{16,0},{24,16},{8,24},{1,9},{17,1},{25,17},{9,25},{2,10},{18... | collective-permute-start | bytes 1179656 | tf_op jit(solution)/shard_map/ppermute | solution.py:664
  79.1 15.8 %all-to-all-start = ((bf16[4,2,128,512]{3,2,1,0:T(8,128)(2,1)}), bf16[4,2,128,512]{3,2,1,0:T(8,128)(2,1)S(1)}, u32[]{:S(2)}, u32[]{:S(2)}) async-start(bf16[4,2,128,512]{3,2,1,0:T(8,128)(2,1)} %bitcast.11), calls=%async_computation | async-start | bytes 2097152 | tf_op jit(solution)/shard_map/all_to_all | solution.py:647
  149.4 9.4 %all-to-all-start.1 = ((f32[4,2,16,512]{3,2,1,0:T(8,128)}), f32[4,2,16,512]{3,2,1,0:T(8,128)S(1)}, u32[]{:S(2)}, u32[]{:S(2)}) async-start(f32[4,2,16,512]{3,2,1,0:T(8,128)} %broadcast_in_dim.78), calls=%async_computation.1 | async-start | bytes 524288 | tf_op jit(solution)/shard_map/all_to_all | solution.py:647
  159.5 31.9 %all-to-all-start.2 = ((bf16[4,512,512]{2,1,0:T(8,128)(2,1)}), bf16[4,512,512]{2,1,0:T(8,128)(2,1)}, u32[]{:S(2)}, u32[]{:S(2)}) async-start(bf16[4,512,512]{2,1,0:T(8,128)(2,1)} %dynamic-slice_bitcast_fusion), calls=%async_computation.2 | async-start | bytes 4194304 | tf_op jit(solution)/shard_map/all_to_all | solution.py:647
  164.0 77.2 %reduce-scatter.2.cloned.1.call-start = ((), (), s32[]{:S(2)}) async-start(), calls=%async_computation.6 | async-start | bytes 4718592 | tf_op jit(solution)/shard_map/reduce_scatter | solution.py:643
  191.4 40.6 %collective-permute-start.5 = (bf16[4,512,512]{2,1,0:T(8,128)(2,1)}, bf16[4,512,512]{2,1,0:T(8,128)(2,1)}, u32[]{:S(2)}, u32[]{:S(2)}) collective-permute-start(bf16[4,512,512]{2,1,0:T(8,128)(2,1)} %all-to-all-done.2.refs_0_), channel_id=1, source_target_pairs={{0,1},{1,0},{2,3},{3,2},{4,5},{5,4},{6,7},{7,6},{8,9},{9,8},{10,11... | collective-permute-start | bytes 6291464 | tf_op jit(solution)/shard_map/ppermute | solution.py:700
  192.5 20.6 %collective-permute-start.6 = (bf16[3,256,512]{2,1,0:T(8,128)(2,1)S(1)}, bf16[3,256,512]{2,1,0:T(8,128)(2,1)}, u32[]{:S(2)}, u32[]{:S(2)}) collective-permute-start(bf16[3,256,512]{2,1,0:T(8,128)(2,1)S(1)} %copy-done.10), channel_id=1, source_target_pairs={{0,16},{16,24},{24,8},{8,0},{1,17},{17,25},{25,9},{9,1},{2,18},{18... | collective-permute-start | bytes 2359304 | tf_op jit(solution)/shard_map/ppermute | solution.py:664
  194.4 20.8 %collective-permute-start.9 = (bf16[3,256,512]{2,1,0:T(8,128)(2,1)}, bf16[3,256,512]{2,1,0:T(8,128)(2,1)}, u32[]{:S(2)}, u32[]{:S(2)}) collective-permute-start(bf16[3,256,512]{2,1,0:T(8,128)(2,1)} %get-tuple-element.71.refs_1_.refs_3_), channel_id=1, source_target_pairs={{0,8},{16,0},{24,16},{8,24},{1,9},{17,1},{25,17},{9,25},{2,10},{18... | collective-permute-start | bytes 2359304 | tf_op jit(solution)/shard_map/ppermute | solution.py:664
  194.5 35.6 %collective-permute-start.7 = (bf16[3,256,512]{2,1,0:T(8,128)(2,1)}, bf16[3,256,512]{2,1,0:T(8,128)(2,1)}, u32[]{:S(2)}, u32[]{:S(2)}) collective-permute-start(bf16[3,256,512]{2,1,0:T(8,128)(2,1)} %get-tuple-element.71.refs_1_.refs_3_), channel_id=1, source_target_pairs={{0,16},{16,24},{24,8},{8,0},{1,17},{17,25},{25,9},{9,1},{2,18},{18... | collective-permute-start | bytes 2359304 | tf_op jit(solution)/shard_map/ppermute | solution.py:664
  196.5 35.6 %collective-permute-start.8 = (bf16[3,256,512]{2,1,0:T(8,128)(2,1)S(1)}, bf16[3,256,512]{2,1,0:T(8,128)(2,1)}, u32[]{:S(2)}, u32[]{:S(2)}) collective-permute-start(bf16[3,256,512]{2,1,0:T(8,128)(2,1)S(1)} %copy-done.10), channel_id=1, source_target_pairs={{0,8},{16,0},{24,16},{8,24},{1,9},{17,1},{25,17},{9,25},{2,10},{18... | collective-permute-start | bytes 2359304 | tf_op jit(solution)/shard_map/ppermute | solution.py:664
  213.1 32.4 %collective-permute-start.11 = (bf16[3,256,512]{2,1,0:T(8,128)(2,1)}, bf16[3,256,512]{2,1,0:T(8,128)(2,1)}, u32[]{:S(2)}, u32[]{:S(2)}) collective-permute-start(bf16[3,256,512]{2,1,0:T(8,128)(2,1)} %collective-permute-done.6.refs_4_), channel_id=1, source_target_pairs={{0,16},{16,24},{24,8},{8,0},{1,17},{17,25},{25,9},{9,1},{2,18},{18... | collective-permute-start | bytes 2359304 | tf_op jit(solution)/shard_map/ppermute | solution.py:664
  215.2 31.9 %collective-permute-start.12 = (bf16[3,256,512]{2,1,0:T(8,128)(2,1)}, bf16[3,256,512]{2,1,0:T(8,128)(2,1)}, u32[]{:S(2)}, u32[]{:S(2)}) collective-permute-start(bf16[3,256,512]{2,1,0:T(8,128)(2,1)} %collective-permute-done.9.refs_7_), channel_id=1, source_target_pairs={{0,8},{16,0},{24,16},{8,24},{1,9},{17,1},{25,17},{9,25},{2,10},{18... | collective-permute-start | bytes 2359304 | tf_op jit(solution)/shard_map/ppermute | solution.py:664
  265.0 27.1 %all-to-all-start.3 = ((bf16[4,4,128,512]{3,2,1,0:T(8,128)(2,1)}), bf16[4,4,128,512]{3,2,1,0:T(8,128)(2,1)S(1)}, u32[]{:S(2)}, u32[]{:S(2)}) async-start(bf16[4,4,128,512]{3,2,1,0:T(8,128)(2,1)} %shard_map.179), calls=%async_computation.4 | async-start | bytes 4194304 | tf_op jit(solution)/shard_map/all_to_all | solution.py:647
  292.9 12.3 %collective-permute-start.13 = (bf16[3,128,512]{2,1,0:T(8,128)(2,1)S(1)}, bf16[3,128,512]{2,1,0:T(8,128)(2,1)S(1)}, u32[]{:S(2)}, u32[]{:S(2)}) collective-permute-start(bf16[3,128,512]{2,1,0:T(8,128)(2,1)S(1)} %get-tuple-element.111.refs_0_.refs_2_), channel_id=1, source_target_pairs={{0,16},{16,24},{24,8},{8,0},{1,17},{17,25},{25,9},{9,1},{2,18},{18... | collective-permute-start | bytes 1179656 | tf_op jit(solution)/shard_map/ppermute | solution.py:664
  293.6 11.7 %collective-permute-start.14 = (bf16[3,128,512]{2,1,0:T(8,128)(2,1)S(1)}, bf16[3,128,512]{2,1,0:T(8,128)(2,1)S(1)}, u32[]{:S(2)}, u32[]{:S(2)}) collective-permute-start(bf16[3,128,512]{2,1,0:T(8,128)(2,1)S(1)} %get-tuple-element.111.refs_0_.refs_2_), channel_id=1, source_target_pairs={{0,8},{16,0},{24,16},{8,24},{1,9},{17,1},{25,17},{9,25},{2,10},{18... | collective-permute-start | bytes 1179656 | tf_op jit(solution)/shard_map/ppermute | solution.py:664
  306.8 12.9 %collective-permute-start.20 = (bf16[3,64,512]{2,1,0:T(8,128)(2,1)S(1)}, bf16[3,64,512]{2,1,0:T(8,128)(2,1)S(1)}, u32[]{:S(2)}, u32[]{:S(2)}) collective-permute-start(bf16[3,64,512]{2,1,0:T(8,128)(2,1)S(1)} %slice.180), channel_id=1, source_target_pairs={{0,16},{16,24},{24,8},{8,0},{1,17},{17,25},{25,9},{9,1},{2,18},{18... | collective-permute-start | bytes 589832 | tf_op jit(solution)/shard_map/ppermute | solution.py:664
  307.6 12.2 %collective-permute-start.21 = (bf16[3,64,512]{2,1,0:T(8,128)(2,1)S(1)}, bf16[3,64,512]{2,1,0:T(8,128)(2,1)S(1)}, u32[]{:S(2)}, u32[]{:S(2)}) collective-permute-start(bf16[3,64,512]{2,1,0:T(8,128)(2,1)S(1)} %slice.181), channel_id=1, source_target_pairs={{0,8},{16,0},{24,16},{8,24},{1,9},{17,1},{25,17},{9,25},{2,10},{18... | collective-permute-start | bytes 589832 | tf_op jit(solution)/shard_map/ppermute | solution.py:664
  315.7 7.7 %collective-permute-start.17 = (bf16[144,512]{1,0:T(8,128)(2,1)S(1)}, bf16[144,512]{1,0:T(8,128)(2,1)S(1)}, u32[]{:S(2)}, u32[]{:S(2)}) collective-permute-start(bf16[144,512]{1,0:T(8,128)(2,1)S(1)} %pad_maximum_fusion.1), channel_id=1, source_target_pairs={{0,2},{1,3},{2,4},{3,5},{4,6},{5,7},{6,0},{7,1},{8,10},{9,11},{10,... | collective-permute-start | bytes 442376 | tf_op jit(solution)/shard_map/ppermute | solution.py:696
  316.9 8.0 %collective-permute-start.19 = (bf16[144,512]{1,0:T(8,128)(2,1)S(1)}, bf16[144,512]{1,0:T(8,128)(2,1)S(1)}, u32[]{:S(2)}, u32[]{:S(2)}) collective-permute-start(bf16[144,512]{1,0:T(8,128)(2,1)S(1)} %pad_maximum_fusion.2), channel_id=1, source_target_pairs={{0,6},{1,7},{2,0},{3,1},{4,2},{5,3},{6,4},{7,5},{8,14},{9,15},{10,... | collective-permute-start | bytes 442376 | tf_op jit(solution)/shard_map/ppermute | solution.py:696
  327.0 15.1 %all-to-all-start.4 = ((bf16[4,144,512]{2,1,0:T(8,128)(2,1)}), bf16[4,144,512]{2,1,0:T(8,128)(2,1)S(1)}, u32[]{:S(2)}, u32[]{:S(2)}) async-start(bf16[4,144,512]{2,1,0:T(8,128)(2,1)} %broadcast_in_dim.81), calls=%async_computation.5 | async-start | bytes 1179648 | tf_op jit(solution)/shard_map/all_to_all | solution.py:647
  (37 other events, 398.3 us)
Sparse Core Ops, SparseCore 0:
  10.5 25.3 all-gather.5
  78.1 48.3 all-gather.7
  191.6 49.5 reduce-scatter.1

commit v4 on v3

--- a/solution.py
+++ b/solution.py
@@ -19,7 +19,7 @@
     return -(-value // multiple) * multiple
 
 
-def call(kernel, grid, in_specs, out_specs, out_shape, scratch, flops, moved, prefetch=0, mib=54):
+def call(kernel, grid, in_specs, out_specs, out_shape, scratch, flops, moved, prefetch=0):
     return pl.pallas_call(
         kernel,
         grid_spec=pltpu.PrefetchScalarGridSpec(
@@ -30,7 +30,7 @@
             scratch_shapes=scratch,
         ),
         out_shape=out_shape,
-        compiler_params=pltpu.CompilerParams(vmem_limit_bytes=mib * 2**20),
+        compiler_params=pltpu.CompilerParams(vmem_limit_bytes=54 * 2**20),
         cost_estimate=pl.CostEstimate(flops=flops, bytes_accessed=moved, transcendentals=0),
     )
 
@@ -100,9 +100,9 @@
     )(chunks, gains, weights)
 
 
-def back_kernel(parts, order_ref, *refs):
+def back_kernel(parts, apart, order_ref, *refs):
     g_refs, w_refs = refs[:parts], refs[parts : parts + 2]
-    extra_ref, o_ref, grads = refs[parts + 2 :]
+    extra_ref, *o_refs, grads = refs[parts + 2 :]
     rows, columns = grads.shape[0], grads.shape[1] // 3
 
     @pl.when(pl.program_id(0) == 0)
@@ -115,25 +115,26 @@
             first += more
 
     for piece, w_ref in enumerate(w_refs):
+        o_ref, at = (o_refs[piece], 0) if apart else (o_refs[0], piece)
         weights = jnp.concatenate([w_ref[j] for j in range(3)], axis=1)
-        o_ref[piece, :rows, :] = lax.dot_general(
+        o_ref[at, :rows, :] = lax.dot_general(
             grads[...], weights, (((1,), (1,)), ((), ())), preferred_element_type=f32
         ).astype(bf16)
         if o_ref.shape[1] > rows:
-            o_ref[piece, rows:, :] = extra_ref[...]
-
-
-def project_back(parts, weights, order, extra=None):
+            o_ref[at, rows:, :] = extra_ref[...]
+
+
+def project_back(parts, weights, order, extra, apart):
     columns = parts[0].shape[2]
     rows = sum(part.shape[1] for part in parts)
     features = weights.shape[1]
     count = order.shape[0]
     width = features // count
-    more = 0 if extra is None else extra.shape[0]
-    if extra is None:
-        extra = jnp.zeros((EDGE, width), bf16)
+    high = rows + (extra.shape[0] if apart else 0)
+    each = 1 if apart else 2
+    out = jax.ShapeDtypeStruct((count * each // 2, high, width), bf16)
     return call(
-        functools.partial(back_kernel, len(parts)),
+        functools.partial(back_kernel, len(parts), apart),
         (count // 2,),
         [whole(part.shape) for part in parts]
         + [
@@ -141,8 +142,8 @@
             pl.BlockSpec((3, width, columns), lambda i, order: (0, order[2 * i + 1], 0)),
             whole(extra.shape),
         ],
-        pl.BlockSpec((2, rows + more, width), lambda i, *_: (i, 0, 0)),
-        jax.ShapeDtypeStruct((count, rows + more, width), bf16),
+        [pl.BlockSpec((each, high, width), lambda i, *_: (i, 0, 0))] * (2 // each),
+        [out] * (2 // each),
         [pltpu.VMEM((rows, 3 * columns), bf16)],
         6 * rows * features * columns,
         6 * features * columns + 2 * rows * features,
@@ -268,8 +269,8 @@
     front, rows, places, token_ref, e_ref, short_ref, medium_ref, *refs,
 ):
     p_refs = refs[: len(places)]
-    middle_ref, filtered_ref = refs[len(places) : len(places) + 2]
-    onehot, table, projected, gated, taps, kept, *mixed = refs[len(places) + 2 :]
+    refs = refs[len(places) :]
+    middle_ref, filtered_ref, onehot, table, projected, gated, taps, kept, *mixed = refs
     window, vocab = onehot.shape
 
     @pl.when(pl.program_id(0) == 0)
@@ -304,7 +305,8 @@
     tables = [table for _, _, table in tables]
     extended = rows + 2 * EDGE
     window = front + rows + EDGE
-    vocab, columns = embedding.shape
+    vocab = embedding.shape[0]
+    columns = embedding.shape[1]
     shapes = [
         jax.ShapeDtypeStruct((extended, columns), bf16),
         jax.ShapeDtypeStruct((rows + EDGE, columns), f32),
@@ -405,7 +407,8 @@
 
 
 def first_backward(tokens, above, halo, features, filtered, short, medium, vocab, parts):
-    rows, columns = above.shape
+    rows = above.shape[0]
+    columns = above.shape[1]
     later = rows + halo.shape[0]
     operands = (above, halo, features, filtered, short, medium)
     shape = jax.ShapeDtypeStruct((parts, 4, vocab // parts, columns), bf16)
@@ -438,20 +441,19 @@
     return terms[0]
 
 
-def scan_modes(source, decays, states, length, forward, residues=None, target=None):
+def scan_modes(source, decays, states, length, forward, residues, target):
     first = 0 if forward else SHIFT
 
     def step(i, held):
         position = first + (i if forward else length - 1 - i)
         value = source[pl.ds(position, SEGMENTS, stride=length), :]
         held = tuple(d * s + value for d, s in zip(decays, held))
-        if target is not None:
-            target[pl.ds(position, SEGMENTS, stride=length), :] = summed(
-                [r * s for r, s in zip(residues, held)]
-            )
+        target[pl.ds(position, SEGMENTS, stride=length), :] = summed(
+            [r * s for r, s in zip(residues, held)]
+        )
         return held
 
-    return lax.fori_loop(0, length, step, tuple(states), unroll=4)
+    return lax.fori_loop(0, length, step, tuple(states), unroll=8)
 
 
 def spread(ref, count):
@@ -459,7 +461,7 @@
 
 
 def second_features_kernel(
-    p_ref, short_ref, above_ref, rate_ref,
+    shards, p_ref, short_ref, above_ref, rate_ref,
     feature_ref, gated_ref, signal_ref, segment_ref, closing_ref, projected, gated, signal, decay,
 ):
     extended = above_ref.shape[0]
@@ -481,20 +483,32 @@
     gated[...] = rounded.astype(f32)
     rates = rate_ref[...]
     decay[...] = jnp.exp(-rates)
-    zeros = [jnp.zeros((SEGMENTS, LANES), f32)] * modes
-    for way, source in enumerate((gated, signal)):
-        ends = scan_modes(source, spread(decay, modes), zeros, length, way == 0)
+    decays = spread(decay, modes)
+
+    def step(i, held):
+        ahead = gated[pl.ds(i, SEGMENTS, stride=length), :]
+        back = signal[pl.ds(SHIFT + length - 1 - i, SEGMENTS, stride=length), :]
+        return tuple(
+            d * s + value
+            for values, value in zip((held[:modes], held[modes:]), (ahead, back))
+            for d, s in zip(decays, values)
+        )
+
+    zeros = (jnp.zeros((SEGMENTS, LANES), f32),) * (2 * modes)
+    ends = lax.fori_loop(0, length, step, zeros, unroll=8)
+    for way in range(2):
         for m in range(modes):
-            segment_ref[way, pl.ds(m, SEGMENTS, stride=modes), :] = ends[m]
+            segment_ref[way, pl.ds(m, SEGMENTS, stride=modes), :] = ends[way * modes + m]
         stride = jnp.exp(-rates * length)
         total = jnp.zeros((modes, LANES), f32)
         for n in range(SEGMENTS):
             at = n if way == 0 else SEGMENTS - 1 - n
             total = stride * total + segment_ref[way, at * modes : (at + 1) * modes, :]
-        closing_ref[way] = total
-
-
-def second_features(projected, short, above, rates):
+        for shard in range(shards):
+            closing_ref[shard, way] = total
+
+
+def second_features(projected, short, above, rates, shards):
     extended, columns = above.shape
     modes = rates.shape[0]
     shapes = [
@@ -502,10 +516,10 @@
         jax.ShapeDtypeStruct((extended, columns), bf16),
         jax.ShapeDtypeStruct((extended, columns), bf16),
         jax.ShapeDtypeStruct((2, SEGMENTS * modes, columns), f32),
-        jax.ShapeDtypeStruct((2, modes, columns), f32),
+        jax.ShapeDtypeStruct((shards, 2, modes, columns), f32),
     ]
     return call(
-        second_features_kernel,
+        functools.partial(second_features_kernel, shards),
         (columns // LANES,),
         [lanes(a.shape) for a in (projected, short, above, rates)],
         [lanes(s.shape) for s in shapes],
@@ -704,17 +718,17 @@
     devices = lax.axis_size("ch")
     me = lax.axis_index("ch")
     places = jnp.arange(devices // 2, dtype=jnp.int32)
-    return jnp.concatenate([(2 * places + other) % devices for other in (me, me ^ 1)])
+    return jnp.stack([(2 * places + other) % devices for other in (me, me ^ 1)], axis=1).reshape(-1)
 
 
 def added(*terms):
     return functools.reduce(lambda a, b: a + b, [t.astype(f32) for t in terms])
 
 
-def ring_scatter(pieces, near, far):
-    half = pieces.shape[0] // 2
-    pieces, *near = tie(pieces, *near)
-    mine = added(pieces[:half], sibling(pieces[half:])).astype(bf16)
+def ring_scatter(pieces, other_pieces, near, far):
+    half = pieces.shape[0]
+    other_pieces, *near = tie(other_pieces, *near)
+    mine = added(pieces, sibling(other_pieces)).astype(bf16)
     if half == 1:
         return mine[0].astype(f32), near, far
     steps = (half - 1) // 2
@@ -803,15 +817,26 @@
 
     middles = gather_ch(middle)
     block = exchange_seq(gathered[:, :share, :].reshape(shards, each, share, width))
-    block, features_first, middles = tie(block, features_first, middles)
+    blocks = [block[:, i] for i in range(each)]
+    block_gains = [
+        jnp.swapaxes(lax.dynamic_slice_in_dim(g, seq * each, each, 0), 1, 2)
+        for g in (gains_first, gains_second)
+    ]
     core = lax.axis_index("ch") % each
+    places = jnp.stack([core, 1 - core]).astype(jnp.int32)
+    straight, scattered = jnp.arange(pieces, dtype=jnp.int32), scatter_order()
+    blank = jnp.zeros((EDGE, width), bf16)
+    features_first, places, straight, scattered, blank, middles, *rest = tie(
+        features_first, places, straight, scattered, blank, middles, *blocks, *block_gains
+    )
+    blocks, block_gains = rest[:each], rest[each:]
     own = middles.reshape(shards, each, rows + 2 * EDGE, width)
     own = lax.dynamic_slice(own, (0, core, EDGE, 0), (shards, 1, rows, width))
     projected, scale = project(middles, gathered, share, 1, w_second, rows + 2 * EDGE)
     features_second, gated, signal, segments, closing = second_features(
-        projected, s_second, cotangents, decay_rates
-    )
-    own, closings = tie(own[:, 0], gather_seq(closing))
+        projected, s_second, cotangents, decay_rates, shards
+    )
+    own, closings = tie(own[:, 0], exchange_seq(closing))
     columns = exchange_seq(own)
     output, *grads, terms = second_filter(
         seq[None], features_second, gated, signal, segments, closings,
@@ -819,7 +844,7 @@
     )
     scale = scale[EDGE : EDGE + rows]
     pieces_of = ring_gather(grads)
-    partial = project_back(grads, w_second, jnp.arange(pieces, dtype=jnp.int32))
+    (partial,) = project_back(grads, w_second, straight, blank, False)
     partial, columns = tie(partial, columns)
     other = sibling(columns)
     partial_sum = scatter_ch(partial)
@@ -839,13 +864,12 @@
     halo, far_up, far_down = tie(halo, pieces_of[-2][2], pieces_of[-1][2])
     pieces_of[-2:] = [pieces_of[-2][:2] + (far_up,), pieces_of[-1][:2] + (far_down,)]
     sums = first_backward(
-        token_ids[None], grad_middle, halo, features_first, filtered_first, s_first, medium, vocab, shards
+        token_ids[None], grad_middle, halo, features_first, filtered_first, s_first, medium, vocab,
+        shards,
     )
     sums = exchange_seq(sums)
-    block_gains = lax.dynamic_slice_in_dim(gains_second, seq * each, each, 0)
-    places = jnp.stack([core, 1 - core]).astype(jnp.int32)
     grad_weights_second = weight_grad(
-        [columns, other], places, pieces_of, order, jnp.swapaxes(block_gains, 1, 2)
+        [columns, other], places, pieces_of, order, block_gains[1]
     )
     sums, grad_weights_second = tie(sums, grad_weights_second)
     own_sums = jnp.sum(sums.astype(f32), axis=0)
@@ -854,21 +878,14 @@
     all_grads = ring_gather([own_grads])
     extra_rows = -(-share // width)
     extra = jnp.pad(terms, (0, EDGE * width - share)).reshape(EDGE, width).astype(bf16)
-    partial = project_back([own_grads], w_first, scatter_order(), extra)
+    partial, other_partial = project_back([own_grads], w_first, scattered, extra, True)
     grad_normed, near, far = ring_scatter(
-        partial, [a for _, _, a in all_grads[1:-2]], [a for _, _, a in all_grads[-2:]]
+        partial, other_partial, [a for _, _, a in all_grads[1:-2]], [a for _, _, a in all_grads[-2:]]
     )
     all_grads[1:] = [old[:2] + (new,) for old, new in zip(all_grads[1:], near + far)]
     terms = grad_normed[share : share + extra_rows].reshape(-1)[:share]
     grad_normed = grad_normed[:share]
-    block_gains = lax.dynamic_slice_in_dim(gains_first, seq * each, each, 0)
-    grad_weights_first = weight_grad(
-        [block[:, i] for i in range(each)],
-        jnp.arange(each, dtype=jnp.int32),
-        all_grads,
-        order,
-        jnp.swapaxes(block_gains, 1, 2),
-    )
+    grad_weights_first = weight_grad(blocks, straight, all_grads, order, block_gains[0])
 
     as_float = own_embedding.astype(f32)
     grad_embedding = (

time: 352 us -> 347 us (0.986)
  local copies, waits for them, and re-layouts: 26.6 us -> 22.7 us
  transfers between devices with their start and end apart: 30 -> 30, of which waited for: 18 -> 18; matrix products, arithmetic and copies ran while one was open for 8% -> 7% of each run, Pallas kernels for 18% -> 19%
where the time goes in v4:
time: 347 us; the launch traced here: 346 us
  Pallas kernels  121 us (35%)
  waiting for transfers between devices  101 us (29%)
  starting transfers between devices  43.8 us (13%)
  blocking collectives  26 us (7%)
  local copies, waits for them, and re-layouts  22.7 us (7%)
  between operations  16.2 us (5%)
  other arithmetic  14.2 us (4%)
    ppermute x14, waiting for transfers between devices, seq_hop(): return lax.ppermute(value, 'seq', pairs)  34.9 us
    all_gather x2, waiting for transfers between devices, gather_ch(): return lax.all_gather(value, 'ch', axis=0, tiled=False)  30.3 us
    pallas_call x2, Pallas kernels, weight_grad(): call(functools.partial(weight_grad_kernel, [(slot, first) for slot, first...  22.2 us
    pallas_call x2, Pallas kernels, project_back(): call(functools.partial(back_kernel, len(parts), apart), (count // 2,), [w...  20.9 us
    pallas_call x2, Pallas kernels, project(): call(functools.partial(project_kernel, per_step, features, rows, gain_row...  19.7 us
    all_to_all x5, starting transfers between devices, exchange_seq(): return lax.all_to_all(value, 'seq', split_axis=0, concat_axis=0, tiled=True)  19.1 us
    all_to_all x5, waiting for transfers between devices, exchange_seq(): return lax.all_to_all(value, 'seq', split_axis=0, concat_axis=0, tiled=True)  15.1 us
    pallas_call x1, Pallas kernels, first_forward(): call(functools.partial(first_forward_kernel, front, rows, places), (colum...  14.9 us
  transfers between devices with their start and end apart: 30, of which 18 were waited for; matrix products, arithmetic and copies ran while one was open for 7% of the time, Pallas kernels for 19%

profile of v4, /device:TPU:0, one launch (start us, length us, event | category | flops | bytes accessed | tf_op | source)
XLA Modules:
  0.0 345.6 jit_solution(11733194161751124298)
XLA Ops:
  18.7 11.6 %all-gather.2 = s32[4,1,512]{2,1,0:T(1,128)S(1)} all-gather(s32[1,1,512]{2,1,0:T(1,128)} %bitcast.96), channel_id=1, replica_groups=mesh['seq'=4,'ch'=8] {'seq'}, dimensions={0}, use_global_device_ids=true | all-gather | bytes 10240 | tf_op jit(solution)/shard_map/all_gather | solution.py:799
  36.0 7.4 %shard_map.172 = (bf16[3,128,512]{2,1,0:T(8,128)(2,1)}, f32[128,1]{1,0:T(8,128)}) custom-call(bf16[8,144,512]{2,1,0:T(8,128)(2,1)} %bitcast.82, bf16[8,144,512]{2,1,0:T(8,128)(2,1)} %bitcast.83, bf16[3,4096,512]{2,1,0:T(8,128)(2,1)} %bitcast.76), custom_call_target="tpu_custom_call" | custom-call | flops 1610612736 | bytes 13631488 | tf_op jit(solution)/shard_map/pallas_call | solution.py:84
  45.6 9.2 %collective-permute-done.1.refs_1_ = bf16[3,128,512]{2,1,0:T(8,128)(2,1)S(1)} collective-permute-done((bf16[3,128,512]{2,1,0:T(8,128)(2,1)}, bf16[3,128,512]{2,1,0:T(8,128)(2,1)S(1)}, u32[]{:S(2)}, u32[]{:S(2)}) %collective-permute-start.1) | collective-permute-done | bytes 393248 | tf_op jit(solution)/shard_map/ppermute | solution.py:678
  63.0 14.9 %shard_map.173 = (bf16[544,512]{1,0:T(8,128)(2,1)}, f32[528,512]{1,0:T(8,128)}) custom-call(s32[688,1]{1,0:T(8,128)} %get-tuple-element.136.token_ref, bf16[512,512]{1,0:T(8,128)(2,1)} %bitcast_select_fusion.e_ref, f32[3,7,512]{2,1,0:T(8,128)} %bitcast.100, bf16[128,512]{1,0:T(8,128)(2,1)} %medium_ref.3, bf16[3,128,512]{2,1,0:T(8,128)(2,1)} %get-tuple-element.65.refs_0_, ...), custom_call_target="tpu_custom_call" | custom-call | flops 11928600576 | bytes 2818048 | tf_op jit(solution)/shard_map/pallas_call | solution.py:314
  84.1 7.2 %shard_map.174.feature_ref = f32[3,672,512]{2,1,0:T(8,128)} custom-call(s32[688,1]{1,0:T(8,128)} %get-tuple-element.67.token_ref, f32[3,7,512]{2,1,0:T(8,128)} %bitcast.101, bf16[3,128,512]{2,1,0:T(8,128)(2,1)} %get-tuple-element.65.refs_0_, bf16[3,128,512]{2,1,0:T(8,128)(2,1)} %copy-done.15, bf16[3,128,512]{2,1,0:T(8,128)(2,1)} %copy-done.16, ...), custom_call_target="tpu_custom_call" | custom-call | flops 3900178432 | bytes 5636096 | tf_op jit(solution)/shard_map/pallas_call | solution.py:358
  91.2 4.3 %all-to-all-done = bf16[4,2,128,512]{3,2,1,0:T(8,128)(2,1)S(1)} async-done(((bf16[4,2,128,512]{3,2,1,0:T(8,128)(2,1)}), bf16[4,2,128,512]{3,2,1,0:T(8,128)(2,1)S(1)}, u32[]{:S(2)}, u32[]{:S(2)}) %all-to-all-start) | async-done | bytes 1048608 | tf_op jit(solution)/shard_map/all_to_all | solution.py:661
  96.7 29.8 %all-gather.8.cloned.1.call-done = bf16[4352,512]{1,0:T(8,128)(2,1)} async-done(((bf16[544,512]{1,0:T(8,128)(2,1)}), bf16[4352,512]{1,0:T(8,128)(2,1)}) %all-gather.8.cloned.1.call-update) | async-done | bytes 4456464 | tf_op jit(solution)/shard_map/all_gather | solution.py:653
  127.0 12.3 %shard_map.175 = (bf16[3,544,512]{2,1,0:T(8,128)(2,1)}, f32[544,1]{1,0:T(8,128)}) custom-call(bf16[8,544,512]{2,1,0:T(8,128)(2,1)} %bitcast.90, bf16[8,144,512]{2,1,0:T(8,128)(2,1)} %bitcast.84, bf16[3,4096,512]{2,1,0:T(8,128)(2,1)} %bitcast.79), custom_call_target="tpu_custom_call" | custom-call | flops 6845104128 | bytes 17039360 | tf_op jit(solution)/shard_map/pallas_call | solution.py:84
  139.2 8.7 %shard_map.176 = (f32[3,528,512]{2,1,0:T(8,128)}, bf16[528,512]{1,0:T(8,128)(2,1)}, bf16[528,512]{1,0:T(8,128)(2,1)}, f32[2,128,512]{2,1,0:T(8,128)}, f32[4,2,16,512]{3,2,1,0:T(8,128)}) custom-call(bf16[3,544,512]{2,1,0:T(8,128)(2,1)} %get-tuple-element.69.p_ref, f32[3,7,512]{2,1,0:T(8,128)} %bitcast.98, bf16[528,512]{1,0:T(8,128)(2,1)} %pad_maximum_fusion.above_ref, ...), custom_call_target="tpu_custom_call" | custom-call | flops 5190451200 | bytes 6488064 | tf_op jit(solution)/shard_map/pallas_call | solution.py:521
  147.9 3.7 %all-to-all-start.1 = ((f32[4,2,16,512]{3,2,1,0:T(8,128)}), f32[4,2,16,512]{3,2,1,0:T(8,128)S(1)}, u32[]{:S(2)}, u32[]{:S(2)}) async-start(f32[4,2,16,512]{3,2,1,0:T(8,128)} %get-tuple-element.75), calls=%async_computation.1 | async-start | bytes 524288 | tf_op jit(solution)/shard_map/all_to_all | solution.py:661
  158.1 4.4 %all-to-all-start.2 = ((bf16[4,512,512]{2,1,0:T(8,128)(2,1)}), bf16[4,512,512]{2,1,0:T(8,128)(2,1)}, u32[]{:S(2)}, u32[]{:S(2)}) async-start(bf16[4,512,512]{2,1,0:T(8,128)(2,1)} %dynamic-slice_bitcast_fusion), calls=%async_computation.2 | async-start | bytes 4194304 | tf_op jit(solution)/shard_map/all_to_all | solution.py:661
  162.6 14.0 %shard_map.177 = (bf16[512,512]{1,0:T(8,128)(2,1)}, bf16[3,256,512]{2,1,0:T(8,128)(2,1)}, bf16[3,256,512]{2,1,0:T(8,128)(2,1)}, f32[512,1]{1,0:T(8,128)}) custom-call(s32[1]{0:T(128)} %bitcast.seq_ref, f32[3,528,512]{2,1,0:T(8,128)} %get-tuple-element.71.feature_ref, bf16[528,512]{1,0:T(8,128)(2,1)} %get-tuple-element.72.gated_ref, ...), custom_call_target="tpu_custom_call" | custom-call | flops 10485760000 | bytes 10485760 | tf_op jit(solution)/shard_map/pallas_call | solution.py:630
  177.2 12.0 %shard_map.178 = bf16[8,512,512]{2,1,0:T(8,128)(2,1)} custom-call(s32[8]{0:T(128)} %iota.19.order_ref.piece_ref, bf16[3,256,512]{2,1,0:T(8,128)(2,1)} %get-tuple-element.80.refs_0_.refs_2_, bf16[3,256,512]{2,1,0:T(8,128)(2,1)} %get-tuple-element.81.refs_1_.refs_3_, bf16[3,4096,512]{2,1,0:T(8,128)(2,1)} %bitcast.80, bf16[3,4096,512]{2,1,0:T(8,128)(2,1)} %bitcast.81, ...), custom_call_target="tpu_custom_call" | custom-call | flops 6442450944 | bytes 16777216 | tf_op jit(solution)/shard_map/pallas_call | solution.py:136
  194.5 16.4 %collective-permute-done.6.refs_4_ = bf16[3,256,512]{2,1,0:T(8,128)(2,1)} collective-permute-done((bf16[3,256,512]{2,1,0:T(8,128)(2,1)S(1)}, bf16[3,256,512]{2,1,0:T(8,128)(2,1)}, u32[]{:S(2)}, u32[]{:S(2)}) %collective-permute-start.6) | collective-permute-done | bytes 786464 | tf_op jit(solution)/shard_map/ppermute | solution.py:678
  213.3 14.4 %psum.7 = f32[512]{0:T(512)S(1)} all-reduce(f32[512]{0:T(512)S(1)} %reduce.21), channel_id=1, replica_groups=mesh['seq'=4,'ch'=8] {'ch'}, use_global_device_ids=true, to_apply=%region_3.4 | all-reduce | flops 512 | bytes 4096 | tf_op jit(solution)/shard_map/psum | solution.py:851
  229.7 9.3 %reduce-scatter.2.cloned.1.call-done = bf16[1,512,512]{2,1,0:T(8,128)(2,1)} async-done(((bf16[8,512,512]{2,1,0:T(8,128)(2,1)}), bf16[1,512,512]{2,1,0:T(8,128)(2,1)}) %reduce-scatter.2.cloned.1.call-update) | async-done | bytes 524304 | tf_op jit(solution)/shard_map/reduce_scatter | solution.py:657
  248.4 13.9 %shard_map.179 = bf16[4,4,128,512]{3,2,1,0:T(8,128)(2,1)} custom-call(s32[1,512]{1,0:T(1,128)} %bitcast.97, bf16[512,512]{1,0:T(8,128)(2,1)} %copy-done.4, bf16[160,512]{1,0:T(8,128)(2,1)} %copy-done.25, f32[3,672,512]{2,1,0:T(8,128)} %shard_map.174.feature_ref, f32[528,512]{1,0:T(8,128)} %get-tuple-element.90.filtered_ref, f32[3,7,512]{2,1,0:T(8,128)} %bitcast.102, ...), custom_call_target="tpu_custom_call" | custom-call | flops 11559501824 | bytes 5505024 | tf_op jit(solution)/shard_map/pallas_call | solution.py:415
  262.3 3.8 %all-to-all-start.3 = ((bf16[4,4,128,512]{3,2,1,0:T(8,128)(2,1)}), bf16[4,4,128,512]{3,2,1,0:T(8,128)(2,1)S(1)}, u32[]{:S(2)}, u32[]{:S(2)}) async-start(bf16[4,4,128,512]{3,2,1,0:T(8,128)(2,1)} %shard_map.179), calls=%async_computation.4 | async-start | bytes 4194304 | tf_op jit(solution)/shard_map/all_to_all | solution.py:661
  268.4 13.4 %shard_map.180 = f32[3,1024,512]{2,1,0:T(8,128)} custom-call(s32[4]{0:T(128)} %dynamic_slice.18.order_ref, s32[2]{0:T(128)} %pad_add_fusion.1.piece_ref, f32[2,512,1]{2,1,0:T(8,128)} %copy.31.gain_ref, bf16[4,512,512]{2,1,0:T(8,128)(2,1)} %all-to-all-done.2.refs_0_, bf16[4,512,512]{2,1,0:T(8,128)(2,1)} %collective-permute-done.5.refs_1_, ...), custom_call_target="tpu_custom_call" | custom-call | flops 6442450944 | bytes 16777216 | tf_op jit(solution)/shard_map/pallas_call | solution.py:177
  281.8 8.0 %all-to-all-done.3 = bf16[4,4,128,512]{3,2,1,0:T(8,128)(2,1)S(1)} async-done(((bf16[4,4,128,512]{3,2,1,0:T(8,128)(2,1)}), bf16[4,4,128,512]{3,2,1,0:T(8,128)(2,1)S(1)}, u32[]{:S(2)}, u32[]{:S(2)}) %all-to-all-start.3) | async-done | bytes 2097184 | tf_op jit(solution)/shard_map/all_to_all | solution.py:661
  293.1 8.9 %shard_map.181 = (bf16[4,144,512]{2,1,0:T(8,128)(2,1)}, bf16[4,144,512]{2,1,0:T(8,128)(2,1)}) custom-call(s32[8]{0:T(128)} %reshape.173.order_ref, bf16[3,128,512]{2,1,0:T(8,128)(2,1)} %copy-done.1, bf16[3,4096,512]{2,1,0:T(8,128)(2,1)} %bitcast.77, bf16[3,4096,512]{2,1,0:T(8,128)(2,1)} %bitcast.78, bf16[16,512]{1,0:T(8,128)(2,1)} %convert_element_type.105.refs_3_), custom_call_target="tpu_custom_call" | custom-call | flops 1610612736 | bytes 13631488 | tf_op jit(solution)/shard_map/pallas_call | solution.py:136
  316.4 3.7 %collective-permute-done.17 = bf16[144,512]{1,0:T(8,128)(2,1)S(1)} collective-permute-done((bf16[144,512]{1,0:T(8,128)(2,1)S(1)}, bf16[144,512]{1,0:T(8,128)(2,1)S(1)}, u32[]{:S(2)}, u32[]{:S(2)}) %collective-permute-start.17) | collective-permute-done | bytes 147488 | tf_op jit(solution)/shard_map/ppermute | solution.py:710
  323.7 3.7 %all-to-all-start.4 = ((bf16[4,144,512]{2,1,0:T(8,128)(2,1)}), bf16[4,144,512]{2,1,0:T(8,128)(2,1)S(1)}, u32[]{:S(2)}, u32[]{:S(2)}) async-start(bf16[4,144,512]{2,1,0:T(8,128)(2,1)} %broadcast_in_dim.74), calls=%async_computation.5 | async-start | bytes 1179648 | tf_op jit(solution)/shard_map/all_to_all | solution.py:661
  328.4 8.8 %shard_map.182 = f32[3,1024,512]{2,1,0:T(8,128)} custom-call(s32[4]{0:T(128)} %dynamic_slice.18.order_ref, s32[8]{0:T(128)} %iota.19.order_ref.piece_ref, f32[2,512,1]{2,1,0:T(8,128)} %copy.32.gain_ref, bf16[4,128,512]{2,1,0:T(8,128)(2,1)} %get-tuple-element.109.refs_0_, bf16[4,128,512]{2,1,0:T(8,128)(2,1)} %get-tuple-element.110.refs_1_, ...), custom_call_target="tpu_custom_call" | custom-call | flops 1610612736 | bytes 8912896 | tf_op jit(solution)/shard_map/pallas_call | solution.py:177
  (174 shorter events, 85.6 us)
Async XLA Ops:
  7.2 28.8 %all-gather.6.cloned.1.call-start = ((), (), s32[]{:S(2)}) async-start(), calls=%async_computation.7 | async-start | bytes 1327104 | tf_op jit(solution)/shard_map/all_gather | solution.py:653
  10.4 116.0 %all-gather.8.cloned.1.call-start = ((), (), s32[]{:S(2)}) async-start(), calls=%async_computation.8 | async-start | bytes 5013504 | tf_op jit(solution)/shard_map/all_gather | solution.py:653
  11.2 23.4 %collective-permute-start = (bf16[16,512]{1,0:T(8,128)(2,1)S(1)}, bf16[16,512]{1,0:T(8,128)(2,1)S(1)}, u32[]{:S(2)}, u32[]{:S(2)}) collective-permute-start(bf16[16,512]{1,0:T(8,128)(2,1)S(1)} %slice.118), channel_id=1, source_target_pairs={{8,0},{16,8},{24,16},{9,1},{17,9},{25,17},{10,2},{18,10},{26,18},{... | collective-permute-start | bytes 49160 | tf_op jit(solution)/shard_map/ppermute | solution.py:649
  43.4 11.5 %collective-permute-start.1 = (bf16[3,128,512]{2,1,0:T(8,128)(2,1)}, bf16[3,128,512]{2,1,0:T(8,128)(2,1)S(1)}, u32[]{:S(2)}, u32[]{:S(2)}) collective-permute-start(bf16[3,128,512]{2,1,0:T(8,128)(2,1)} %get-tuple-element.65.refs_0_), channel_id=1, source_target_pairs={{0,16},{16,24},{24,8},{8,0},{1,17},{17,25},{25,9},{9,1},{2,18},{18... | collective-permute-start | bytes 1179656 | tf_op jit(solution)/shard_map/ppermute | solution.py:678
  44.8 11.5 %collective-permute-start.2 = (bf16[3,128,512]{2,1,0:T(8,128)(2,1)}, bf16[3,128,512]{2,1,0:T(8,128)(2,1)S(1)}, u32[]{:S(2)}, u32[]{:S(2)}) collective-permute-start(bf16[3,128,512]{2,1,0:T(8,128)(2,1)} %get-tuple-element.65.refs_0_), channel_id=1, source_target_pairs={{0,8},{16,0},{24,16},{8,24},{1,9},{17,1},{25,17},{9,25},{2,10},{18... | collective-permute-start | bytes 1179656 | tf_op jit(solution)/shard_map/ppermute | solution.py:678
  79.8 15.8 %all-to-all-start = ((bf16[4,2,128,512]{3,2,1,0:T(8,128)(2,1)}), bf16[4,2,128,512]{3,2,1,0:T(8,128)(2,1)S(1)}, u32[]{:S(2)}, u32[]{:S(2)}) async-start(bf16[4,2,128,512]{3,2,1,0:T(8,128)(2,1)} %bitcast.16), calls=%async_computation | async-start | bytes 2097152 | tf_op jit(solution)/shard_map/all_to_all | solution.py:661
  147.9 9.4 %all-to-all-start.1 = ((f32[4,2,16,512]{3,2,1,0:T(8,128)}), f32[4,2,16,512]{3,2,1,0:T(8,128)S(1)}, u32[]{:S(2)}, u32[]{:S(2)}) async-start(f32[4,2,16,512]{3,2,1,0:T(8,128)} %get-tuple-element.75), calls=%async_computation.1 | async-start | bytes 524288 | tf_op jit(solution)/shard_map/all_to_all | solution.py:661
  158.1 31.1 %all-to-all-start.2 = ((bf16[4,512,512]{2,1,0:T(8,128)(2,1)}), bf16[4,512,512]{2,1,0:T(8,128)(2,1)}, u32[]{:S(2)}, u32[]{:S(2)}) async-start(bf16[4,512,512]{2,1,0:T(8,128)(2,1)} %dynamic-slice_bitcast_fusion), calls=%async_computation.2 | async-start | bytes 4194304 | tf_op jit(solution)/shard_map/all_to_all | solution.py:661
  162.5 76.4 %reduce-scatter.2.cloned.1.call-start = ((), (), s32[]{:S(2)}) async-start(), calls=%async_computation.6 | async-start | bytes 4718592 | tf_op jit(solution)/shard_map/reduce_scatter | solution.py:657
  189.2 40.4 %collective-permute-start.5 = (bf16[4,512,512]{2,1,0:T(8,128)(2,1)}, bf16[4,512,512]{2,1,0:T(8,128)(2,1)}, u32[]{:S(2)}, u32[]{:S(2)}) collective-permute-start(bf16[4,512,512]{2,1,0:T(8,128)(2,1)} %all-to-all-done.2.refs_0_), channel_id=1, source_target_pairs={{0,1},{1,0},{2,3},{3,2},{4,5},{5,4},{6,7},{7,6},{8,9},{9,8},{10,11... | collective-permute-start | bytes 6291464 | tf_op jit(solution)/shard_map/ppermute | solution.py:714
  190.3 20.6 %collective-permute-start.6 = (bf16[3,256,512]{2,1,0:T(8,128)(2,1)S(1)}, bf16[3,256,512]{2,1,0:T(8,128)(2,1)}, u32[]{:S(2)}, u32[]{:S(2)}) collective-permute-start(bf16[3,256,512]{2,1,0:T(8,128)(2,1)S(1)} %copy-done.7), channel_id=1, source_target_pairs={{0,16},{16,24},{24,8},{8,0},{1,17},{17,25},{25,9},{9,1},{2,18},{18... | collective-permute-start | bytes 2359304 | tf_op jit(solution)/shard_map/ppermute | solution.py:678
  192.2 20.6 %collective-permute-start.9 = (bf16[3,256,512]{2,1,0:T(8,128)(2,1)S(1)}, bf16[3,256,512]{2,1,0:T(8,128)(2,1)}, u32[]{:S(2)}, u32[]{:S(2)}) collective-permute-start(bf16[3,256,512]{2,1,0:T(8,128)(2,1)S(1)} %copy-done.8), channel_id=1, source_target_pairs={{0,8},{16,0},{24,16},{8,24},{1,9},{17,1},{25,17},{9,25},{2,10},{18... | collective-permute-start | bytes 2359304 | tf_op jit(solution)/shard_map/ppermute | solution.py:678
  192.4 35.3 %collective-permute-start.7 = (bf16[3,256,512]{2,1,0:T(8,128)(2,1)S(1)}, bf16[3,256,512]{2,1,0:T(8,128)(2,1)}, u32[]{:S(2)}, u32[]{:S(2)}) collective-permute-start(bf16[3,256,512]{2,1,0:T(8,128)(2,1)S(1)} %copy-done.8), channel_id=1, source_target_pairs={{0,16},{16,24},{24,8},{8,0},{1,17},{17,25},{25,9},{9,1},{2,18},{18... | collective-permute-start | bytes 2359304 | tf_op jit(solution)/shard_map/ppermute | solution.py:678
  194.2 35.4 %collective-permute-start.8 = (bf16[3,256,512]{2,1,0:T(8,128)(2,1)S(1)}, bf16[3,256,512]{2,1,0:T(8,128)(2,1)}, u32[]{:S(2)}, u32[]{:S(2)}) collective-permute-start(bf16[3,256,512]{2,1,0:T(8,128)(2,1)S(1)} %copy-done.7), channel_id=1, source_target_pairs={{0,8},{16,0},{24,16},{8,24},{1,9},{17,1},{25,17},{9,25},{2,10},{18... | collective-permute-start | bytes 2359304 | tf_op jit(solution)/shard_map/ppermute | solution.py:678
  210.9 32.8 %collective-permute-start.11 = (bf16[3,256,512]{2,1,0:T(8,128)(2,1)}, bf16[3,256,512]{2,1,0:T(8,128)(2,1)}, u32[]{:S(2)}, u32[]{:S(2)}) collective-permute-start(bf16[3,256,512]{2,1,0:T(8,128)(2,1)} %collective-permute-done.6.refs_4_), channel_id=1, source_target_pairs={{0,16},{16,24},{24,8},{8,0},{1,17},{17,25},{25,9},{9,1},{2,18},{18... | collective-permute-start | bytes 2359304 | tf_op jit(solution)/shard_map/ppermute | solution.py:678
  212.8 31.9 %collective-permute-start.12 = (bf16[3,256,512]{2,1,0:T(8,128)(2,1)}, bf16[3,256,512]{2,1,0:T(8,128)(2,1)}, u32[]{:S(2)}, u32[]{:S(2)}) collective-permute-start(bf16[3,256,512]{2,1,0:T(8,128)(2,1)} %collective-permute-done.9.refs_7_), channel_id=1, source_target_pairs={{0,8},{16,0},{24,16},{8,24},{1,9},{17,1},{25,17},{9,25},{2,10},{18... | collective-permute-start | bytes 2359304 | tf_op jit(solution)/shard_map/ppermute | solution.py:678
  262.3 27.6 %all-to-all-start.3 = ((bf16[4,4,128,512]{3,2,1,0:T(8,128)(2,1)}), bf16[4,4,128,512]{3,2,1,0:T(8,128)(2,1)S(1)}, u32[]{:S(2)}, u32[]{:S(2)}) async-start(bf16[4,4,128,512]{3,2,1,0:T(8,128)(2,1)} %shard_map.179), calls=%async_computation.4 | async-start | bytes 4194304 | tf_op jit(solution)/shard_map/all_to_all | solution.py:661
  290.4 11.6 %collective-permute-start.13 = (bf16[3,128,512]{2,1,0:T(8,128)(2,1)S(1)}, bf16[3,128,512]{2,1,0:T(8,128)(2,1)S(1)}, u32[]{:S(2)}, u32[]{:S(2)}) collective-permute-start(bf16[3,128,512]{2,1,0:T(8,128)(2,1)S(1)} %get-tuple-element.127.refs_0_.refs_2_), channel_id=1, source_target_pairs={{0,16},{16,24},{24,8},{8,0},{1,17},{17,25},{25,9},{9,1},{2,18},{18... | collective-permute-start | bytes 1179656 | tf_op jit(solution)/shard_map/ppermute | solution.py:678
  291.1 10.9 %collective-permute-start.14 = (bf16[3,128,512]{2,1,0:T(8,128)(2,1)S(1)}, bf16[3,128,512]{2,1,0:T(8,128)(2,1)S(1)}, u32[]{:S(2)}, u32[]{:S(2)}) collective-permute-start(bf16[3,128,512]{2,1,0:T(8,128)(2,1)S(1)} %get-tuple-element.127.refs_0_.refs_2_), channel_id=1, source_target_pairs={{0,8},{16,0},{24,16},{8,24},{1,9},{17,1},{25,17},{9,25},{2,10},{18... | collective-permute-start | bytes 1179656 | tf_op jit(solution)/shard_map/ppermute | solution.py:678
  302.1 14.3 %collective-permute-start.20 = (bf16[3,64,512]{2,1,0:T(8,128)(2,1)S(1)}, bf16[3,64,512]{2,1,0:T(8,128)(2,1)S(1)}, u32[]{:S(2)}, u32[]{:S(2)}) collective-permute-start(bf16[3,64,512]{2,1,0:T(8,128)(2,1)S(1)} %slice.174), channel_id=1, source_target_pairs={{0,16},{16,24},{24,8},{8,0},{1,17},{17,25},{25,9},{9,1},{2,18},{18... | collective-permute-start | bytes 589832 | tf_op jit(solution)/shard_map/ppermute | solution.py:678
  302.9 13.5 %collective-permute-start.21 = (bf16[3,64,512]{2,1,0:T(8,128)(2,1)S(1)}, bf16[3,64,512]{2,1,0:T(8,128)(2,1)S(1)}, u32[]{:S(2)}, u32[]{:S(2)}) collective-permute-start(bf16[3,64,512]{2,1,0:T(8,128)(2,1)S(1)} %slice.175), channel_id=1, source_target_pairs={{0,8},{16,0},{24,16},{8,24},{1,9},{17,1},{25,17},{9,25},{2,10},{18... | collective-permute-start | bytes 589832 | tf_op jit(solution)/shard_map/ppermute | solution.py:678
  312.4 7.7 %collective-permute-start.17 = (bf16[144,512]{1,0:T(8,128)(2,1)S(1)}, bf16[144,512]{1,0:T(8,128)(2,1)S(1)}, u32[]{:S(2)}, u32[]{:S(2)}) collective-permute-start(bf16[144,512]{1,0:T(8,128)(2,1)S(1)} %pad_maximum_fusion.1), channel_id=1, source_target_pairs={{0,2},{1,3},{2,4},{3,5},{4,6},{5,7},{6,0},{7,1},{8,10},{9,11},{10,... | collective-permute-start | bytes 442376 | tf_op jit(solution)/shard_map/ppermute | solution.py:710
  313.2 8.3 %collective-permute-start.19 = (bf16[144,512]{1,0:T(8,128)(2,1)S(1)}, bf16[144,512]{1,0:T(8,128)(2,1)S(1)}, u32[]{:S(2)}, u32[]{:S(2)}) collective-permute-start(bf16[144,512]{1,0:T(8,128)(2,1)S(1)} %pad_maximum_fusion.2), channel_id=1, source_target_pairs={{0,6},{1,7},{2,0},{3,1},{4,2},{5,3},{6,4},{7,5},{8,14},{9,15},{10,... | collective-permute-start | bytes 442376 | tf_op jit(solution)/shard_map/ppermute | solution.py:710
  323.7 13.5 %all-to-all-start.4 = ((bf16[4,144,512]{2,1,0:T(8,128)(2,1)}), bf16[4,144,512]{2,1,0:T(8,128)(2,1)S(1)}, u32[]{:S(2)}, u32[]{:S(2)}) async-start(bf16[4,144,512]{2,1,0:T(8,128)(2,1)} %broadcast_in_dim.74), calls=%async_computation.5 | async-start | bytes 1179648 | tf_op jit(solution)/shard_map/all_to_all | solution.py:661
  (32 other events, 340.9 us)
Sparse Core Ops, SparseCore 0:
  10.5 25.3 all-gather.5
  78.1 48.3 all-gather.7
  189.4 49.5 reduce-scatter.1

commit v5 on v4

--- a/solution.py
+++ b/solution.py
@@ -153,6 +153,7 @@
 
 def weight_grad_kernel(spans, pieces, order_ref, piece_ref, gain_ref, *refs):
     x_refs, g_refs, out_ref = refs[:pieces], refs[pieces:-1], refs[-1]
+    gain = jnp.broadcast_to(gain_ref[0], (8, gain_ref.shape[2])).T[:, :1]
 
     for piece, x_ref in enumerate(x_refs):
 
@@ -166,7 +167,7 @@
                         some, g_ref[j], (((0,), (0,)), ((), ())), preferred_element_type=f32
                     )
                     total = term if total is None else total + term
-                out_ref[j] = total * gain_ref[0]
+                out_ref[j] = total * gain
 
 
 def weight_grad(columns, places, grads, order, gains):
@@ -177,7 +178,7 @@
     return call(
         functools.partial(weight_grad_kernel, [(slot, first) for slot, first, _ in grads], pieces),
         (pieces,),
-        [pl.BlockSpec((1, width, 1), lambda i, order, places: (places[i], 0, 0))]
+        [pl.BlockSpec((1, 1, width), lambda i, order, places: (places[i], 0, 0))]
         + [whole(array.shape) for array in list(columns) + arrays],
         pl.BlockSpec((3, width, out), lambda i, order, places: (0, places[i], 0)),
         jax.ShapeDtypeStruct((3, pieces * width, out), f32),
@@ -791,9 +792,8 @@
     share = vocab // shards
     at = seq * share
 
-    gains = jnp.concatenate(
-        [gain_first[None], gain_second[None], jnp.zeros((EDGE - 2, width), bf16)], axis=0
-    )
+    row = lax.broadcasted_iota(jnp.int32, (EDGE, width), 0)
+    gains = jnp.where(row == 0, gain_first, jnp.where(row == 1, gain_second, jnp.zeros((), bf16)))
     own_embedding = lax.dynamic_slice_in_dim(embedding, at, share, 0)
     gathered = gather_ch(jnp.concatenate([own_embedding, gains], axis=0))
     tokens = lax.all_gather(token_ids, "seq", axis=0, tiled=True)
@@ -819,8 +819,7 @@
     block = exchange_seq(gathered[:, :share, :].reshape(shards, each, share, width))
     blocks = [block[:, i] for i in range(each)]
     block_gains = [
-        jnp.swapaxes(lax.dynamic_slice_in_dim(g, seq * each, each, 0), 1, 2)
-        for g in (gains_first, gains_second)
+        lax.dynamic_slice_in_dim(g, seq * each, each, 0) for g in (gains_first, gains_second)
     ]
     core = lax.axis_index("ch") % each
     places = jnp.stack([core, 1 - core]).astype(jnp.int32)

time: 347 us -> 346 us (level)
  local copies, waits for them, and re-layouts: 22.7 us -> 19.2 us
where the time goes in v5:
time: 346 us; the launch traced here: 344 us
  Pallas kernels  122 us (35%)
  waiting for transfers between devices  102 us (29%)
  starting transfers between devices  43.8 us (13%)
  blocking collectives  26 us (8%)
  local copies, waits for them, and re-layouts  19.2 us (6%)
  between operations  16.2 us (5%)
  other arithmetic  15.4 us (4%)
    ppermute x14, waiting for transfers between devices, seq_hop(): return lax.ppermute(value, 'seq', pairs)  34.8 us
    all_gather x2, waiting for transfers between devices, gather_ch(): return lax.all_gather(value, 'ch', axis=0, tiled=False)  30.2 us
    pallas_call x2, Pallas kernels, weight_grad(): call(functools.partial(weight_grad_kernel, [(slot, first) for slot, first...  22.8 us
    pallas_call x2, Pallas kernels, project_back(): call(functools.partial(back_kernel, len(parts), apart), (count // 2,), [w...  20.9 us
    pallas_call x2, Pallas kernels, project(): call(functools.partial(project_kernel, per_step, features, rows, gain_row...  19.7 us
    all_to_all x5, starting transfers between devices, exchange_seq(): return lax.all_to_all(value, 'seq', split_axis=0, concat_axis=0, tiled=True)  19.1 us
    all_to_all x5, waiting for transfers between devices, exchange_seq(): return lax.all_to_all(value, 'seq', split_axis=0, concat_axis=0, tiled=True)  15.8 us
    pallas_call x1, Pallas kernels, first_forward(): call(functools.partial(first_forward_kernel, front, rows, places), (colum...  14.9 us
  transfers between devices with their start and end apart: 30, of which 18 were waited for; matrix products, arithmetic and copies ran while one was open for 7% of the time, Pallas kernels for 19%

profile of v5, /device:TPU:0, one launch (start us, length us, event | category | flops | bytes accessed | tf_op | source)
XLA Modules:
  0.0 344.5 jit_solution(9548748342364232615)
XLA Ops:
  18.0 11.6 %all-gather.2 = s32[4,1,512]{2,1,0:T(1,128)S(1)} all-gather(s32[1,1,512]{2,1,0:T(1,128)} %bitcast.88), channel_id=1, replica_groups=mesh['seq'=4,'ch'=8] {'seq'}, dimensions={0}, use_global_device_ids=true | all-gather | bytes 10240 | tf_op jit(solution)/shard_map/all_gather | solution.py:799
  35.7 7.4 %shard_map.172 = (bf16[3,128,512]{2,1,0:T(8,128)(2,1)}, f32[128,1]{1,0:T(8,128)}) custom-call(bf16[8,144,512]{2,1,0:T(8,128)(2,1)} %bitcast.76, bf16[8,144,512]{2,1,0:T(8,128)(2,1)} %bitcast.77, bf16[3,4096,512]{2,1,0:T(8,128)(2,1)} %bitcast.70), custom_call_target="tpu_custom_call" | custom-call | flops 1610612736 | bytes 13631488 | tf_op jit(solution)/shard_map/pallas_call | solution.py:84
  45.3 9.2 %collective-permute-done.1.refs_1_ = bf16[3,128,512]{2,1,0:T(8,128)(2,1)S(1)} collective-permute-done((bf16[3,128,512]{2,1,0:T(8,128)(2,1)}, bf16[3,128,512]{2,1,0:T(8,128)(2,1)S(1)}, u32[]{:S(2)}, u32[]{:S(2)}) %collective-permute-start.1) | collective-permute-done | bytes 393248 | tf_op jit(solution)/shard_map/ppermute | solution.py:679
  62.7 14.9 %shard_map.173 = (bf16[544,512]{1,0:T(8,128)(2,1)}, f32[528,512]{1,0:T(8,128)}) custom-call(s32[688,1]{1,0:T(8,128)} %get-tuple-element.136.token_ref, bf16[512,512]{1,0:T(8,128)(2,1)} %bitcast_select_fusion.e_ref, f32[3,7,512]{2,1,0:T(8,128)} %bitcast.92, bf16[128,512]{1,0:T(8,128)(2,1)} %medium_ref.3, bf16[3,128,512]{2,1,0:T(8,128)(2,1)} %get-tuple-element.65.refs_0_, ...), custom_call_target="tpu_custom_call" | custom-call | flops 11928600576 | bytes 2818048 | tf_op jit(solution)/shard_map/pallas_call | solution.py:315
  84.9 7.2 %shard_map.174.feature_ref = f32[3,672,512]{2,1,0:T(8,128)} custom-call(s32[688,1]{1,0:T(8,128)} %get-tuple-element.67.token_ref, f32[3,7,512]{2,1,0:T(8,128)} %bitcast.93, bf16[3,128,512]{2,1,0:T(8,128)(2,1)} %get-tuple-element.65.refs_0_, bf16[3,128,512]{2,1,0:T(8,128)(2,1)} %copy-done.15, bf16[3,128,512]{2,1,0:T(8,128)(2,1)} %copy-done.16, ...), custom_call_target="tpu_custom_call" | custom-call | flops 3900178432 | bytes 5636096 | tf_op jit(solution)/shard_map/pallas_call | solution.py:359
  92.1 3.8 %all-to-all-done = bf16[4,2,128,512]{3,2,1,0:T(8,128)(2,1)S(1)} async-done(((bf16[4,2,128,512]{3,2,1,0:T(8,128)(2,1)}), bf16[4,2,128,512]{3,2,1,0:T(8,128)(2,1)S(1)}, u32[]{:S(2)}, u32[]{:S(2)}) %all-to-all-start) | async-done | bytes 1048608 | tf_op jit(solution)/shard_map/all_to_all | solution.py:662
  97.0 29.2 %all-gather.8.cloned.1.call-done = bf16[4352,512]{1,0:T(8,128)(2,1)} async-done(((bf16[544,512]{1,0:T(8,128)(2,1)}), bf16[4352,512]{1,0:T(8,128)(2,1)}) %all-gather.8.cloned.1.call-update) | async-done | bytes 4456464 | tf_op jit(solution)/shard_map/all_gather | solution.py:654
  126.7 12.3 %shard_map.175 = (bf16[3,544,512]{2,1,0:T(8,128)(2,1)}, f32[544,1]{1,0:T(8,128)}) custom-call(bf16[8,544,512]{2,1,0:T(8,128)(2,1)} %bitcast.84, bf16[8,144,512]{2,1,0:T(8,128)(2,1)} %bitcast.78, bf16[3,4096,512]{2,1,0:T(8,128)(2,1)} %bitcast.73), custom_call_target="tpu_custom_call" | custom-call | flops 6845104128 | bytes 17039360 | tf_op jit(solution)/shard_map/pallas_call | solution.py:84
  139.0 8.7 %shard_map.176 = (f32[3,528,512]{2,1,0:T(8,128)}, bf16[528,512]{1,0:T(8,128)(2,1)}, bf16[528,512]{1,0:T(8,128)(2,1)}, f32[2,128,512]{2,1,0:T(8,128)}, f32[4,2,16,512]{3,2,1,0:T(8,128)}) custom-call(bf16[3,544,512]{2,1,0:T(8,128)(2,1)} %get-tuple-element.69.p_ref, f32[3,7,512]{2,1,0:T(8,128)} %bitcast.90, bf16[528,512]{1,0:T(8,128)(2,1)} %pad_maximum_fusion.above_ref, ...), custom_call_target="tpu_custom_call" | custom-call | flops 5190451200 | bytes 6488064 | tf_op jit(solution)/shard_map/pallas_call | solution.py:522
  147.7 3.6 %all-to-all-start.1 = ((f32[4,2,16,512]{3,2,1,0:T(8,128)}), f32[4,2,16,512]{3,2,1,0:T(8,128)S(1)}, u32[]{:S(2)}, u32[]{:S(2)}) async-start(f32[4,2,16,512]{3,2,1,0:T(8,128)} %get-tuple-element.75), calls=%async_computation.1 | async-start | bytes 524288 | tf_op jit(solution)/shard_map/all_to_all | solution.py:662
  157.8 4.4 %all-to-all-start.2 = ((bf16[4,512,512]{2,1,0:T(8,128)(2,1)}), bf16[4,512,512]{2,1,0:T(8,128)(2,1)}, u32[]{:S(2)}, u32[]{:S(2)}) async-start(bf16[4,512,512]{2,1,0:T(8,128)(2,1)} %dynamic-slice_bitcast_fusion), calls=%async_computation.2 | async-start | bytes 4194304 | tf_op jit(solution)/shard_map/all_to_all | solution.py:662
  162.3 14.0 %shard_map.177 = (bf16[512,512]{1,0:T(8,128)(2,1)}, bf16[3,256,512]{2,1,0:T(8,128)(2,1)}, bf16[3,256,512]{2,1,0:T(8,128)(2,1)}, f32[512,1]{1,0:T(8,128)}) custom-call(s32[1]{0:T(128)} %bitcast.seq_ref, f32[3,528,512]{2,1,0:T(8,128)} %get-tuple-element.71.feature_ref, bf16[528,512]{1,0:T(8,128)(2,1)} %get-tuple-element.72.gated_ref, ...), custom_call_target="tpu_custom_call" | custom-call | flops 10485760000 | bytes 10485760 | tf_op jit(solution)/shard_map/pallas_call | solution.py:631
  176.9 12.0 %shard_map.178 = bf16[8,512,512]{2,1,0:T(8,128)(2,1)} custom-call(s32[8]{0:T(128)} %iota.33.order_ref.piece_ref, bf16[3,256,512]{2,1,0:T(8,128)(2,1)} %get-tuple-element.80.refs_0_.refs_2_, bf16[3,256,512]{2,1,0:T(8,128)(2,1)} %get-tuple-element.81.refs_1_.refs_3_, bf16[3,4096,512]{2,1,0:T(8,128)(2,1)} %bitcast.74, bf16[3,4096,512]{2,1,0:T(8,128)(2,1)} %bitcast.75, ...), custom_call_target="tpu_custom_call" | custom-call | flops 6442450944 | bytes 16777216 | tf_op jit(solution)/shard_map/pallas_call | solution.py:136
  194.2 16.4 %collective-permute-done.6.refs_4_ = bf16[3,256,512]{2,1,0:T(8,128)(2,1)} collective-permute-done((bf16[3,256,512]{2,1,0:T(8,128)(2,1)S(1)}, bf16[3,256,512]{2,1,0:T(8,128)(2,1)}, u32[]{:S(2)}, u32[]{:S(2)}) %collective-permute-start.6) | collective-permute-done | bytes 786464 | tf_op jit(solution)/shard_map/ppermute | solution.py:679
  213.0 14.5 %psum.7 = f32[512]{0:T(512)S(1)} all-reduce(f32[512]{0:T(512)S(1)} %reduce.21), channel_id=1, replica_groups=mesh['seq'=4,'ch'=8] {'ch'}, use_global_device_ids=true, to_apply=%region_3.4 | all-reduce | flops 512 | bytes 4096 | tf_op jit(solution)/shard_map/psum | solution.py:850
  229.4 9.3 %reduce-scatter.2.cloned.1.call-done = bf16[1,512,512]{2,1,0:T(8,128)(2,1)} async-done(((bf16[8,512,512]{2,1,0:T(8,128)(2,1)}), bf16[1,512,512]{2,1,0:T(8,128)(2,1)}) %reduce-scatter.2.cloned.1.call-update) | async-done | bytes 524304 | tf_op jit(solution)/shard_map/reduce_scatter | solution.py:658
  248.1 13.9 %shard_map.179 = bf16[4,4,128,512]{3,2,1,0:T(8,128)(2,1)} custom-call(s32[1,512]{1,0:T(1,128)} %bitcast.89, bf16[512,512]{1,0:T(8,128)(2,1)} %copy-done.4, bf16[160,512]{1,0:T(8,128)(2,1)} %copy-done.23, f32[3,672,512]{2,1,0:T(8,128)} %shard_map.174.feature_ref, f32[528,512]{1,0:T(8,128)} %get-tuple-element.90.filtered_ref, f32[3,7,512]{2,1,0:T(8,128)} %bitcast.94, ...), custom_call_target="tpu_custom_call" | custom-call | flops 11559501824 | bytes 5505024 | tf_op jit(solution)/shard_map/pallas_call | solution.py:416
  262.0 3.8 %all-to-all-start.3 = ((bf16[4,4,128,512]{3,2,1,0:T(8,128)(2,1)}), bf16[4,4,128,512]{3,2,1,0:T(8,128)(2,1)S(1)}, u32[]{:S(2)}, u32[]{:S(2)}) async-start(bf16[4,4,128,512]{3,2,1,0:T(8,128)(2,1)} %shard_map.179), calls=%async_computation.4 | async-start | bytes 4194304 | tf_op jit(solution)/shard_map/all_to_all | solution.py:662
  266.5 13.8 %shard_map.180 = f32[3,1024,512]{2,1,0:T(8,128)} custom-call(s32[4]{0:T(128)} %dynamic_slice.18.order_ref, s32[2]{0:T(128)} %pad_add_fusion.1.piece_ref, f32[2,1,512]{2,1,0:T(1,128)} %dynamic-slice_convert_fusion.gain_ref, bf16[4,512,512]{2,1,0:T(8,128)(2,1)} %all-to-all-done.2.refs_0_, bf16[4,512,512]{2,1,0:T(8,128)(2,1)} %collective-permute-done.5.refs_1_, ...), custom_call_target="tpu_custom_call" | custom-call | flops 6442450944 | bytes 16777216 | tf_op jit(solution)/shard_map/pallas_call | solution.py:178
  280.3 9.3 %all-to-all-done.3 = bf16[4,4,128,512]{3,2,1,0:T(8,128)(2,1)S(1)} async-done(((bf16[4,4,128,512]{3,2,1,0:T(8,128)(2,1)}), bf16[4,4,128,512]{3,2,1,0:T(8,128)(2,1)S(1)}, u32[]{:S(2)}, u32[]{:S(2)}) %all-to-all-start.3) | async-done | bytes 2097184 | tf_op jit(solution)/shard_map/all_to_all | solution.py:662
  292.8 8.9 %shard_map.181 = (bf16[4,144,512]{2,1,0:T(8,128)(2,1)}, bf16[4,144,512]{2,1,0:T(8,128)(2,1)}) custom-call(s32[8]{0:T(128)} %reshape.173.order_ref, bf16[3,128,512]{2,1,0:T(8,128)(2,1)} %copy-done.1, bf16[3,4096,512]{2,1,0:T(8,128)(2,1)} %bitcast.71, bf16[3,4096,512]{2,1,0:T(8,128)(2,1)} %bitcast.72, bf16[16,512]{1,0:T(8,128)(2,1)} %convert_element_type.105.refs_3_), custom_call_target="tpu_custom_call" | custom-call | flops 1610612736 | bytes 13631488 | tf_op jit(solution)/shard_map/pallas_call | solution.py:136
  316.2 3.6 %collective-permute-done.17 = bf16[144,512]{1,0:T(8,128)(2,1)S(1)} collective-permute-done((bf16[144,512]{1,0:T(8,128)(2,1)S(1)}, bf16[144,512]{1,0:T(8,128)(2,1)S(1)}, u32[]{:S(2)}, u32[]{:S(2)}) %collective-permute-start.17) | collective-permute-done | bytes 147488 | tf_op jit(solution)/shard_map/ppermute | solution.py:711
  323.4 3.7 %all-to-all-start.4 = ((bf16[4,144,512]{2,1,0:T(8,128)(2,1)}), bf16[4,144,512]{2,1,0:T(8,128)(2,1)S(1)}, u32[]{:S(2)}, u32[]{:S(2)}) async-start(bf16[4,144,512]{2,1,0:T(8,128)(2,1)} %broadcast_in_dim.77), calls=%async_computation.5 | async-start | bytes 1179648 | tf_op jit(solution)/shard_map/all_to_all | solution.py:662
  327.1 9.0 %shard_map.182 = f32[3,1024,512]{2,1,0:T(8,128)} custom-call(s32[4]{0:T(128)} %dynamic_slice.18.order_ref, s32[8]{0:T(128)} %iota.33.order_ref.piece_ref, f32[2,1,512]{2,1,0:T(1,128)} %dynamic-slice_convert_fusion.1.gain_ref, bf16[4,128,512]{2,1,0:T(8,128)(2,1)} %get-tuple-element.109.refs_0_, bf16[4,128,512]{2,1,0:T(8,128)(2,1)} %get-tuple-element.110.refs_1_, ...), custom_call_target="tpu_custom_call" | custom-call | flops 1610612736 | bytes 8912896 | tf_op jit(solution)/shard_map/pallas_call | solution.py:178
  (167 shorter events, 83.8 us)
Async XLA Ops:
  7.2 28.5 %all-gather.6.cloned.1.call-start = ((), (), s32[]{:S(2)}) async-start(), calls=%async_computation.7 | async-start | bytes 1327104 | tf_op jit(solution)/shard_map/all_gather | solution.py:654
  9.7 116.5 %all-gather.8.cloned.1.call-start = ((), (), s32[]{:S(2)}) async-start(), calls=%async_computation.8 | async-start | bytes 5013504 | tf_op jit(solution)/shard_map/all_gather | solution.py:654
  10.4 23.4 %collective-permute-start = (bf16[16,512]{1,0:T(8,128)(2,1)S(1)}, bf16[16,512]{1,0:T(8,128)(2,1)S(1)}, u32[]{:S(2)}, u32[]{:S(2)}) collective-permute-start(bf16[16,512]{1,0:T(8,128)(2,1)S(1)} %slice.118), channel_id=1, source_target_pairs={{8,0},{16,8},{24,16},{9,1},{17,9},{25,17},{10,2},{18,10},{26,18},{... | collective-permute-start | bytes 49160 | tf_op jit(solution)/shard_map/ppermute | solution.py:650
  43.1 11.5 %collective-permute-start.1 = (bf16[3,128,512]{2,1,0:T(8,128)(2,1)}, bf16[3,128,512]{2,1,0:T(8,128)(2,1)S(1)}, u32[]{:S(2)}, u32[]{:S(2)}) collective-permute-start(bf16[3,128,512]{2,1,0:T(8,128)(2,1)} %get-tuple-element.65.refs_0_), channel_id=1, source_target_pairs={{0,16},{16,24},{24,8},{8,0},{1,17},{17,25},{25,9},{9,1},{2,18},{18... | collective-permute-start | bytes 1179656 | tf_op jit(solution)/shard_map/ppermute | solution.py:679
  44.5 11.5 %collective-permute-start.2 = (bf16[3,128,512]{2,1,0:T(8,128)(2,1)}, bf16[3,128,512]{2,1,0:T(8,128)(2,1)S(1)}, u32[]{:S(2)}, u32[]{:S(2)}) collective-permute-start(bf16[3,128,512]{2,1,0:T(8,128)(2,1)} %get-tuple-element.65.refs_0_), channel_id=1, source_target_pairs={{0,8},{16,0},{24,16},{8,24},{1,9},{17,1},{25,17},{9,25},{2,10},{18... | collective-permute-start | bytes 1179656 | tf_op jit(solution)/shard_map/ppermute | solution.py:679
  80.1 15.8 %all-to-all-start = ((bf16[4,2,128,512]{3,2,1,0:T(8,128)(2,1)}), bf16[4,2,128,512]{3,2,1,0:T(8,128)(2,1)S(1)}, u32[]{:S(2)}, u32[]{:S(2)}) async-start(bf16[4,2,128,512]{3,2,1,0:T(8,128)(2,1)} %bitcast.16), calls=%async_computation | async-start | bytes 2097152 | tf_op jit(solution)/shard_map/all_to_all | solution.py:662
  147.7 9.4 %all-to-all-start.1 = ((f32[4,2,16,512]{3,2,1,0:T(8,128)}), f32[4,2,16,512]{3,2,1,0:T(8,128)S(1)}, u32[]{:S(2)}, u32[]{:S(2)}) async-start(f32[4,2,16,512]{3,2,1,0:T(8,128)} %get-tuple-element.75), calls=%async_computation.1 | async-start | bytes 524288 | tf_op jit(solution)/shard_map/all_to_all | solution.py:662
  157.8 31.1 %all-to-all-start.2 = ((bf16[4,512,512]{2,1,0:T(8,128)(2,1)}), bf16[4,512,512]{2,1,0:T(8,128)(2,1)}, u32[]{:S(2)}, u32[]{:S(2)}) async-start(bf16[4,512,512]{2,1,0:T(8,128)(2,1)} %dynamic-slice_bitcast_fusion), calls=%async_computation.2 | async-start | bytes 4194304 | tf_op jit(solution)/shard_map/all_to_all | solution.py:662
  162.2 76.4 %reduce-scatter.2.cloned.1.call-start = ((), (), s32[]{:S(2)}) async-start(), calls=%async_computation.6 | async-start | bytes 4718592 | tf_op jit(solution)/shard_map/reduce_scatter | solution.py:658
  189.0 40.4 %collective-permute-start.5 = (bf16[4,512,512]{2,1,0:T(8,128)(2,1)}, bf16[4,512,512]{2,1,0:T(8,128)(2,1)}, u32[]{:S(2)}, u32[]{:S(2)}) collective-permute-start(bf16[4,512,512]{2,1,0:T(8,128)(2,1)} %all-to-all-done.2.refs_0_), channel_id=1, source_target_pairs={{0,1},{1,0},{2,3},{3,2},{4,5},{5,4},{6,7},{7,6},{8,9},{9,8},{10,11... | collective-permute-start | bytes 6291464 | tf_op jit(solution)/shard_map/ppermute | solution.py:715
  190.0 20.6 %collective-permute-start.6 = (bf16[3,256,512]{2,1,0:T(8,128)(2,1)S(1)}, bf16[3,256,512]{2,1,0:T(8,128)(2,1)}, u32[]{:S(2)}, u32[]{:S(2)}) collective-permute-start(bf16[3,256,512]{2,1,0:T(8,128)(2,1)S(1)} %copy-done.7), channel_id=1, source_target_pairs={{0,16},{16,24},{24,8},{8,0},{1,17},{17,25},{25,9},{9,1},{2,18},{18... | collective-permute-start | bytes 2359304 | tf_op jit(solution)/shard_map/ppermute | solution.py:679
  191.9 20.6 %collective-permute-start.9 = (bf16[3,256,512]{2,1,0:T(8,128)(2,1)S(1)}, bf16[3,256,512]{2,1,0:T(8,128)(2,1)}, u32[]{:S(2)}, u32[]{:S(2)}) collective-permute-start(bf16[3,256,512]{2,1,0:T(8,128)(2,1)S(1)} %copy-done.8), channel_id=1, source_target_pairs={{0,8},{16,0},{24,16},{8,24},{1,9},{17,1},{25,17},{9,25},{2,10},{18... | collective-permute-start | bytes 2359304 | tf_op jit(solution)/shard_map/ppermute | solution.py:679
  192.2 35.3 %collective-permute-start.7 = (bf16[3,256,512]{2,1,0:T(8,128)(2,1)S(1)}, bf16[3,256,512]{2,1,0:T(8,128)(2,1)}, u32[]{:S(2)}, u32[]{:S(2)}) collective-permute-start(bf16[3,256,512]{2,1,0:T(8,128)(2,1)S(1)} %copy-done.8), channel_id=1, source_target_pairs={{0,16},{16,24},{24,8},{8,0},{1,17},{17,25},{25,9},{9,1},{2,18},{18... | collective-permute-start | bytes 2359304 | tf_op jit(solution)/shard_map/ppermute | solution.py:679
  193.9 35.4 %collective-permute-start.8 = (bf16[3,256,512]{2,1,0:T(8,128)(2,1)S(1)}, bf16[3,256,512]{2,1,0:T(8,128)(2,1)}, u32[]{:S(2)}, u32[]{:S(2)}) collective-permute-start(bf16[3,256,512]{2,1,0:T(8,128)(2,1)S(1)} %copy-done.7), channel_id=1, source_target_pairs={{0,8},{16,0},{24,16},{8,24},{1,9},{17,1},{25,17},{9,25},{2,10},{18... | collective-permute-start | bytes 2359304 | tf_op jit(solution)/shard_map/ppermute | solution.py:679
  210.6 32.8 %collective-permute-start.11 = (bf16[3,256,512]{2,1,0:T(8,128)(2,1)}, bf16[3,256,512]{2,1,0:T(8,128)(2,1)}, u32[]{:S(2)}, u32[]{:S(2)}) collective-permute-start(bf16[3,256,512]{2,1,0:T(8,128)(2,1)} %collective-permute-done.6.refs_4_), channel_id=1, source_target_pairs={{0,16},{16,24},{24,8},{8,0},{1,17},{17,25},{25,9},{9,1},{2,18},{18... | collective-permute-start | bytes 2359304 | tf_op jit(solution)/shard_map/ppermute | solution.py:679
  212.5 31.9 %collective-permute-start.12 = (bf16[3,256,512]{2,1,0:T(8,128)(2,1)}, bf16[3,256,512]{2,1,0:T(8,128)(2,1)}, u32[]{:S(2)}, u32[]{:S(2)}) collective-permute-start(bf16[3,256,512]{2,1,0:T(8,128)(2,1)} %collective-permute-done.9.refs_7_), channel_id=1, source_target_pairs={{0,8},{16,0},{24,16},{8,24},{1,9},{17,1},{25,17},{9,25},{2,10},{18... | collective-permute-start | bytes 2359304 | tf_op jit(solution)/shard_map/ppermute | solution.py:679
  262.0 27.6 %all-to-all-start.3 = ((bf16[4,4,128,512]{3,2,1,0:T(8,128)(2,1)}), bf16[4,4,128,512]{3,2,1,0:T(8,128)(2,1)S(1)}, u32[]{:S(2)}, u32[]{:S(2)}) async-start(bf16[4,4,128,512]{3,2,1,0:T(8,128)(2,1)} %shard_map.179), calls=%async_computation.4 | async-start | bytes 4194304 | tf_op jit(solution)/shard_map/all_to_all | solution.py:662
  290.1 11.6 %collective-permute-start.13 = (bf16[3,128,512]{2,1,0:T(8,128)(2,1)S(1)}, bf16[3,128,512]{2,1,0:T(8,128)(2,1)S(1)}, u32[]{:S(2)}, u32[]{:S(2)}) collective-permute-start(bf16[3,128,512]{2,1,0:T(8,128)(2,1)S(1)} %get-tuple-element.127.refs_0_.refs_2_), channel_id=1, source_target_pairs={{0,16},{16,24},{24,8},{8,0},{1,17},{17,25},{25,9},{9,1},{2,18},{18... | collective-permute-start | bytes 1179656 | tf_op jit(solution)/shard_map/ppermute | solution.py:679
  290.8 11.0 %collective-permute-start.14 = (bf16[3,128,512]{2,1,0:T(8,128)(2,1)S(1)}, bf16[3,128,512]{2,1,0:T(8,128)(2,1)S(1)}, u32[]{:S(2)}, u32[]{:S(2)}) collective-permute-start(bf16[3,128,512]{2,1,0:T(8,128)(2,1)S(1)} %get-tuple-element.127.refs_0_.refs_2_), channel_id=1, source_target_pairs={{0,8},{16,0},{24,16},{8,24},{1,9},{17,1},{25,17},{9,25},{2,10},{18... | collective-permute-start | bytes 1179656 | tf_op jit(solution)/shard_map/ppermute | solution.py:679
  301.8 14.4 %collective-permute-start.20 = (bf16[3,64,512]{2,1,0:T(8,128)(2,1)S(1)}, bf16[3,64,512]{2,1,0:T(8,128)(2,1)S(1)}, u32[]{:S(2)}, u32[]{:S(2)}) collective-permute-start(bf16[3,64,512]{2,1,0:T(8,128)(2,1)S(1)} %slice.174), channel_id=1, source_target_pairs={{0,16},{16,24},{24,8},{8,0},{1,17},{17,25},{25,9},{9,1},{2,18},{18... | collective-permute-start | bytes 589832 | tf_op jit(solution)/shard_map/ppermute | solution.py:679
  302.6 13.7 %collective-permute-start.21 = (bf16[3,64,512]{2,1,0:T(8,128)(2,1)S(1)}, bf16[3,64,512]{2,1,0:T(8,128)(2,1)S(1)}, u32[]{:S(2)}, u32[]{:S(2)}) collective-permute-start(bf16[3,64,512]{2,1,0:T(8,128)(2,1)S(1)} %slice.175), channel_id=1, source_target_pairs={{0,8},{16,0},{24,16},{8,24},{1,9},{17,1},{25,17},{9,25},{2,10},{18... | collective-permute-start | bytes 589832 | tf_op jit(solution)/shard_map/ppermute | solution.py:679
  312.1 7.7 %collective-permute-start.17 = (bf16[144,512]{1,0:T(8,128)(2,1)S(1)}, bf16[144,512]{1,0:T(8,128)(2,1)S(1)}, u32[]{:S(2)}, u32[]{:S(2)}) collective-permute-start(bf16[144,512]{1,0:T(8,128)(2,1)S(1)} %pad_maximum_fusion.2), channel_id=1, source_target_pairs={{0,2},{1,3},{2,4},{3,5},{4,6},{5,7},{6,0},{7,1},{8,10},{9,11},{10,... | collective-permute-start | bytes 442376 | tf_op jit(solution)/shard_map/ppermute | solution.py:711
  313.0 8.3 %collective-permute-start.19 = (bf16[144,512]{1,0:T(8,128)(2,1)S(1)}, bf16[144,512]{1,0:T(8,128)(2,1)S(1)}, u32[]{:S(2)}, u32[]{:S(2)}) collective-permute-start(bf16[144,512]{1,0:T(8,128)(2,1)S(1)} %pad_maximum_fusion.3), channel_id=1, source_target_pairs={{0,6},{1,7},{2,0},{3,1},{4,2},{5,3},{6,4},{7,5},{8,14},{9,15},{10,... | collective-permute-start | bytes 442376 | tf_op jit(solution)/shard_map/ppermute | solution.py:711
  323.4 12.7 %all-to-all-start.4 = ((bf16[4,144,512]{2,1,0:T(8,128)(2,1)}), bf16[4,144,512]{2,1,0:T(8,128)(2,1)S(1)}, u32[]{:S(2)}, u32[]{:S(2)}) async-start(bf16[4,144,512]{2,1,0:T(8,128)(2,1)} %broadcast_in_dim.77), calls=%async_computation.5 | async-start | bytes 1179648 | tf_op jit(solution)/shard_map/all_to_all | solution.py:662
  (30 other events, 312.8 us)
Sparse Core Ops, SparseCore 0:
  10.2 25.4 all-gather.5
  77.8 48.3 all-gather.7
  189.1 49.5 reduce-scatter.1

commit v6 on v5

--- a/solution.py
+++ b/solution.py
@@ -454,7 +454,7 @@
         )
         return held
 
-    return lax.fori_loop(0, length, step, tuple(states), unroll=8)
+    return lax.fori_loop(0, length, step, tuple(states), unroll=16)
 
 
 def spread(ref, count):
@@ -496,7 +496,7 @@
         )
 
     zeros = (jnp.zeros((SEGMENTS, LANES), f32),) * (2 * modes)
-    ends = lax.fori_loop(0, length, step, zeros, unroll=8)
+    ends = lax.fori_loop(0, length, step, zeros, unroll=16)
     for way in range(2):
         for m in range(modes):
             segment_ref[way, pl.ds(m, SEGMENTS, stride=modes), :] = ends[way * modes + m]

time: 346 us -> 346 us (level)
  transfers between devices with their start and end apart: 30 -> 30, of which waited for: 18 -> 20; matrix products, arithmetic and copies ran while one was open for 7% -> 7% of each run, Pallas kernels for 19% -> 19%
where the time goes in v6:
time: 346 us; the launch traced here: 344 us
  Pallas kernels  122 us (35%)
  waiting for transfers between devices  102 us (29%)
  starting transfers between devices  43.4 us (13%)
  blocking collectives  26 us (8%)
  local copies, waits for them, and re-layouts  19.2 us (6%)
  between operations  16.2 us (5%)
  other arithmetic  15.4 us (4%)
    ppermute x14, waiting for transfers between devices, seq_hop(): return lax.ppermute(value, 'seq', pairs)  34.9 us
    all_gather x2, waiting for transfers between devices, gather_ch(): return lax.all_gather(value, 'ch', axis=0, tiled=False)  30.2 us
    pallas_call x2, Pallas kernels, weight_grad(): call(functools.partial(weight_grad_kernel, [(slot, first) for slot, first...  22.8 us
    pallas_call x2, Pallas kernels, project_back(): call(functools.partial(back_kernel, len(parts), apart), (count // 2,), [w...  20.9 us
    pallas_call x2, Pallas kernels, project(): call(functools.partial(project_kernel, per_step, features, rows, gain_row...  19.7 us
    all_to_all x5, starting transfers between devices, exchange_seq(): return lax.all_to_all(value, 'seq', split_axis=0, concat_axis=0, tiled=True)  19.1 us
    all_to_all x5, waiting for transfers between devices, exchange_seq(): return lax.all_to_all(value, 'seq', split_axis=0, concat_axis=0, tiled=True)  15.8 us
    pallas_call x1, Pallas kernels, first_forward(): call(functools.partial(first_forward_kernel, front, rows, places), (colum...  14.9 us
  transfers between devices with their start and end apart: 30, of which 20 were waited for; matrix products, arithmetic and copies ran while one was open for 7% of the time, Pallas kernels for 19%

profile of v6, /device:TPU:0, one launch (start us, length us, event | category | flops | bytes accessed | tf_op | source)
XLA Modules:
  0.0 344.3 jit_solution(16653785000137631742)
XLA Ops:
  18.0 11.6 %all-gather.2 = s32[4,1,512]{2,1,0:T(1,128)S(1)} all-gather(s32[1,1,512]{2,1,0:T(1,128)} %bitcast.88), channel_id=1, replica_groups=mesh['seq'=4,'ch'=8] {'seq'}, dimensions={0}, use_global_device_ids=true | all-gather | bytes 10240 | tf_op jit(solution)/shard_map/all_gather | solution.py:799
  35.7 7.4 %shard_map.172 = (bf16[3,128,512]{2,1,0:T(8,128)(2,1)}, f32[128,1]{1,0:T(8,128)}) custom-call(bf16[8,144,512]{2,1,0:T(8,128)(2,1)} %bitcast.76, bf16[8,144,512]{2,1,0:T(8,128)(2,1)} %bitcast.77, bf16[3,4096,512]{2,1,0:T(8,128)(2,1)} %bitcast.70), custom_call_target="tpu_custom_call" | custom-call | flops 1610612736 | bytes 13631488 | tf_op jit(solution)/shard_map/pallas_call | solution.py:84
  45.3 9.2 %collective-permute-done.1.refs_1_ = bf16[3,128,512]{2,1,0:T(8,128)(2,1)S(1)} collective-permute-done((bf16[3,128,512]{2,1,0:T(8,128)(2,1)}, bf16[3,128,512]{2,1,0:T(8,128)(2,1)S(1)}, u32[]{:S(2)}, u32[]{:S(2)}) %collective-permute-start.1) | collective-permute-done | bytes 393248 | tf_op jit(solution)/shard_map/ppermute | solution.py:679
  62.7 14.9 %shard_map.173 = (bf16[544,512]{1,0:T(8,128)(2,1)}, f32[528,512]{1,0:T(8,128)}) custom-call(s32[688,1]{1,0:T(8,128)} %get-tuple-element.136.token_ref, bf16[512,512]{1,0:T(8,128)(2,1)} %bitcast_select_fusion.e_ref, f32[3,7,512]{2,1,0:T(8,128)} %bitcast.92, bf16[128,512]{1,0:T(8,128)(2,1)} %medium_ref.3, bf16[3,128,512]{2,1,0:T(8,128)(2,1)} %get-tuple-element.65.refs_0_, ...), custom_call_target="tpu_custom_call" | custom-call | flops 11928600576 | bytes 2818048 | tf_op jit(solution)/shard_map/pallas_call | solution.py:315
  80.1 3.5 %all-to-all-start = ((bf16[4,2,128,512]{3,2,1,0:T(8,128)(2,1)}), bf16[4,2,128,512]{3,2,1,0:T(8,128)(2,1)S(1)}, u32[]{:S(2)}, u32[]{:S(2)}) async-start(bf16[4,2,128,512]{3,2,1,0:T(8,128)(2,1)} %bitcast.16), calls=%async_computation | async-start | bytes 2097152 | tf_op jit(solution)/shard_map/all_to_all | solution.py:662
  84.9 7.2 %shard_map.174.feature_ref = f32[3,672,512]{2,1,0:T(8,128)} custom-call(s32[688,1]{1,0:T(8,128)} %get-tuple-element.67.token_ref, f32[3,7,512]{2,1,0:T(8,128)} %bitcast.93, bf16[3,128,512]{2,1,0:T(8,128)(2,1)} %get-tuple-element.65.refs_0_, bf16[3,128,512]{2,1,0:T(8,128)(2,1)} %copy-done.15, bf16[3,128,512]{2,1,0:T(8,128)(2,1)} %copy-done.16, ...), custom_call_target="tpu_custom_call" | custom-call | flops 3900178432 | bytes 5636096 | tf_op jit(solution)/shard_map/pallas_call | solution.py:359
  92.1 3.8 %all-to-all-done = bf16[4,2,128,512]{3,2,1,0:T(8,128)(2,1)S(1)} async-done(((bf16[4,2,128,512]{3,2,1,0:T(8,128)(2,1)}), bf16[4,2,128,512]{3,2,1,0:T(8,128)(2,1)S(1)}, u32[]{:S(2)}, u32[]{:S(2)}) %all-to-all-start) | async-done | bytes 1048608 | tf_op jit(solution)/shard_map/all_to_all | solution.py:662
  97.0 29.2 %all-gather.8.cloned.1.call-done = bf16[4352,512]{1,0:T(8,128)(2,1)} async-done(((bf16[544,512]{1,0:T(8,128)(2,1)}), bf16[4352,512]{1,0:T(8,128)(2,1)}) %all-gather.8.cloned.1.call-update) | async-done | bytes 4456464 | tf_op jit(solution)/shard_map/all_gather | solution.py:654
  126.7 12.3 %shard_map.175 = (bf16[3,544,512]{2,1,0:T(8,128)(2,1)}, f32[544,1]{1,0:T(8,128)}) custom-call(bf16[8,544,512]{2,1,0:T(8,128)(2,1)} %bitcast.84, bf16[8,144,512]{2,1,0:T(8,128)(2,1)} %bitcast.78, bf16[3,4096,512]{2,1,0:T(8,128)(2,1)} %bitcast.73), custom_call_target="tpu_custom_call" | custom-call | flops 6845104128 | bytes 17039360 | tf_op jit(solution)/shard_map/pallas_call | solution.py:84
  139.0 8.5 %shard_map.176 = (f32[3,528,512]{2,1,0:T(8,128)}, bf16[528,512]{1,0:T(8,128)(2,1)}, bf16[528,512]{1,0:T(8,128)(2,1)}, f32[2,128,512]{2,1,0:T(8,128)}, f32[4,2,16,512]{3,2,1,0:T(8,128)}) custom-call(bf16[3,544,512]{2,1,0:T(8,128)(2,1)} %get-tuple-element.69.p_ref, f32[3,7,512]{2,1,0:T(8,128)} %bitcast.90, bf16[528,512]{1,0:T(8,128)(2,1)} %pad_maximum_fusion.above_ref, ...), custom_call_target="tpu_custom_call" | custom-call | flops 5190451200 | bytes 6488064 | tf_op jit(solution)/shard_map/pallas_call | solution.py:522
  147.5 3.6 %all-to-all-start.1 = ((f32[4,2,16,512]{3,2,1,0:T(8,128)}), f32[4,2,16,512]{3,2,1,0:T(8,128)S(1)}, u32[]{:S(2)}, u32[]{:S(2)}) async-start(f32[4,2,16,512]{3,2,1,0:T(8,128)} %get-tuple-element.75), calls=%async_computation.1 | async-start | bytes 524288 | tf_op jit(solution)/shard_map/all_to_all | solution.py:662
  157.6 4.4 %all-to-all-start.2 = ((bf16[4,512,512]{2,1,0:T(8,128)(2,1)}), bf16[4,512,512]{2,1,0:T(8,128)(2,1)}, u32[]{:S(2)}, u32[]{:S(2)}) async-start(bf16[4,512,512]{2,1,0:T(8,128)(2,1)} %dynamic-slice_bitcast_fusion), calls=%async_computation.2 | async-start | bytes 4194304 | tf_op jit(solution)/shard_map/all_to_all | solution.py:662
  162.3 14.0 %shard_map.177 = (bf16[512,512]{1,0:T(8,128)(2,1)}, bf16[3,256,512]{2,1,0:T(8,128)(2,1)}, bf16[3,256,512]{2,1,0:T(8,128)(2,1)}, f32[512,1]{1,0:T(8,128)}) custom-call(s32[1]{0:T(128)} %bitcast.seq_ref, f32[3,528,512]{2,1,0:T(8,128)} %get-tuple-element.71.feature_ref, bf16[528,512]{1,0:T(8,128)(2,1)} %get-tuple-element.72.gated_ref, ...), custom_call_target="tpu_custom_call" | custom-call | flops 10485760000 | bytes 10485760 | tf_op jit(solution)/shard_map/pallas_call | solution.py:631
  176.9 12.0 %shard_map.178 = bf16[8,512,512]{2,1,0:T(8,128)(2,1)} custom-call(s32[8]{0:T(128)} %iota.33.order_ref.piece_ref, bf16[3,256,512]{2,1,0:T(8,128)(2,1)} %get-tuple-element.80.refs_0_.refs_2_, bf16[3,256,512]{2,1,0:T(8,128)(2,1)} %get-tuple-element.81.refs_1_.refs_3_, bf16[3,4096,512]{2,1,0:T(8,128)(2,1)} %bitcast.74, bf16[3,4096,512]{2,1,0:T(8,128)(2,1)} %bitcast.75, ...), custom_call_target="tpu_custom_call" | custom-call | flops 6442450944 | bytes 16777216 | tf_op jit(solution)/shard_map/pallas_call | solution.py:136
  194.1 16.5 %collective-permute-done.6.refs_4_ = bf16[3,256,512]{2,1,0:T(8,128)(2,1)} collective-permute-done((bf16[3,256,512]{2,1,0:T(8,128)(2,1)S(1)}, bf16[3,256,512]{2,1,0:T(8,128)(2,1)}, u32[]{:S(2)}, u32[]{:S(2)}) %collective-permute-start.6) | collective-permute-done | bytes 786464 | tf_op jit(solution)/shard_map/ppermute | solution.py:679
  213.0 14.4 %psum.7 = f32[512]{0:T(512)S(1)} all-reduce(f32[512]{0:T(512)S(1)} %reduce.21), channel_id=1, replica_groups=mesh['seq'=4,'ch'=8] {'ch'}, use_global_device_ids=true, to_apply=%region_3.4 | all-reduce | flops 512 | bytes 4096 | tf_op jit(solution)/shard_map/psum | solution.py:850
  229.2 9.3 %reduce-scatter.2.cloned.1.call-done = bf16[1,512,512]{2,1,0:T(8,128)(2,1)} async-done(((bf16[8,512,512]{2,1,0:T(8,128)(2,1)}), bf16[1,512,512]{2,1,0:T(8,128)(2,1)}) %reduce-scatter.2.cloned.1.call-update) | async-done | bytes 524304 | tf_op jit(solution)/shard_map/reduce_scatter | solution.py:658
  247.9 13.9 %shard_map.179 = bf16[4,4,128,512]{3,2,1,0:T(8,128)(2,1)} custom-call(s32[1,512]{1,0:T(1,128)} %bitcast.89, bf16[512,512]{1,0:T(8,128)(2,1)} %copy-done.4, bf16[160,512]{1,0:T(8,128)(2,1)} %copy-done.23, f32[3,672,512]{2,1,0:T(8,128)} %shard_map.174.feature_ref, f32[528,512]{1,0:T(8,128)} %get-tuple-element.90.filtered_ref, f32[3,7,512]{2,1,0:T(8,128)} %bitcast.94, ...), custom_call_target="tpu_custom_call" | custom-call | flops 11559501824 | bytes 5505024 | tf_op jit(solution)/shard_map/pallas_call | solution.py:416
  261.8 4.0 %all-to-all-start.3 = ((bf16[4,4,128,512]{3,2,1,0:T(8,128)(2,1)}), bf16[4,4,128,512]{3,2,1,0:T(8,128)(2,1)S(1)}, u32[]{:S(2)}, u32[]{:S(2)}) async-start(bf16[4,4,128,512]{3,2,1,0:T(8,128)(2,1)} %shard_map.179), calls=%async_computation.4 | async-start | bytes 4194304 | tf_op jit(solution)/shard_map/all_to_all | solution.py:662
  266.5 13.8 %shard_map.180 = f32[3,1024,512]{2,1,0:T(8,128)} custom-call(s32[4]{0:T(128)} %dynamic_slice.18.order_ref, s32[2]{0:T(128)} %pad_add_fusion.1.piece_ref, f32[2,1,512]{2,1,0:T(1,128)} %dynamic-slice_convert_fusion.gain_ref, bf16[4,512,512]{2,1,0:T(8,128)(2,1)} %all-to-all-done.2.refs_0_, bf16[4,512,512]{2,1,0:T(8,128)(2,1)} %collective-permute-done.5.refs_1_, ...), custom_call_target="tpu_custom_call" | custom-call | flops 6442450944 | bytes 16777216 | tf_op jit(solution)/shard_map/pallas_call | solution.py:178
  280.3 9.1 %all-to-all-done.3 = bf16[4,4,128,512]{3,2,1,0:T(8,128)(2,1)S(1)} async-done(((bf16[4,4,128,512]{3,2,1,0:T(8,128)(2,1)}), bf16[4,4,128,512]{3,2,1,0:T(8,128)(2,1)S(1)}, u32[]{:S(2)}, u32[]{:S(2)}) %all-to-all-start.3) | async-done | bytes 2097184 | tf_op jit(solution)/shard_map/all_to_all | solution.py:662
  292.7 8.9 %shard_map.181 = (bf16[4,144,512]{2,1,0:T(8,128)(2,1)}, bf16[4,144,512]{2,1,0:T(8,128)(2,1)}) custom-call(s32[8]{0:T(128)} %reshape.173.order_ref, bf16[3,128,512]{2,1,0:T(8,128)(2,1)} %copy-done.1, bf16[3,4096,512]{2,1,0:T(8,128)(2,1)} %bitcast.71, bf16[3,4096,512]{2,1,0:T(8,128)(2,1)} %bitcast.72, bf16[16,512]{1,0:T(8,128)(2,1)} %convert_element_type.105.refs_3_), custom_call_target="tpu_custom_call" | custom-call | flops 1610612736 | bytes 13631488 | tf_op jit(solution)/shard_map/pallas_call | solution.py:136
  315.8 3.9 %collective-permute-done.17 = bf16[144,512]{1,0:T(8,128)(2,1)S(1)} collective-permute-done((bf16[144,512]{1,0:T(8,128)(2,1)S(1)}, bf16[144,512]{1,0:T(8,128)(2,1)S(1)}, u32[]{:S(2)}, u32[]{:S(2)}) %collective-permute-start.17) | collective-permute-done | bytes 147488 | tf_op jit(solution)/shard_map/ppermute | solution.py:711
  326.8 9.0 %shard_map.182 = f32[3,1024,512]{2,1,0:T(8,128)} custom-call(s32[4]{0:T(128)} %dynamic_slice.18.order_ref, s32[8]{0:T(128)} %iota.33.order_ref.piece_ref, f32[2,1,512]{2,1,0:T(1,128)} %dynamic-slice_convert_fusion.1.gain_ref, bf16[4,128,512]{2,1,0:T(8,128)(2,1)} %get-tuple-element.109.refs_0_, bf16[4,128,512]{2,1,0:T(8,128)(2,1)} %get-tuple-element.110.refs_1_, ...), custom_call_target="tpu_custom_call" | custom-call | flops 1610612736 | bytes 8912896 | tf_op jit(solution)/shard_map/pallas_call | solution.py:178
  (167 shorter events, 83.5 us)
Async XLA Ops:
  7.2 28.5 %all-gather.6.cloned.1.call-start = ((), (), s32[]{:S(2)}) async-start(), calls=%async_computation.7 | async-start | bytes 1327104 | tf_op jit(solution)/shard_map/all_gather | solution.py:654
  9.7 116.5 %all-gather.8.cloned.1.call-start = ((), (), s32[]{:S(2)}) async-start(), calls=%async_computation.8 | async-start | bytes 5013504 | tf_op jit(solution)/shard_map/all_gather | solution.py:654
  10.4 23.4 %collective-permute-start = (bf16[16,512]{1,0:T(8,128)(2,1)S(1)}, bf16[16,512]{1,0:T(8,128)(2,1)S(1)}, u32[]{:S(2)}, u32[]{:S(2)}) collective-permute-start(bf16[16,512]{1,0:T(8,128)(2,1)S(1)} %slice.118), channel_id=1, source_target_pairs={{8,0},{16,8},{24,16},{9,1},{17,9},{25,17},{10,2},{18,10},{26,18},{... | collective-permute-start | bytes 49160 | tf_op jit(solution)/shard_map/ppermute | solution.py:650
  43.1 11.5 %collective-permute-start.1 = (bf16[3,128,512]{2,1,0:T(8,128)(2,1)}, bf16[3,128,512]{2,1,0:T(8,128)(2,1)S(1)}, u32[]{:S(2)}, u32[]{:S(2)}) collective-permute-start(bf16[3,128,512]{2,1,0:T(8,128)(2,1)} %get-tuple-element.65.refs_0_), channel_id=1, source_target_pairs={{0,16},{16,24},{24,8},{8,0},{1,17},{17,25},{25,9},{9,1},{2,18},{18... | collective-permute-start | bytes 1179656 | tf_op jit(solution)/shard_map/ppermute | solution.py:679
  44.5 11.5 %collective-permute-start.2 = (bf16[3,128,512]{2,1,0:T(8,128)(2,1)}, bf16[3,128,512]{2,1,0:T(8,128)(2,1)S(1)}, u32[]{:S(2)}, u32[]{:S(2)}) collective-permute-start(bf16[3,128,512]{2,1,0:T(8,128)(2,1)} %get-tuple-element.65.refs_0_), channel_id=1, source_target_pairs={{0,8},{16,0},{24,16},{8,24},{1,9},{17,1},{25,17},{9,25},{2,10},{18... | collective-permute-start | bytes 1179656 | tf_op jit(solution)/shard_map/ppermute | solution.py:679
  80.1 15.8 %all-to-all-start = ((bf16[4,2,128,512]{3,2,1,0:T(8,128)(2,1)}), bf16[4,2,128,512]{3,2,1,0:T(8,128)(2,1)S(1)}, u32[]{:S(2)}, u32[]{:S(2)}) async-start(bf16[4,2,128,512]{3,2,1,0:T(8,128)(2,1)} %bitcast.16), calls=%async_computation | async-start | bytes 2097152 | tf_op jit(solution)/shard_map/all_to_all | solution.py:662
  147.5 9.4 %all-to-all-start.1 = ((f32[4,2,16,512]{3,2,1,0:T(8,128)}), f32[4,2,16,512]{3,2,1,0:T(8,128)S(1)}, u32[]{:S(2)}, u32[]{:S(2)}) async-start(f32[4,2,16,512]{3,2,1,0:T(8,128)} %get-tuple-element.75), calls=%async_computation.1 | async-start | bytes 524288 | tf_op jit(solution)/shard_map/all_to_all | solution.py:662
  157.6 31.4 %all-to-all-start.2 = ((bf16[4,512,512]{2,1,0:T(8,128)(2,1)}), bf16[4,512,512]{2,1,0:T(8,128)(2,1)}, u32[]{:S(2)}, u32[]{:S(2)}) async-start(bf16[4,512,512]{2,1,0:T(8,128)(2,1)} %dynamic-slice_bitcast_fusion), calls=%async_computation.2 | async-start | bytes 4194304 | tf_op jit(solution)/shard_map/all_to_all | solution.py:662
  162.0 76.5 %reduce-scatter.2.cloned.1.call-start = ((), (), s32[]{:S(2)}) async-start(), calls=%async_computation.6 | async-start | bytes 4718592 | tf_op jit(solution)/shard_map/reduce_scatter | solution.py:658
  189.0 40.2 %collective-permute-start.5 = (bf16[4,512,512]{2,1,0:T(8,128)(2,1)}, bf16[4,512,512]{2,1,0:T(8,128)(2,1)}, u32[]{:S(2)}, u32[]{:S(2)}) collective-permute-start(bf16[4,512,512]{2,1,0:T(8,128)(2,1)} %all-to-all-done.2.refs_0_), channel_id=1, source_target_pairs={{0,1},{1,0},{2,3},{3,2},{4,5},{5,4},{6,7},{7,6},{8,9},{9,8},{10,11... | collective-permute-start | bytes 6291464 | tf_op jit(solution)/shard_map/ppermute | solution.py:715
  190.0 20.6 %collective-permute-start.6 = (bf16[3,256,512]{2,1,0:T(8,128)(2,1)S(1)}, bf16[3,256,512]{2,1,0:T(8,128)(2,1)}, u32[]{:S(2)}, u32[]{:S(2)}) collective-permute-start(bf16[3,256,512]{2,1,0:T(8,128)(2,1)S(1)} %copy-done.7), channel_id=1, source_target_pairs={{0,16},{16,24},{24,8},{8,0},{1,17},{17,25},{25,9},{9,1},{2,18},{18... | collective-permute-start | bytes 2359304 | tf_op jit(solution)/shard_map/ppermute | solution.py:679
  191.8 20.6 %collective-permute-start.9 = (bf16[3,256,512]{2,1,0:T(8,128)(2,1)S(1)}, bf16[3,256,512]{2,1,0:T(8,128)(2,1)}, u32[]{:S(2)}, u32[]{:S(2)}) collective-permute-start(bf16[3,256,512]{2,1,0:T(8,128)(2,1)S(1)} %copy-done.8), channel_id=1, source_target_pairs={{0,8},{16,0},{24,16},{8,24},{1,9},{17,1},{25,17},{9,25},{2,10},{18... | collective-permute-start | bytes 2359304 | tf_op jit(solution)/shard_map/ppermute | solution.py:679
  192.1 35.4 %collective-permute-start.7 = (bf16[3,256,512]{2,1,0:T(8,128)(2,1)S(1)}, bf16[3,256,512]{2,1,0:T(8,128)(2,1)}, u32[]{:S(2)}, u32[]{:S(2)}) collective-permute-start(bf16[3,256,512]{2,1,0:T(8,128)(2,1)S(1)} %copy-done.8), channel_id=1, source_target_pairs={{0,16},{16,24},{24,8},{8,0},{1,17},{17,25},{25,9},{9,1},{2,18},{18... | collective-permute-start | bytes 2359304 | tf_op jit(solution)/shard_map/ppermute | solution.py:679
  193.8 35.4 %collective-permute-start.8 = (bf16[3,256,512]{2,1,0:T(8,128)(2,1)S(1)}, bf16[3,256,512]{2,1,0:T(8,128)(2,1)}, u32[]{:S(2)}, u32[]{:S(2)}) collective-permute-start(bf16[3,256,512]{2,1,0:T(8,128)(2,1)S(1)} %copy-done.7), channel_id=1, source_target_pairs={{0,8},{16,0},{24,16},{8,24},{1,9},{17,1},{25,17},{9,25},{2,10},{18... | collective-permute-start | bytes 2359304 | tf_op jit(solution)/shard_map/ppermute | solution.py:679
  210.6 32.6 %collective-permute-start.11 = (bf16[3,256,512]{2,1,0:T(8,128)(2,1)}, bf16[3,256,512]{2,1,0:T(8,128)(2,1)}, u32[]{:S(2)}, u32[]{:S(2)}) collective-permute-start(bf16[3,256,512]{2,1,0:T(8,128)(2,1)} %collective-permute-done.6.refs_4_), channel_id=1, source_target_pairs={{0,16},{16,24},{24,8},{8,0},{1,17},{17,25},{25,9},{9,1},{2,18},{18... | collective-permute-start | bytes 2359304 | tf_op jit(solution)/shard_map/ppermute | solution.py:679
  212.4 31.9 %collective-permute-start.12 = (bf16[3,256,512]{2,1,0:T(8,128)(2,1)}, bf16[3,256,512]{2,1,0:T(8,128)(2,1)}, u32[]{:S(2)}, u32[]{:S(2)}) collective-permute-start(bf16[3,256,512]{2,1,0:T(8,128)(2,1)} %collective-permute-done.9.refs_7_), channel_id=1, source_target_pairs={{0,8},{16,0},{24,16},{8,24},{1,9},{17,1},{25,17},{9,25},{2,10},{18... | collective-permute-start | bytes 2359304 | tf_op jit(solution)/shard_map/ppermute | solution.py:679
  261.8 27.6 %all-to-all-start.3 = ((bf16[4,4,128,512]{3,2,1,0:T(8,128)(2,1)}), bf16[4,4,128,512]{3,2,1,0:T(8,128)(2,1)S(1)}, u32[]{:S(2)}, u32[]{:S(2)}) async-start(bf16[4,4,128,512]{3,2,1,0:T(8,128)(2,1)} %shard_map.179), calls=%async_computation.4 | async-start | bytes 4194304 | tf_op jit(solution)/shard_map/all_to_all | solution.py:662
  289.9 11.7 %collective-permute-start.13 = (bf16[3,128,512]{2,1,0:T(8,128)(2,1)S(1)}, bf16[3,128,512]{2,1,0:T(8,128)(2,1)S(1)}, u32[]{:S(2)}, u32[]{:S(2)}) collective-permute-start(bf16[3,128,512]{2,1,0:T(8,128)(2,1)S(1)} %get-tuple-element.127.refs_0_.refs_2_), channel_id=1, source_target_pairs={{0,16},{16,24},{24,8},{8,0},{1,17},{17,25},{25,9},{9,1},{2,18},{18... | collective-permute-start | bytes 1179656 | tf_op jit(solution)/shard_map/ppermute | solution.py:679
  290.6 11.0 %collective-permute-start.14 = (bf16[3,128,512]{2,1,0:T(8,128)(2,1)S(1)}, bf16[3,128,512]{2,1,0:T(8,128)(2,1)S(1)}, u32[]{:S(2)}, u32[]{:S(2)}) collective-permute-start(bf16[3,128,512]{2,1,0:T(8,128)(2,1)S(1)} %get-tuple-element.127.refs_0_.refs_2_), channel_id=1, source_target_pairs={{0,8},{16,0},{24,16},{8,24},{1,9},{17,1},{25,17},{9,25},{2,10},{18... | collective-permute-start | bytes 1179656 | tf_op jit(solution)/shard_map/ppermute | solution.py:679
  301.7 14.1 %collective-permute-start.20 = (bf16[3,64,512]{2,1,0:T(8,128)(2,1)S(1)}, bf16[3,64,512]{2,1,0:T(8,128)(2,1)S(1)}, u32[]{:S(2)}, u32[]{:S(2)}) collective-permute-start(bf16[3,64,512]{2,1,0:T(8,128)(2,1)S(1)} %slice.174), channel_id=1, source_target_pairs={{0,16},{16,24},{24,8},{8,0},{1,17},{17,25},{25,9},{9,1},{2,18},{18... | collective-permute-start | bytes 589832 | tf_op jit(solution)/shard_map/ppermute | solution.py:679
  302.4 13.4 %collective-permute-start.21 = (bf16[3,64,512]{2,1,0:T(8,128)(2,1)S(1)}, bf16[3,64,512]{2,1,0:T(8,128)(2,1)S(1)}, u32[]{:S(2)}, u32[]{:S(2)}) collective-permute-start(bf16[3,64,512]{2,1,0:T(8,128)(2,1)S(1)} %slice.175), channel_id=1, source_target_pairs={{0,8},{16,0},{24,16},{8,24},{1,9},{17,1},{25,17},{9,25},{2,10},{18... | collective-permute-start | bytes 589832 | tf_op jit(solution)/shard_map/ppermute | solution.py:679
  311.7 8.0 %collective-permute-start.17 = (bf16[144,512]{1,0:T(8,128)(2,1)S(1)}, bf16[144,512]{1,0:T(8,128)(2,1)S(1)}, u32[]{:S(2)}, u32[]{:S(2)}) collective-permute-start(bf16[144,512]{1,0:T(8,128)(2,1)S(1)} %pad_maximum_fusion.2), channel_id=1, source_target_pairs={{0,2},{1,3},{2,4},{3,5},{4,6},{5,7},{6,0},{7,1},{8,10},{9,11},{10,... | collective-permute-start | bytes 442376 | tf_op jit(solution)/shard_map/ppermute | solution.py:711
  312.8 8.4 %collective-permute-start.19 = (bf16[144,512]{1,0:T(8,128)(2,1)S(1)}, bf16[144,512]{1,0:T(8,128)(2,1)S(1)}, u32[]{:S(2)}, u32[]{:S(2)}) collective-permute-start(bf16[144,512]{1,0:T(8,128)(2,1)S(1)} %pad_maximum_fusion.3), channel_id=1, source_target_pairs={{0,6},{1,7},{2,0},{3,1},{4,2},{5,3},{6,4},{7,5},{8,14},{9,15},{10,... | collective-permute-start | bytes 442376 | tf_op jit(solution)/shard_map/ppermute | solution.py:711
  323.3 12.6 %all-to-all-start.4 = ((bf16[4,144,512]{2,1,0:T(8,128)(2,1)}), bf16[4,144,512]{2,1,0:T(8,128)(2,1)S(1)}, u32[]{:S(2)}, u32[]{:S(2)}) async-start(bf16[4,144,512]{2,1,0:T(8,128)(2,1)} %broadcast_in_dim.77), calls=%async_computation.5 | async-start | bytes 1179648 | tf_op jit(solution)/shard_map/all_to_all | solution.py:662
  (30 other events, 311.3 us)
Sparse Core Ops, SparseCore 0:
  10.2 25.4 all-gather.5
  77.8 48.3 all-gather.7
  189.1 49.3 reduce-scatter.1
